TPU v7x, 256 devices: a whole 4x4x8 slice. The times are simulated.
256 devices in a mesh: row: 32 (over y, z_hi, x), col: 8 (over z_lo, core).
Axes of the slice: x: 4, y: 4, z: 8 (z_hi: 2, z_lo: 4; z = z_hi * 4 + z_lo), core: 2. Of those that a mesh axis runs over, the one named last changes fastest.
Arguments:
- pair: float32 [576, 576, 128], P('row', 'col'), may hold values from -6 to 6
- cotangent: float32 [576, 576, 128], P('row', 'col'), may hold values from -6 to 6
- residue_mask: int32 [576], replicated, may hold values 0 or 1
- ln_gain: float32 [128], replicated, may hold values from 0.25 to 1.75
- ln_bias: float32 [128], replicated, may hold values from -3 to 3
- proj_weight: float32 [128, 640], replicated, may hold values from -0.5 to 0.5
- proj_bias: float32 [640], replicated, may hold values from -3 to 3
- norm_gain: float32 [128], replicated, may hold values from 0.25 to 1.75
- norm_bias: float32 [128], replicated, may hold values from -3 to 3
- out_weight: float32 [128, 128], replicated, may hold values from -0.5 to 0.5
- out_bias: float32 [128], replicated, may hold values from -3 to 3
Outputs:
- update: float32 [576, 576, 128], P('row', 'col')
- grad_pair: float32 [576, 576, 128], P('row', 'col')
- grad_proj: float32 [128, 640], replicated
- grad_out: float32 [128, 128], replicated
All inputs are finite; a program needn't handle non-finite values.
Results may differ from a plain program's by a relative error of at most 0.015.
Values may be sent and summed in bfloat16 or wider, within the bound.
No kernel may reach another device: no remote copies, remote signals or barrier semaphores. Data moves between devices by JAX's collectives and lax.ppermute only.
A program may use at most 192 MiB of HBM per device.

v0:
```python
import functools

import jax
import jax.numpy as jnp
import numpy as np
from jax import lax
from jax.experimental import pallas as pl
from jax.experimental.pallas import tpu as pltpu
from jax.sharding import PartitionSpec as P

BOTH = ("row", "col")
SWAP = [(0, 1), (1, 0), (2, 3), (3, 2), (4, 5), (5, 4), (6, 7), (7, 6)]
ROWS, COLS, WIDTH = 18, 72, 128
ROW_N, COL_N = 32, 8
DEVICES = ROW_N * COL_N
HALF = ROWS // 2
PIECE = HALF * COLS
WIRE = 768
LANES = 2 * WIRE
TOTAL = ROW_N * ROWS
GROUP = ROW_N // COL_N
STEP = 256
F32, BF16 = jnp.float32, jnp.bfloat16
EXACT = lax.Precision.HIGHEST


def one_hot(targets, length):
    table = np.zeros((len(targets), length), np.float32)
    table[np.arange(len(targets)), targets] = 1
    return jnp.asarray(table, BF16)


def tables():
    col, row = np.divmod(np.arange(DEVICES), ROW_N)
    by_col = one_hot(row * COL_N + col, DEVICES)
    row, col = np.divmod(np.arange(DEVICES), COL_N)
    by_row = one_hot(col * ROW_N + row, DEVICES)
    half, channel = np.divmod(np.arange(DEVICES), WIDTH)
    by_half = one_hot(channel * 2 + half, DEVICES)
    channel, half = np.divmod(np.arange(DEVICES), 2)
    by_channel = one_hot(half * WIDTH + channel, DEVICES)
    place, row = np.divmod(np.arange(TOTAL), ROW_N)
    col, part = np.divmod(row, GROUP)
    spread = one_hot(col * 128 + part * ROWS + place, COL_N * 128)
    return by_col, by_row, by_half, by_channel, spread


def dot(a, b, contract=((1,), (0,)), precision=None):
    return lax.dot_general(
        a, b, (contract, ((), ())), precision=precision, preferred_element_type=F32
    )


def move(table, values):
    return dot(table[...], values).astype(BF16)


def sigmoid(x):
    return 0.5 * jnp.tanh(0.5 * x) + 0.5


def normalise(values):
    centred = values - jnp.mean(values, axis=0, keepdims=True)
    spread = jnp.mean(centred * centred, axis=0, keepdims=True)
    scale = lax.rsqrt(spread + 1e-05)
    return centred * scale, scale


def normalise_back(d_hat, hat, scale):
    return scale * (
        d_hat
        - jnp.mean(d_hat, axis=0, keepdims=True)
        - hat * jnp.mean(d_hat * hat, axis=0, keepdims=True)
    )


def fill(padded, block):
    for half in range(2):
        padded[pl.ds(half * WIRE, PIECE), :] = block[pl.ds(half * PIECE, PIECE), :]
        padded[pl.ds(half * WIRE + PIECE, WIRE - PIECE), :] = jnp.zeros(
            (WIRE - PIECE, WIDTH), F32
        )


def drain(block, padded):
    for half in range(2):
        block[pl.ds(half * PIECE, PIECE), :] = padded[pl.ds(half * WIRE, PIECE), :]


def place_of(step):
    per = WIRE // STEP
    half = step // per
    return (
        pl.ds(pl.multiple_of(half * WIDTH, WIDTH), WIDTH),
        pl.ds(pl.multiple_of((step - half * per) * STEP, STEP), STEP),
    )


def lanes_of(step):
    return pl.ds(pl.multiple_of(step * STEP, STEP), STEP)


def project_kernel(
    pair, weight_t, bias, gain, shift, mask, by_channel, wire, gate, padded, left_s, right_s
):
    fill(padded, pair)

    @pl.loop(0, LANES // STEP)
    def _(step):
        lanes = lanes_of(step)
        hat, _ = normalise(padded[lanes, :].T)
        normed = hat * gain[...] + shift[...]
        hidden = dot(weight_t[...], normed, precision=EXACT) + bias[...]
        valid = mask[:, lanes]
        rows, cols = place_of(step)
        left = valid * sigmoid(hidden[WIDTH : 2 * WIDTH]) * hidden[:WIDTH]
        left_s[rows, cols] = left.astype(BF16)
        right = valid * sigmoid(hidden[3 * WIDTH : 4 * WIDTH]) * hidden[2 * WIDTH : 3 * WIDTH]
        right_s[rows, cols] = right.astype(BF16)
        gate[:, lanes] = hidden[4 * WIDTH :]

    wire[:, :WIRE] = move(by_channel, left_s[...])
    wire[:, WIRE:] = move(by_channel, right_s[...])


def unpack(values, out, base):
    keep = lax.broadcasted_iota(jnp.int32, (DEVICES, 128), 1) < COLS
    for i in range(HALF):
        tile, offset = divmod(i * COLS, 128)
        part = values[:, tile * 128 : tile * 128 + 256]
        if offset:
            part = pltpu.roll(part, 256 - offset, 1)
        part = jnp.where(keep, part[:, :128], 0.0).astype(BF16)
        for q in range(COL_N):
            out[pl.ds(base + i * ROW_N, ROW_N), q * 128 : (q + 1) * 128] = part[
                q * ROW_N : (q + 1) * ROW_N
            ]


def pack(values, out):
    out[...] = jnp.zeros_like(out)
    for i in range(HALF):
        tile, offset = divmod(i * COLS, 128)
        part = jnp.concatenate(
            [
                values[i * ROW_N : (i + 1) * ROW_N, q * 128 : (q + 1) * 128]
                for q in range(COL_N)
            ],
            axis=0,
        )
        part = jnp.concatenate([part, jnp.zeros_like(part)], axis=1)
        if offset:
            part = pltpu.roll(part, offset, 1)
        out[:, tile * 128 : tile * 128 + 256] += part


def mix_kernel(
    core, left_w, right_w, other_w, by_col, by_row, spread, wire, left_m, right_m, packed
):
    own = core[0] * (TOTAL // 2)
    away = (TOTAL // 2) - own
    unpack(dot(by_col[...], left_w[...]), left_m, 0)
    unpack(dot(by_col[...], right_w[...]), right_m, pl.multiple_of(own, 32))
    unpack(dot(by_col[...], other_w[...]), right_m, pl.multiple_of(away, 32))
    mixed = dot(left_m[...], right_m[...], ((1,), (1,))).astype(BF16)
    pack(dot(mixed, spread[...]), packed)
    wire[...] = move(by_row, packed[...].astype(BF16))


def finish_kernel(
    mixed_w, cotangent, gate, gain, shift, weight, weight_t, bias, by_half, by_channel,
    update, d_wire, d_gate, grad_out, mixed_s, padded, padded_out, d_mixed_s,
):
    fill(padded, cotangent)
    mixed_s[...] = dot(by_half[...], mixed_w[...])
    grad_out[...] = jnp.zeros_like(grad_out)

    @pl.loop(0, LANES // STEP)
    def _(step):
        lanes = lanes_of(step)
        rows, cols = place_of(step)
        hat, scale = normalise(mixed_s[rows, cols])
        normed = hat * gain[...] + shift[...]
        result = dot(weight_t[...], normed, precision=EXACT) + bias[...]
        opened = sigmoid(gate[:, lanes])
        padded_out[lanes, :] = (opened * result).T
        given = padded[lanes, :].T
        d_result = given * opened
        d_gate[:, lanes] = given * result * (opened * (1.0 - opened))
        grad_out[...] += dot(normed, d_result, ((1,), (1,)), EXACT)
        d_hat = dot(weight[...], d_result, precision=EXACT) * gain[...]
        d_mixed_s[rows, cols] = normalise_back(d_hat, hat, scale).astype(BF16)

    drain(update, padded_out)
    d_wire[...] = move(by_channel, d_mixed_s[...])


def unmix_kernel(
    core, d_w, left_m, right_m, by_col, by_row, spread, left_wire, own_wire, away_wire,
    d_mixed_m, terms, packed,
):
    own = core[0] * (TOTAL // 2)
    away = (TOTAL // 2) - own
    unpack(dot(by_col[...], d_w[...]), d_mixed_m, 0)
    d_mixed = dot(d_mixed_m[...], spread[...], ((1,), (1,))).astype(BF16)
    terms[...] = dot(d_mixed, left_m[...], ((0,), (0,)))
    pack(terms[pl.ds(pl.multiple_of(away, 32), TOTAL // 2), :], packed)
    away_wire[...] = move(by_row, packed[...].astype(BF16))
    pack(terms[pl.ds(pl.multiple_of(own, 32), TOTAL // 2), :], packed)
    own_wire[...] = move(by_row, packed[...].astype(BF16))
    pack(dot(d_mixed, right_m[...]), packed)
    left_wire[...] = move(by_row, packed[...].astype(BF16))


def pull_kernel(
    pair, d_left_w, d_right_w, d_gate, weight, weight_t, bias, gain, shift, mask, by_half,
    grad_pair, grad_proj, padded, padded_out, d_left_s, d_right_s,
):
    fill(padded, pair)
    d_left_s[...] = dot(by_half[...], d_left_w[...])
    d_right_s[...] = dot(by_half[...], d_right_w[...])
    grad_proj[...] = jnp.zeros_like(grad_proj)

    @pl.loop(0, LANES // STEP)
    def _(step):
        lanes = lanes_of(step)
        rows, cols = place_of(step)
        hat, scale = normalise(padded[lanes, :].T)
        normed = hat * gain[...] + shift[...]
        hidden = dot(weight_t[: 4 * WIDTH, :], normed, precision=EXACT) + bias[: 4 * WIDTH, :]
        valid = mask[:, lanes]
        parts = []
        for i, ref in enumerate((d_left_s, d_right_s)):
            value = hidden[2 * i * WIDTH : (2 * i + 1) * WIDTH]
            opened = sigmoid(hidden[(2 * i + 1) * WIDTH : (2 * i + 2) * WIDTH])
            given = ref[rows, cols] * valid * opened
            parts += [given, given * value * (1.0 - opened)]
        d_hidden = jnp.concatenate(parts + [d_gate[:, lanes]], axis=0)
        grad_proj[...] += dot(normed, d_hidden, ((1,), (1,)), EXACT)
        d_hat = dot(weight[...], d_hidden, precision=EXACT) * gain[...]
        padded_out[lanes, :] = normalise_back(d_hat, hat, scale).T

    drain(grad_pair, padded_out)


def call(kernel, outs, scratch, *args, smem=0):
    vmem = pl.BlockSpec(memory_space=pltpu.VMEM)
    return pl.pallas_call(
        kernel,
        out_shape=[jax.ShapeDtypeStruct(*o) for o in outs],
        in_specs=[pl.BlockSpec(memory_space=pltpu.SMEM)] * smem + [vmem] * (len(args) - smem),
        out_specs=[vmem] * len(outs),
        scratch_shapes=[pltpu.VMEM(*s) for s in scratch],
        compiler_params=pltpu.CompilerParams(vmem_limit_bytes=48 * 2**20),
    )(*args)


def exchange(chunks):
    return lax.all_to_all(chunks, BOTH, 0, 0, tiled=True)


def shards(
    pair,
    cotangent,
    residue_mask,
    ln_gain,
    ln_bias,
    proj_weight,
    proj_bias,
    norm_gain,
    norm_bias,
    out_weight,
    out_bias,
):
    by_col, by_row, by_half, by_channel, spread = tables()
    shape = pair.shape
    places = ROWS * COLS
    core = (lax.axis_index("col") % 2).astype(jnp.int32).reshape(1)
    valid = residue_mask.astype(F32)
    row_valid = lax.dynamic_slice_in_dim(valid, lax.axis_index("row") * ROWS, ROWS)
    col_valid = lax.dynamic_slice_in_dim(valid, lax.axis_index("col") * COLS, COLS)
    mask = (row_valid[:, None] * col_valid[None, :]).reshape(2, PIECE)
    mask = jnp.pad(mask, ((0, 0), (0, WIRE - PIECE))).reshape(1, LANES)
    pair = pair.reshape(places, WIDTH)
    cotangent = cotangent.reshape(places, WIDTH)
    column = lambda v: v.reshape(-1, 1)
    weight_t = proj_weight.T
    whole = ((LANES, WIDTH), F32)
    halves = lambda kind: ((DEVICES, WIRE), kind)

    wire, gate = call(
        project_kernel,
        [((DEVICES, LANES), BF16), ((WIDTH, LANES), F32)],
        [whole, halves(BF16), halves(BF16)],
        pair, weight_t, column(proj_bias), column(ln_gain), column(ln_bias), mask, by_channel,
    )
    got = exchange(wire.reshape(DEVICES, 2, WIRE))
    right_w = got[:, 1]
    other_w = lax.ppermute(right_w, "col", SWAP)
    wire, left_m, right_m = call(
        mix_kernel,
        [halves(BF16), ((TOTAL // 2, COL_N * 128), BF16), ((TOTAL, COL_N * 128), BF16)],
        [halves(F32)],
        core, got[:, 0], right_w, other_w, by_col, by_row, spread,
        smem=1,
    )
    got = exchange(wire.reshape(DEVICES, 2, WIRE // 2)).reshape(DEVICES, WIRE)
    update, wire, d_gate, grad_out = call(
        finish_kernel,
        [((places, WIDTH), F32), halves(BF16), ((WIDTH, LANES), F32), ((WIDTH, WIDTH), F32)],
        [halves(F32), whole, whole, halves(BF16)],
        got, cotangent, gate, column(norm_gain), column(norm_bias), out_weight, out_weight.T,
        column(out_bias), by_half, by_channel,
    )
    got = exchange(wire.reshape(DEVICES, 2, WIRE // 2)).reshape(DEVICES, WIRE)
    left_wire, own_wire, away_wire = call(
        unmix_kernel,
        [halves(BF16)] * 3,
        [((TOTAL // 2, COL_N * 128), BF16), ((TOTAL, COL_N * 128), F32), halves(F32)],
        core, got, left_m, right_m, by_col, by_row, spread,
        smem=1,
    )
    other_wire = lax.ppermute(away_wire, "col", SWAP)
    right_wire = (own_wire.astype(F32) + other_wire.astype(F32)).astype(BF16)
    got = exchange(jnp.stack([left_wire, right_wire], axis=1))
    grad_pair, proj_term = call(
        pull_kernel,
        [((places, WIDTH), F32), ((WIDTH, 5 * WIDTH), F32)],
        [whole, whole, halves(F32), halves(F32)],
        pair, got[:, 0], got[:, 1], d_gate, proj_weight, weight_t, column(proj_bias),
        column(ln_gain), column(ln_bias), mask, by_half,
    )
    grads = jnp.concatenate([proj_term, grad_out], axis=1)
    pieces = exchange(grads.reshape(DEVICES, -1))
    summed = jnp.sum(pieces, axis=0, keepdims=True)
    grads = exchange(jnp.broadcast_to(summed, pieces.shape)).reshape(grads.shape)
    return (
        update.reshape(shape),
        grad_pair.reshape(shape),
        grads[:, : 5 * WIDTH],
        grads[:, 5 * WIDTH :],
    )


def solution(mesh):
    in_specs = (P("row", "col", None), P("row", "col", None)) + (P(),) * 9
    out_specs = (P("row", "col", None), P("row", "col", None), P(), P())
    return jax.shard_map(shards, mesh=mesh, in_specs=in_specs, out_specs=out_specs, check_vma=False)
```

profile of v0, /device:TPU:1, one launch (start us, length us, event | category | flops | bytes accessed | tf_op | source)
XLA Modules:
  0.0 236.5 jit_solution(8154217685197340173)
XLA Ops:
  0.7 0.8 convert_element_type.14
  1.4 0.1 dynamic_slice.7
  1.5 0.1 dynamic_slice.6
  1.6 0.1 mul.29
  1.7 0.1 mul.34
  1.8 0.1 mul.31
  1.9 0.8 copy.44.gain
  2.7 0.8 copy.45.shift
  3.5 0.8 reshape.101.bias
  4.3 1.1 copy.42
  5.5 5.5 %shard_map.183 = (bf16[256,1536]{1,0:T(8,128)(2,1)S(1)}, f32[128,1536]{1,0:T(8,128)S(1)}) custom-call(f32[1296,128]{1,0:T(8,128)S(1)} %bitcast.36, f32[640,128]{1,0:T(8,128)S(1)} %bitcast.34, f32[640,1]{1,0:T(8,128)S(1)} %reshape.101.bias, f32[128,1]{1,0:T(8,128)S(1)} %copy.44.gain, f32[128,1]{1,0:T(8,128)S(1)} %copy.45.shift, f32[1,1536]{1,0:T(1,128)S(1)} %bitcast.46, ...), custom_call_target="tpu_custom_call" | custom-call | tf_op jit(solution)/shard_map/pallas_call | solution.py:248
  10.9 0.9 copy-done.5
  11.8 0.3 copy.46
  12.1 0.8 copy.47
  12.9 42.4 %all_to_all.36 = bf16[256,2,768]{2,1,0:T(2,128)(2,1)S(1)} all-to-all(bf16[256,2,768]{2,1,0:T(2,128)(2,1)S(1)} %copy.47), channel_id=1, replica_groups=mesh['row'=32,'col'=8] {'row','col'}, dimensions={0} | all-to-all | bytes 1572864 | tf_op jit(solution)/shard_map/all_to_all | solution.py:259
  55.3 2.0 fusion.2
  57.3 0.1 collective-permute-start
  57.4 1.3 copy.73
  58.7 0.6 collective-permute-done.other_w
  59.3 3.7 %shard_map.184 = (bf16[256,768]{1,0:T(8,128)(2,1)S(1)}, bf16[288,1024]{1,0:T(8,128)(2,1)S(1)}, bf16[576,1024]{1,0:T(8,128)(2,1)S(1)}) custom-call(s32[1]{0:T(128)} %bitcast.core, bf16[256,768]{1,0:T(8,128)(2,1)S(1)} %bitcast.42, bf16[256,768]{1,0:T(8,128)(2,1)S(1)} %bitcast.41, bf16[256,768]{1,0:T(8,128)(2,1)} %collective-permute-done.other_w, ...), custom_call_target="tpu_custom_call" | custom-call | tf_op jit(solution)/shard_map/pallas_call | solution.py:248
  63.0 1.0 copy-done.3
  64.0 0.8 copy-done.10
  64.8 0.7 copy-done.20
  65.6 1.9 reshape.90
  67.5 6.6 %all-to-all-start.1 = ((bf16[256,2,384]{2,1,0:T(2,128)(2,1)}), bf16[256,2,384]{2,1,0:T(2,128)(2,1)}, u32[]{:S(2)}, u32[]{:S(2)}) async-start(bf16[256,2,384]{2,1,0:T(2,128)(2,1)} %reshape.90), calls=%async_computation.1 | async-start | bytes 786432 | tf_op jit(solution)/shard_map/all_to_all | solution.py:259
  74.1 1.4 copy.51.gain
  75.5 1.4 copy.52.shift
  76.9 1.4 copy.53.bias
  78.3 1.6 copy.50
  79.8 12.1 %all-to-all-done.1 = bf16[256,2,384]{2,1,0:T(2,128)(2,1)} async-done(((bf16[256,2,384]{2,1,0:T(2,128)(2,1)}), bf16[256,2,384]{2,1,0:T(2,128)(2,1)}, u32[]{:S(2)}, u32[]{:S(2)}) %all-to-all-start.1) | async-done | bytes 393248 | tf_op jit(solution)/shard_map/all_to_all | solution.py:259
  91.9 1.1 copy.66
  93.1 0.9 copy-done.14
  94.0 0.8 copy-done.21
  94.9 0.8 copy-done.22
  95.7 0.8 copy-done.23
  96.5 0.8 copy-done.24
  97.4 0.8 copy-done.25
  98.2 5.0 %shard_map.185 = (f32[1296,128]{1,0:T(8,128)}, bf16[256,768]{1,0:T(8,128)(2,1)S(1)}, f32[128,1536]{1,0:T(8,128)S(1)}, f32[128,128]{1,0:T(8,128)S(1)}) custom-call(bf16[256,768]{1,0:T(8,128)(2,1)S(1)} %bitcast.38, f32[1296,128]{1,0:T(8,128)S(1)} %bitcast.43, f32[128,1536]{1,0:T(8,128)S(1)} %copy-done.6, f32[128,1]{1,0:T(8,128)S(1)} %copy-done.22, ...), custom_call_target="tpu_custom_call" | custom-call | tf_op jit(solution)/shard_map/pallas_call | solution.py:248
  103.2 0.9 copy-done.7
  104.1 0.7 copy-done.19
  104.8 0.6 copy-done.26
  105.5 1.9 reshape.97
  107.4 24.4 %all_to_all.37 = bf16[256,2,384]{2,1,0:T(2,128)(2,1)S(1)} all-to-all(bf16[256,2,384]{2,1,0:T(2,128)(2,1)} %reshape.97), channel_id=1, replica_groups=mesh['row'=32,'col'=8] {'row','col'}, dimensions={0} | all-to-all | bytes 786432 | tf_op jit(solution)/shard_map/all_to_all | solution.py:259
  131.9 3.4 %shard_map.186 = (bf16[256,768]{1,0:T(8,128)(2,1)S(1)}, bf16[256,768]{1,0:T(8,128)(2,1)S(1)}, bf16[256,768]{1,0:T(8,128)(2,1)S(1)}) custom-call(s32[1]{0:T(128)} %bitcast.core, bf16[256,768]{1,0:T(8,128)(2,1)S(1)} %bitcast.39, bf16[288,1024]{1,0:T(8,128)(2,1)S(1)} %copy-done.11, bf16[576,1024]{1,0:T(8,128)(2,1)S(1)} %copy-done.4, ...), custom_call_target="tpu_custom_call" | custom-call | tf_op jit(solution)/shard_map/pallas_call | solution.py:248
  135.3 0.2 collective-permute-start.1
  135.5 1.6 collective-permute-done.1
  137.1 0.1 fusion
  137.2 0.1 pad_maximum_fusion
  137.3 0.8 copy.54
  138.1 31.9 %all_to_all.38 = bf16[256,2,768]{2,1,0:T(2,128)(2,1)S(1)} all-to-all(bf16[256,2,768]{2,1,0:T(2,128)(2,1)S(1)} %copy.54), channel_id=1, replica_groups=mesh['row'=32,'col'=8] {'row','col'}, dimensions={0} | all-to-all | bytes 1572864 | tf_op jit(solution)/shard_map/all_to_all | solution.py:259
  170.0 1.1 fusion.1
  171.1 0.1 copy_bitcast_fusion
  171.2 0.8 copy-done.2
  172.1 0.3 copy-done.8
  172.3 13.8 %shard_map.187 = (f32[1296,128]{1,0:T(8,128)}, f32[128,640]{1,0:T(8,128)S(1)}) custom-call(f32[1296,128]{1,0:T(8,128)S(1)} %bitcast.37, bf16[256,768]{1,0:T(8,128)(2,1)S(1)} %get-tuple-element.37.d_left_w, bf16[256,768]{1,0:T(8,128)(2,1)S(1)} %get-tuple-element.36.d_right_w, f32[128,1536]{1,0:T(8,128)S(1)} %copy-done.8, f32[128,640]{1,0:T(8,128)S(1)} %copy-done.2, ...), custom_call_target="tpu_custom_call" | custom-call | tf_op jit(solution)/shard_map/pallas_call | solution.py:248
  186.2 0.4 all_to_all.29
  186.6 23.2 %all_to_all.39 = f32[256,1,384]{2,1,0:T(1,128)S(1)} all-to-all(f32[256,1,384]{2,1,0:T(1,128)S(1)} %all_to_all.29), channel_id=1, replica_groups=mesh['row'=32,'col'=8] {'row','col'}, dimensions={0} | all-to-all | bytes 786432 | tf_op jit(solution)/shard_map/all_to_all | solution.py:259
  209.8 0.3 reduce_sum.9
  210.1 0.2 broadcast_in_dim.2
  210.3 23.7 %all_to_all.40 = f32[256,1,384]{2,1,0:T(1,128)S(1)} all-to-all(f32[256,1,384]{2,1,0:T(1,128)S(1)} %broadcast_in_dim.2), channel_id=1, replica_groups=mesh['row'=32,'col'=8] {'row','col'}, dimensions={0} | all-to-all | bytes 786432 | tf_op jit(solution)/shard_map/all_to_all | solution.py:259
  234.0 0.9 reduce.1
  235.0 0.1 reshape.100
  235.1 0.6 slice.29
  235.7 0.7 slice.28
  (49 shorter events, 0.4 us)
Async XLA Ops:
  0.6 4.8 %copy-start.13 = (bf16[256,256]{1,0:T(8,128)(2,1)S(1)}, bf16[256,256]{1,0:T(8,128)(2,1)}, u32[]{:S(2)}) copy-start(bf16[256,256]{1,0:T(8,128)(2,1)} %constant.45.clone.by_channel) | copy-start | bytes 393220
  0.6 4.8 %copy-start.1 = (f32[18,72,128]{2,1,0:T(8,128)S(1)}, f32[18,72,128]{2,1,0:T(8,128)}, u32[]{:S(2)}) copy-start(f32[18,72,128]{2,1,0:T(8,128)} %param.16) | copy-start | bytes 1990660
  10.9 0.9 copy-start.5
  57.3 2.0 copy-start
  57.3 2.0 copy-start.15
  57.3 2.0 copy-start.17
  57.3 1.9 collective-permute-start
  63.0 1.0 copy-start.3
  64.0 0.8 copy-start.10
  64.8 0.7 copy-start.20
  65.5 27.5 %copy-start.6 = (f32[128,1536]{1,0:T(8,128)S(1)}, f32[128,1536]{1,0:T(8,128)}, u32[]{:S(2)}) copy-start(f32[128,1536]{1,0:T(8,128)} %copy-done.5) | copy-start | bytes 2359300
  65.6 27.5 %copy-start.12 = (bf16[256,256]{1,0:T(8,128)(2,1)S(1)}, bf16[256,256]{1,0:T(8,128)(2,1)}, u32[]{:S(2)}) copy-start(bf16[256,256]{1,0:T(8,128)(2,1)} %constant.44.clone.by_half) | copy-start | bytes 393220
  67.5 24.4 %all-to-all-start.1 = ((bf16[256,2,384]{2,1,0:T(2,128)(2,1)}), bf16[256,2,384]{2,1,0:T(2,128)(2,1)}, u32[]{:S(2)}, u32[]{:S(2)}) async-start(bf16[256,2,384]{2,1,0:T(2,128)(2,1)} %reshape.90), calls=%async_computation.1 | async-start | bytes 786432 | tf_op jit(solution)/shard_map/all_to_all | solution.py:259
  91.9 1.2 copy-start.9
  93.1 0.9 copy-start.14
  94.0 0.8 copy-start.21
  94.9 0.8 copy-start.22
  95.7 0.8 copy-start.23
  96.5 0.8 copy-start.24
  97.4 0.8 copy-start.25
  103.2 0.9 copy-start.7
  104.1 0.7 copy-start.19
  104.8 0.6 copy-start.26
  105.5 26.4 %copy-start.11 = (bf16[288,1024]{1,0:T(8,128)(2,1)S(1)}, bf16[288,1024]{1,0:T(8,128)(2,1)}, u32[]{:S(2)}) copy-start(bf16[288,1024]{1,0:T(8,128)(2,1)} %copy-done.10) | copy-start | bytes 1769476
  105.5 26.4 %copy-start.16 = (bf16[256,256]{1,0:T(8,128)(2,1)S(1)}, bf16[256,256]{1,0:T(8,128)(2,1)}, u32[]{:S(2)}) copy-start(bf16[256,256]{1,0:T(8,128)(2,1)} %constant.43.clone.by_row) | copy-start | bytes 393220
  107.4 24.5 %copy-start.4 = (bf16[576,1024]{1,0:T(8,128)(2,1)S(1)}, bf16[576,1024]{1,0:T(8,128)(2,1)}, u32[]{:S(2)}) copy-start(bf16[576,1024]{1,0:T(8,128)(2,1)} %copy-done.3) | copy-start | bytes 3538948
  107.4 24.5 %copy-start.18 = (bf16[256,256]{1,0:T(8,128)(2,1)S(1)}, bf16[256,256]{1,0:T(8,128)(2,1)}, u32[]{:S(2)}) copy-start(bf16[256,256]{1,0:T(8,128)(2,1)} %constant.42.clone.by_col) | copy-start | bytes 393220
  135.3 1.8 collective-permute-start.1
  171.1 1.0 copy-start.2
  171.1 1.2 copy-start.8
  172.3 13.8 %copy-start.27 = (f32[128,128]{1,0:T(8,128)S(1)}, f32[128,128]{1,0:T(8,128)}, u32[]{:S(2)}) copy-start(f32[128,128]{1,0:T(8,128)} %copy-done.26) | copy-start | bytes 196612
where the time goes:
time: 237 us; the launch traced here: 236 us
  blocking collectives  146 us (62%)
  local copies, waits for them, and re-layouts  35.2 us (15%)
  Pallas kernels  31.3 us (13%)
  waiting for transfers between devices  14.2 us (6%)
  starting transfers between devices  6.94 us (3%)
    all_to_all x5, blocking collectives, exchange(): return lax.all_to_all(chunks, BOTH, 0, 0, tiled=True)  146 us
    pallas_call x5, Pallas kernels, call(): pl.pallas_call(kernel, out_shape=[jax.ShapeDtypeStruct(*o) for o in outs]...  31.3 us
    unnamed x64, local copies, waits for them, and re-layouts  17.2 us
    all_to_all x1, waiting for transfers between devices, exchange(): return lax.all_to_all(chunks, BOTH, 0, 0, tiled=True)  12.1 us
    all_to_all x1, starting transfers between devices, exchange(): return lax.all_to_all(chunks, BOTH, 0, 0, tiled=True)  6.63 us
    reshape x6, local copies, waits for them, and re-layouts, shards(): column = lambda v: v.reshape(-1, 1)  6.5 us
  transfers between devices with their start and end apart: 3, of which 3 were waited for; matrix products, arithmetic and copies ran while one was open for 3% of the time, Pallas kernels for 0%

commit v1 on v0

v1 whole, which is shorter than its diff:
```python
import jax
import jax.numpy as jnp
import numpy as np
from jax import lax
from jax.experimental import pallas as pl
from jax.experimental.pallas import tpu as pltpu
from jax.sharding import PartitionSpec as P

BOTH = ("row", "col")
SWAP = [(0, 1), (1, 0), (2, 3), (3, 2), (4, 5), (5, 4), (6, 7), (7, 6)]
ROWS, COLS, WIDTH = 18, 72, 128
ROW_N, COL_N = 32, 8
DEVICES = ROW_N * COL_N
HALF = ROWS // 2
PIECE = HALF * COLS
WIRE = 768
LANES = 2 * WIRE
TOTAL = ROW_N * ROWS
GROUP = ROW_N // COL_N
STEP = 256
F32, BF16 = jnp.float32, jnp.bfloat16


def one_hot(targets, length):
    table = np.zeros((len(targets), length), np.float32)
    table[np.arange(len(targets)), targets] = 1
    return jnp.asarray(table, BF16)


def tables():
    col, row = np.divmod(np.arange(DEVICES), ROW_N)
    by_col = one_hot(row * COL_N + col, DEVICES)
    row, col = np.divmod(np.arange(DEVICES), COL_N)
    by_row = one_hot(col * ROW_N + row, DEVICES)
    half, channel = np.divmod(np.arange(DEVICES), WIDTH)
    by_half = one_hot(channel * 2 + half, DEVICES)
    channel, half = np.divmod(np.arange(DEVICES), 2)
    by_channel = one_hot(half * WIDTH + channel, DEVICES)
    place, row = np.divmod(np.arange(TOTAL), ROW_N)
    col, part = np.divmod(row, GROUP)
    spread = one_hot(col * 128 + part * ROWS + place, COL_N * 128)
    return by_col, by_row, by_half, by_channel, spread


PLAIN = ((1,), (0,))
LAST = ((1,), (1,))


def dot(a, b, contract=PLAIN):
    return lax.dot_general(a, b, (contract, ((), ())), preferred_element_type=F32)


def split(x):
    high = x.astype(BF16)
    return high, (x - high.astype(F32)).astype(BF16)


def fine(a, b, contract=PLAIN):
    return dot(a[0], b[0], contract) + (dot(a[0], b[1], contract) + dot(a[1], b[0], contract))


def move(table, values):
    return dot(table[...], values).astype(BF16)


def sigmoid(x):
    return 0.5 * jnp.tanh(0.5 * x) + 0.5


def normalise(values):
    centred = values - jnp.mean(values, axis=0, keepdims=True)
    spread = jnp.mean(centred * centred, axis=0, keepdims=True)
    scale = lax.rsqrt(spread + 1e-05)
    return centred * scale, scale


def normalise_back(d_hat, hat, scale):
    return scale * (
        d_hat
        - jnp.mean(d_hat, axis=0, keepdims=True)
        - hat * jnp.mean(d_hat * hat, axis=0, keepdims=True)
    )


def column(ref):
    return jnp.broadcast_to(ref[...], (8, WIDTH)).T[:, :1]


def columns(ref):
    table = jnp.concatenate([ref[...], jnp.zeros((3, WIDTH), F32)], axis=0).T
    return [table[:, i : i + 1] for i in range(5)]


def fill(padded, block):
    for half in range(2):
        padded[pl.ds(half * WIRE, PIECE), :] = block[pl.ds(half * PIECE, PIECE), :]
        padded[pl.ds(half * WIRE + PIECE, WIRE - PIECE), :] = jnp.zeros(
            (WIRE - PIECE, WIDTH), F32
        )


def drain(block, padded):
    for half in range(2):
        block[pl.ds(half * PIECE, PIECE), :] = padded[pl.ds(half * WIRE, PIECE), :]


def place_of(step):
    per = WIRE // STEP
    half = step // per
    return (
        pl.ds(pl.multiple_of(half * WIDTH, WIDTH), WIDTH),
        pl.ds(pl.multiple_of((step - half * per) * STEP, STEP), STEP),
    )


def lanes_of(step):
    return pl.ds(pl.multiple_of(step * STEP, STEP), STEP)


def build_mask(place, valid_s, valid_v, mask):
    values = jnp.concatenate([valid_v[...].astype(F32), jnp.zeros((1, WIRE - TOTAL), F32)], axis=1)
    values = jnp.broadcast_to(values, (8, WIRE))
    shift = place[1] * COLS
    values = pltpu.roll(values, jnp.where(shift == 0, 0, WIRE - shift), 1)
    lane = lax.broadcasted_iota(jnp.int32, (8, WIRE), 1)
    values = jnp.where(lane < COLS, values, 0.0)
    shifted = [values] + [pltpu.roll(values, i * COLS, 1) for i in range(1, HALF)]
    for half in range(2):
        total = jnp.zeros((8, WIRE), F32)
        for i in range(HALF):
            row = valid_s[place[0] * ROWS + half * HALF + i].astype(F32)
            total = total + row * shifted[i]
        mask[:, half * WIRE : (half + 1) * WIRE] = total[:1]


def project_kernel(
    place, valid_s, valid_v, pair, weight, bias, gain, shift, by_channel,
    wire, mask,
    padded, left_s, right_s,
):
    build_mask(place, valid_s, valid_v, mask)
    fill(padded, pair)
    gain_c, shift_c = column(gain), column(shift)
    bias_c = jnp.concatenate(columns(bias)[:4], axis=0)
    weight_t = split(weight[:, : 4 * WIDTH].T)

    @pl.loop(0, LANES // STEP)
    def _(step):
        lanes = lanes_of(step)
        hat, _ = normalise(padded[lanes, :].T)
        hidden = fine(weight_t, split(hat * gain_c + shift_c)) + bias_c
        valid = mask[:, lanes]
        rows, cols = place_of(step)
        left = valid * sigmoid(hidden[WIDTH : 2 * WIDTH]) * hidden[:WIDTH]
        left_s[rows, cols] = left.astype(BF16)
        right = valid * sigmoid(hidden[3 * WIDTH : 4 * WIDTH]) * hidden[2 * WIDTH : 3 * WIDTH]
        right_s[rows, cols] = right.astype(BF16)

    wire[:, :WIRE] = move(by_channel, left_s[...])
    wire[:, WIRE:] = move(by_channel, right_s[...])


def prepare_kernel(
    mask, pair, cotangent, weight, bias, gain, shift, out_gain, out_weight,
    hat_o, scale_o, factors, opened_o, d_result_o, d_hat_o,
    padded, padded_c,
):
    fill(padded, pair)
    fill(padded_c, cotangent)
    gain_c, shift_c, out_gain_c = column(gain), column(shift), column(out_gain)
    bias_c = jnp.concatenate(columns(bias), axis=0)
    weight_t = split(weight[...].T)
    out_w = split(out_weight[...])

    @pl.loop(0, LANES // STEP)
    def _(step):
        lanes = lanes_of(step)
        hat, scale = normalise(padded[lanes, :].T)
        hat_o[:, lanes] = hat
        scale_o[:, lanes] = scale
        hidden = fine(weight_t, split(hat * gain_c + shift_c)) + bias_c
        valid = mask[:, lanes]
        for i in range(2):
            opened = sigmoid(hidden[(2 * i + 1) * WIDTH : (2 * i + 2) * WIDTH])
            factor = valid * opened
            factors[2 * i * WIDTH : (2 * i + 1) * WIDTH, lanes] = factor
            factors[(2 * i + 1) * WIDTH : (2 * i + 2) * WIDTH, lanes] = (
                factor * (1.0 - opened) * hidden[2 * i * WIDTH : (2 * i + 1) * WIDTH]
            )
        opened = sigmoid(hidden[4 * WIDTH :])
        opened_o[:, lanes] = opened
        d_result = padded_c[lanes, :].T * opened
        d_result_o[:, lanes] = d_result
        d_hat_o[:, lanes] = fine(out_w, split(d_result)) * out_gain_c


def unpack(values, out, base):
    keep = lax.broadcasted_iota(jnp.int32, (DEVICES, 128), 1) < COLS
    for i in range(HALF):
        tile, offset = divmod(i * COLS, 128)
        part = values[:, tile * 128 : tile * 128 + 256]
        if offset:
            part = pltpu.roll(part, 256 - offset, 1)
        part = jnp.where(keep, part[:, :128], 0.0).astype(BF16)
        for q in range(COL_N):
            out[pl.ds(base + i * ROW_N, ROW_N), q * 128 : (q + 1) * 128] = part[
                q * ROW_N : (q + 1) * ROW_N
            ]


def pack(values, out):
    out[...] = jnp.zeros_like(out)
    for i in range(HALF):
        tile, offset = divmod(i * COLS, 128)
        part = jnp.concatenate(
            [
                values[i * ROW_N : (i + 1) * ROW_N, q * 128 : (q + 1) * 128]
                for q in range(COL_N)
            ],
            axis=0,
        )
        part = jnp.concatenate([part, jnp.zeros_like(part)], axis=1)
        if offset:
            part = pltpu.roll(part, offset, 1)
        out[:, tile * 128 : tile * 128 + 256] += part


def mix_kernel(place, both_w, other_w, by_col, by_row, spread, wire, left_m, right_m, packed):
    own = place[2] * (TOTAL // 2)
    away = (TOTAL // 2) - own
    unpack(dot(by_col[...], both_w[:, :WIRE]), left_m, 0)
    unpack(dot(by_col[...], both_w[:, WIRE:]), right_m, pl.multiple_of(own, 32))
    unpack(dot(by_col[...], other_w[...]), right_m, pl.multiple_of(away, 32))
    mixed = dot(left_m[...], right_m[...], LAST).astype(BF16)
    pack(dot(mixed, spread[...]), packed)
    wire[...] = move(by_row, packed[...].astype(BF16))


def turn_kernel(mixed_w, d_hat, by_half, by_channel, wire, hat_o, mixed_s, d_mixed_s):
    mixed_s[...] = dot(by_half[...], mixed_w[...])

    @pl.loop(0, LANES // STEP)
    def _(step):
        lanes = lanes_of(step)
        rows, cols = place_of(step)
        hat, scale = normalise(mixed_s[rows, cols])
        hat_o[:, lanes] = hat
        d_mixed_s[rows, cols] = normalise_back(d_hat[:, lanes], hat, scale).astype(BF16)

    wire[...] = move(by_channel, d_mixed_s[...])


def update_kernel(
    hat_m, opened, d_result, hat, weight, gain, shift, out_gain, out_shift, out_weight, out_bias,
    update, grad_out, grad_gate, d_normed,
    padded,
):
    gain_c, shift_c = column(gain), column(shift)
    out_gain_c, out_shift_c, out_bias_c = column(out_gain), column(out_shift), column(out_bias)
    out_t = split(out_weight[...].T)
    gate_w = split(weight[:, 4 * WIDTH :])
    grad_out[...] = jnp.zeros_like(grad_out)
    grad_gate[...] = jnp.zeros_like(grad_gate)

    @pl.loop(0, LANES // STEP)
    def _(step):
        lanes = lanes_of(step)
        normed = split(hat_m[:, lanes] * out_gain_c + out_shift_c)
        result = fine(out_t, normed) + out_bias_c
        is_open = opened[:, lanes]
        padded[lanes, :] = (is_open * result).T
        given = d_result[:, lanes]
        grad_out[...] += fine(normed, split(given), LAST)
        d_gate = split(given * result * (1.0 - is_open))
        grad_gate[...] += fine(split(hat[:, lanes] * gain_c + shift_c), d_gate, LAST)
        d_normed[:, lanes] = fine(gate_w, d_gate)

    drain(update, padded)


def unmix_kernel(
    place, d_w, left_m, right_m, by_col, by_row, spread,
    left_wire, own_wire, away_wire,
    d_mixed_m, terms, packed,
):
    own = place[2] * (TOTAL // 2)
    away = (TOTAL // 2) - own
    unpack(dot(by_col[...], d_w[...]), d_mixed_m, 0)
    d_mixed = dot(d_mixed_m[...], spread[...], LAST).astype(BF16)
    terms[...] = dot(d_mixed, left_m[...], ((0,), (0,)))
    pack(terms[pl.ds(pl.multiple_of(away, 32), TOTAL // 2), :], packed)
    away_wire[...] = move(by_row, packed[...].astype(BF16))
    pack(terms[pl.ds(pl.multiple_of(own, 32), TOTAL // 2), :], packed)
    own_wire[...] = move(by_row, packed[...].astype(BF16))
    pack(dot(d_mixed, right_m[...]), packed)
    left_wire[...] = move(by_row, packed[...].astype(BF16))


def d_hidden_of(d_left_s, d_right_s, factors, step):
    rows, cols = place_of(step)
    lanes = lanes_of(step)
    parts = []
    for i, ref in enumerate((d_left_s, d_right_s)):
        given = ref[rows, cols]
        for j in range(2):
            start = (2 * i + j) * WIDTH
            parts.append(given * factors[start : start + WIDTH, lanes])
    return split(jnp.concatenate(parts, axis=0))


def weight_kernel(
    both_w, factors, hat, gain, shift, grad_gate, grad_out, by_half,
    grads,
    d_left_s, d_right_s, total,
):
    d_left_s[...] = dot(by_half[...], both_w[:, :WIRE])
    d_right_s[...] = dot(by_half[...], both_w[:, WIRE:])
    gain_c, shift_c = column(gain), column(shift)
    total[...] = jnp.zeros_like(total)

    @pl.loop(0, LANES // STEP)
    def _(step):
        d_hidden = d_hidden_of(d_left_s, d_right_s, factors, step)
        normed = split(hat[:, lanes_of(step)] * gain_c + shift_c)
        total[...] += fine(normed, d_hidden, LAST)

    grads[:WIDTH, :] = total[:, : 3 * WIDTH]
    grads[WIDTH:, :WIDTH] = total[:, 3 * WIDTH :]
    grads[WIDTH:, WIDTH : 2 * WIDTH] = grad_gate[...]
    grads[WIDTH:, 2 * WIDTH :] = grad_out[...]


def pair_kernel(
    both_w, factors, hat, scale, d_normed, weight, gain, by_half,
    grad_pair,
    d_left_s, d_right_s, padded,
):
    d_left_s[...] = dot(by_half[...], both_w[:, :WIRE])
    d_right_s[...] = dot(by_half[...], both_w[:, WIRE:])
    gain_c = column(gain)
    weight_s = split(weight[:, : 4 * WIDTH])

    @pl.loop(0, LANES // STEP)
    def _(step):
        lanes = lanes_of(step)
        d_hidden = d_hidden_of(d_left_s, d_right_s, factors, step)
        d_hat = (fine(weight_s, d_hidden) + d_normed[:, lanes]) * gain_c
        padded[lanes, :] = normalise_back(d_hat, hat[:, lanes], scale[:, lanes]).T

    drain(grad_pair, padded)


def call(kernel, outs, scratch, *args, smem=0, work=2e9):
    whole = lambda shape: pl.BlockSpec(shape, lambda i: (0,) * len(shape))
    scalars = [pl.BlockSpec(memory_space=pltpu.SMEM)] * smem
    return pl.pallas_call(
        kernel,
        grid=(1,),
        out_shape=[jax.ShapeDtypeStruct(*o) for o in outs],
        in_specs=scalars + [whole(a.shape) for a in args[smem:]],
        out_specs=[whole(o[0]) for o in outs],
        scratch_shapes=[pltpu.VMEM(*s) for s in scratch],
        compiler_params=pltpu.CompilerParams(vmem_limit_bytes=48 * 2**20),
        cost_estimate=pl.CostEstimate(flops=int(work), bytes_accessed=4 * 2**20, transcendentals=0),
    )(*args)


def exchange(chunks):
    return lax.all_to_all(chunks, BOTH, 0, 0, tiled=True)


def shards(
    pair,
    cotangent,
    residue_mask,
    ln_gain,
    ln_bias,
    proj_weight,
    proj_bias,
    norm_gain,
    norm_bias,
    out_weight,
    out_bias,
):
    by_col, by_row, by_half, by_channel, spread = tables()
    shape = pair.shape
    places = ROWS * COLS
    row, col = lax.axis_index("row"), lax.axis_index("col")
    place = jnp.stack([row, col, col % 2]).astype(jnp.int32)
    pair = pair.reshape(places, WIDTH)
    cotangent = cotangent.reshape(places, WIDTH)
    line = lambda v: v.reshape(-1, WIDTH)
    gain, shift, bias = line(ln_gain), line(ln_bias), line(proj_bias)
    out_gain, out_shift, out_bias = line(norm_gain), line(norm_bias), line(out_bias)
    whole = ((LANES, WIDTH), F32)
    turned = ((WIDTH, LANES), F32)
    square = ((WIDTH, WIDTH), F32)
    halves = lambda kind: ((DEVICES, WIRE), kind)

    wire, mask = call(
        project_kernel,
        [((DEVICES, LANES), BF16), ((1, LANES), F32)],
        [whole, halves(BF16), halves(BF16)],
        place, residue_mask, residue_mask.reshape(1, TOTAL), pair, proj_weight, bias, gain, shift,
        by_channel,
        smem=2,
    )
    got = exchange(wire.reshape(DEVICES, 2, WIRE)).reshape(DEVICES, LANES)
    hat, scale, factors, opened, d_result, d_hat = call(
        prepare_kernel,
        [turned, ((1, LANES), F32), ((4 * WIDTH, LANES), F32), turned, turned, turned],
        [whole, whole],
        mask, pair, cotangent, proj_weight, bias, gain, shift, out_gain, out_weight,
        work=1e10,
    )
    other_w = lax.ppermute(got[:, WIRE:], "col", SWAP)
    wire, left_m, right_m = call(
        mix_kernel,
        [halves(BF16), ((TOTAL // 2, COL_N * 128), BF16), ((TOTAL, COL_N * 128), BF16)],
        [halves(F32)],
        place, got, other_w, by_col, by_row, spread,
        smem=1,
    )
    got = exchange(wire.reshape(DEVICES, 2, WIRE // 2)).reshape(DEVICES, WIRE)
    wire, hat_m = call(
        turn_kernel,
        [halves(BF16), turned],
        [halves(F32), halves(BF16)],
        got, d_hat, by_half, by_channel,
    )
    got = exchange(wire.reshape(DEVICES, 2, WIRE // 2)).reshape(DEVICES, WIRE)
    update, grad_out, grad_gate, d_normed = call(
        update_kernel,
        [((places, WIDTH), F32), square, square, turned],
        [whole],
        hat_m, opened, d_result, hat, proj_weight, gain, shift, out_gain, out_shift, out_weight,
        out_bias,
        work=8e9,
    )
    left_wire, own_wire, away_wire = call(
        unmix_kernel,
        [halves(BF16)] * 3,
        [((TOTAL // 2, COL_N * 128), BF16), ((TOTAL, COL_N * 128), F32), halves(F32)],
        place, got, left_m, right_m, by_col, by_row, spread,
        smem=1,
    )
    other_wire = lax.ppermute(away_wire, "col", SWAP)
    right_wire = (own_wire.astype(F32) + other_wire.astype(F32)).astype(BF16)
    got = exchange(jnp.stack([left_wire, right_wire], axis=1)).reshape(DEVICES, LANES)
    (grads,) = call(
        weight_kernel,
        [((DEVICES, 3 * WIDTH), F32)],
        [halves(F32), halves(F32), ((WIDTH, 4 * WIDTH), F32)],
        got, factors, hat, gain, shift, grad_gate, grad_out, by_half,
    )
    pieces = exchange(grads)
    (grad_pair,) = call(
        pair_kernel,
        [((places, WIDTH), F32)],
        [halves(F32), halves(F32), whole],
        got, factors, hat, scale, d_normed, proj_weight, gain, by_half,
        work=8e9,
    )
    summed = jnp.sum(pieces, axis=0, keepdims=True)
    grads = exchange(jnp.broadcast_to(summed, pieces.shape))
    grad_proj = jnp.concatenate([grads[:WIDTH], grads[WIDTH:, : 2 * WIDTH]], axis=1)
    return update.reshape(shape), grad_pair.reshape(shape), grad_proj, grads[WIDTH:, 2 * WIDTH :]


def solution(mesh):
    in_specs = (P("row", "col", None), P("row", "col", None)) + (P(),) * 9
    out_specs = (P("row", "col", None), P("row", "col", None), P(), P())
    return jax.shard_map(shards, mesh=mesh, in_specs=in_specs, out_specs=out_specs, check_vma=False)
```

time: 237 us -> 214 us (0.903)
  blocking collectives: 146 us -> 90.1 us
  waiting for transfers between devices: 14.2 us -> 43.4 us
  starting transfers between devices: 6.94 us -> 17.5 us
  local copies, waits for them, and re-layouts: 35.2 us -> 28 us
    all_to_all x5 -> x3, blocking collectives: 146 us -> 90.1 us  [exchange(): return lax.all_to_all(chunks, BOTH, 0, 0, tiled=True)]
    all_to_all x1 -> x3, waiting for transfers between devices: 12.1 us -> 40.1 us  [exchange(): return lax.all_to_all(chunks, BOTH, 0, 0, tiled=True)]
    all_to_all x1 -> x3, starting transfers between devices: 6.63 us -> 17.1 us  [exchange(): return lax.all_to_all(chunks, BOTH, 0, 0, tiled=True)]
    reshape x8 -> x2, local copies, waits for them, and re-layouts: 7.44 us -> 0.87 us  [the longest x1 0.69 us: shards(): residue_mask.reshape(1, TOTAL)]
    unnamed x64 -> x84, local copies, waits for them, and re-layouts: 17.2 us -> 21.7 us
    slice x4, local copies, waits for them, and re-layouts: 4.46 us -> 0.76 us  [the longest x1 0.63 us: shards(): grads[WIDTH:, 2 * WIDTH:]]
    pallas_call x5 -> x8, Pallas kernels: 31.3 us -> 31.5 us  [call(): pl.pallas_call(kernel, grid=(1,), out_shape=[jax.ShapeDtypeStruct(*o) for...]
  transfers between devices with their start and end apart: 3 -> 5, of which waited for: 3 -> 5; matrix products, arithmetic and copies ran while one was open for 3% -> 0% of each run, Pallas kernels for 0% -> 7%
where the time goes in v1:
time: 214 us; the launch traced here: 213 us
  blocking collectives  90.1 us (42%)
  waiting for transfers between devices  43.4 us (20%)
  Pallas kernels  31.5 us (15%)
  local copies, waits for them, and re-layouts  28 us (13%)
  starting transfers between devices  17.5 us (8%)
    all_to_all x3, blocking collectives, exchange(): return lax.all_to_all(chunks, BOTH, 0, 0, tiled=True)  90.1 us
    all_to_all x3, waiting for transfers between devices, exchange(): return lax.all_to_all(chunks, BOTH, 0, 0, tiled=True)  40.1 us
    pallas_call x8, Pallas kernels, call(): pl.pallas_call(kernel, grid=(1,), out_shape=[jax.ShapeDtypeStruct(*o) for...  31.5 us
    unnamed x84, local copies, waits for them, and re-layouts  21.7 us
    all_to_all x3, starting transfers between devices, exchange(): return lax.all_to_all(chunks, BOTH, 0, 0, tiled=True)  17.1 us
  transfers between devices with their start and end apart: 5, of which 5 were waited for; matrix products, arithmetic and copies ran while one was open for 0% of the time, Pallas kernels for 7%

profile of v1, /device:TPU:1, one launch (start us, length us, event | category | flops | bytes accessed | tf_op | source)
XLA Modules:
  0.0 212.7 jit_solution(4514841508489430562)
XLA Ops:
  0.6 0.7 reshape.71.valid_v
  1.3 0.1 pad_add_fusion.place
  1.4 0.7 copy-done
  2.1 1.1 copy-done.1
  3.2 1.0 copy-done.4
  4.2 0.7 copy-done.7
  4.8 0.7 copy-done.12
  5.5 0.7 copy-done.14
  6.2 0.9 copy-done.21
  7.1 4.5 %shard_map.183 = (bf16[256,1536]{1,0:T(8,128)(2,1)S(1)}, f32[1,1536]{1,0:T(1,128)S(1)}) custom-call(s32[3]{0:T(128)S(1)} %pad_add_fusion.place, s32[576]{0:T(1024)S(1)} %copy-done, s32[1,576]{1,0:T(1,128)S(1)} %reshape.71.valid_v, f32[1296,128]{1,0:T(8,128)S(1)} %bitcast.39, f32[128,640]{1,0:T(8,128)S(1)} %copy-done.4, f32[5,128]{1,0:T(8,128)S(1)} %bitcast.42, ...), custom_call_target="tpu_custom_call" | custom-call | flops 2000000000 | bytes 4194304 | tf_op jit(solution)/shard_map/pallas_call | solution.py:356
  11.6 0.2 reshape.76
  11.7 42.4 %all_to_all.38 = bf16[256,2,768]{2,1,0:T(2,128)(2,1)S(1)} all-to-all(bf16[256,2,768]{2,1,0:T(2,128)(2,1)S(1)} %reshape.76), channel_id=1, replica_groups=mesh['row'=32,'col'=8] {'row','col'}, dimensions={0} | all-to-all | bytes 1572864 | tf_op jit(solution)/shard_map/all_to_all | solution.py:369
  54.1 0.1 copy.25
  54.2 0.1 collective-permute-start
  54.3 1.7 collective-permute-done.other_w
  56.1 3.2 %shard_map.184 = (bf16[256,768]{1,0:T(8,128)(2,1)S(1)}, bf16[288,1024]{1,0:T(8,128)(2,1)S(1)}, bf16[576,1024]{1,0:T(8,128)(2,1)S(1)}) custom-call(s32[3]{0:T(128)S(1)} %pad_add_fusion.place, bf16[256,1536]{1,0:T(8,128)(2,1)S(1)} %bitcast.32, bf16[256,768]{1,0:T(8,128)(2,1)S(1)} %collective-permute-done.other_w, bf16[256,256]{1,0:T(8,128)(2,1)S(1)} %copy-done.19, ...), custom_call_target="tpu_custom_call" | custom-call | flops 2000000000 | bytes 4194304 | tf_op jit(solution)/shard_map/pallas_call | solution.py:356
  59.3 1.0 copy-done.25
  60.4 0.8 copy-done.27
  61.2 0.0 copy-start.9
  61.2 0.0 copy-start.13
  61.2 0.8 reshape.78
  62.1 5.2 %all-to-all-start.1 = ((bf16[256,2,384]{2,1,0:T(2,128)(2,1)}), bf16[256,2,384]{2,1,0:T(2,128)(2,1)S(1)}, u32[]{:S(2)}, u32[]{:S(2)}) async-start(bf16[256,2,384]{2,1,0:T(2,128)(2,1)} %reshape.78), calls=%async_computation.1 | async-start | bytes 786432 | tf_op jit(solution)/shard_map/all_to_all | solution.py:369
  67.3 0.0 copy-start.18
  67.3 0.0 copy-start.22
  67.4 7.0 %shard_map.185 = (f32[128,1536]{1,0:T(8,128)S(1)}, f32[1,1536]{1,0:T(1,128)S(1)}, f32[512,1536]{1,0:T(8,128)}, f32[128,1536]{1,0:T(8,128)S(1)}, f32[128,1536]{1,0:T(8,128)S(1)}, /*index=5*/f32[128,1536]{1,0:T(8,128)S(1)}) custom-call(f32[1,1536]{1,0:T(1,128)S(1)} %get-tuple-element.26.mask, f32[1296,128]{1,0:T(8,128)S(1)} %bitcast.40, ...), custom_call_target="tpu_custom_call" | custom-call | flops 10000000000 | bytes 4194304 | tf_op jit(solution)/shard_map/pallas_call | solution.py:356
  74.4 0.9 copy-done.31
  75.3 0.9 copy-done.35
  76.2 0.9 copy-done.37
  77.0 8.8 %all-to-all-done.1 = bf16[256,2,384]{2,1,0:T(2,128)(2,1)S(1)} async-done(((bf16[256,2,384]{2,1,0:T(2,128)(2,1)}), bf16[256,2,384]{2,1,0:T(2,128)(2,1)S(1)}, u32[]{:S(2)}, u32[]{:S(2)}) %all-to-all-start.1) | async-done | bytes 393248 | tf_op jit(solution)/shard_map/all_to_all | solution.py:369
  85.9 0.1 copy.26
  85.9 1.1 copy-done.32
  87.1 1.3 shard_map.186
  88.4 0.9 copy-done.29
  89.3 0.8 reshape.85
  90.1 24.5 %all_to_all.39 = bf16[256,2,384]{2,1,0:T(2,128)(2,1)S(1)} all-to-all(bf16[256,2,384]{2,1,0:T(2,128)(2,1)} %reshape.85), channel_id=1, replica_groups=mesh['row'=32,'col'=8] {'row','col'}, dimensions={0} | all-to-all | bytes 786432 | tf_op jit(solution)/shard_map/all_to_all | solution.py:369
  114.6 0.1 copy.27
  114.6 0.0 copy-start.28
  114.7 1.1 copy-done.28
  115.7 3.9 %shard_map.188 = (bf16[256,768]{1,0:T(8,128)(2,1)S(1)}, bf16[256,768]{1,0:T(8,128)(2,1)S(1)}, bf16[256,768]{1,0:T(8,128)(2,1)S(1)}) custom-call(s32[3]{0:T(128)S(1)} %pad_add_fusion.place, bf16[256,768]{1,0:T(8,128)(2,1)S(1)} %bitcast.35, bf16[288,1024]{1,0:T(8,128)(2,1)S(1)} %copy-done.28, bf16[576,1024]{1,0:T(8,128)(2,1)S(1)} %copy-done.26, ...), custom_call_target="tpu_custom_call" | custom-call | flops 2000000000 | bytes 4194304 | tf_op jit(solution)/shard_map/pallas_call | solution.py:356
  119.6 0.2 collective-permute-start.1
  119.8 1.6 collective-permute-done.1
  121.4 0.1 fusion
  121.5 0.1 pad_maximum_fusion
  121.6 1.7 copy.21
  123.3 6.8 %all-to-all-start.3 = ((bf16[256,2,768]{2,1,0:T(2,128)(2,1)}), bf16[256,2,768]{2,1,0:T(2,128)(2,1)}, u32[]{:S(2)}, u32[]{:S(2)}) async-start(bf16[256,2,768]{2,1,0:T(2,128)(2,1)} %copy.21), calls=%async_computation.3 | async-start | bytes 1572864 | tf_op jit(solution)/shard_map/all_to_all | solution.py:369
  130.2 1.1 copy-done.36
  131.3 1.1 copy-done.38
  132.4 4.7 %shard_map.187 = (f32[1296,128]{1,0:T(8,128)}, f32[128,128]{1,0:T(8,128)S(1)}, f32[128,128]{1,0:T(8,128)S(1)}, f32[128,1536]{1,0:T(8,128)S(1)}) custom-call(f32[128,1536]{1,0:T(8,128)S(1)} %copy-done.30, f32[128,1536]{1,0:T(8,128)S(1)} %copy-done.36, f32[128,1536]{1,0:T(8,128)S(1)} %copy-done.38, f32[128,1536]{1,0:T(8,128)S(1)} %get-tuple-element.31.hat, ...), custom_call_target="tpu_custom_call" | custom-call | flops 8000000000 | bytes 4194304 | tf_op jit(solution)/shard_map/pallas_call | solution.py:356
  137.1 0.9 copy-done.33
  138.0 18.4 %all-to-all-done.3 = bf16[256,2,768]{2,1,0:T(2,128)(2,1)} async-done(((bf16[256,2,768]{2,1,0:T(2,128)(2,1)}), bf16[256,2,768]{2,1,0:T(2,128)(2,1)}, u32[]{:S(2)}, u32[]{:S(2)}) %all-to-all-start.3) | async-done | bytes 786464 | tf_op jit(solution)/shard_map/all_to_all | solution.py:369
  156.3 1.2 copy.28
  157.6 1.9 copy-done.23
  159.4 3.0 %shard_map.190 = f32[256,384]{1,0:T(8,128)S(1)} custom-call(bf16[256,1536]{1,0:T(8,128)(2,1)S(1)} %bitcast.33, f32[512,1536]{1,0:T(8,128)S(1)} %copy-done.23, f32[128,1536]{1,0:T(8,128)S(1)} %get-tuple-element.31.hat, f32[1,128]{1,0:T(1,128)S(1)} %bitcast.55, f32[1,128]{1,0:T(1,128)S(1)} %bitcast.51, f32[128,128]{1,0:T(8,128)S(1)} %get-tuple-element.42.grad_gate, ...), custom_call_target="tpu_custom_call" | custom-call | flops 2000000000 | bytes 4194304 | tf_op jit(solution)/shard_map/pallas_call | solution.py:356
  162.5 0.4 copy.22
  162.9 23.2 %all_to_all.40 = f32[256,1,384]{2,1,0:T(1,128)S(1)} all-to-all(f32[256,1,384]{2,1,0:T(1,128)S(1)} %copy.22), channel_id=1, replica_groups=mesh['row'=32,'col'=8] {'row','col'}, dimensions={0} | all-to-all | bytes 786432 | tf_op jit(solution)/shard_map/all_to_all | solution.py:369
  186.1 0.3 reduce_sum.9
  186.4 1.0 broadcast_in_dim.2
  187.4 5.2 %all-to-all-start.5 = ((f32[256,1,384]{2,1,0:T(1,128)}), f32[256,1,384]{2,1,0:T(1,128)S(1)}, u32[]{:S(2)}, u32[]{:S(2)}) async-start(f32[256,1,384]{2,1,0:T(1,128)} %broadcast_in_dim.2), calls=%async_computation.5 | async-start | bytes 786432 | tf_op jit(solution)/shard_map/all_to_all | solution.py:369
  192.6 1.9 copy-done.24
  194.5 3.8 %shard_map.189 = f32[1296,128]{1,0:T(8,128)} custom-call(bf16[256,1536]{1,0:T(8,128)(2,1)S(1)} %bitcast.34, f32[512,1536]{1,0:T(8,128)S(1)} %copy-done.24, f32[128,1536]{1,0:T(8,128)S(1)} %get-tuple-element.31.hat, f32[1,1536]{1,0:T(1,128)S(1)} %get-tuple-element.40.scale, f32[128,1536]{1,0:T(8,128)S(1)} %copy-done.34, f32[128,640]{1,0:T(8,128)S(1)} %copy-done.5, ...), custom_call_target="tpu_custom_call" | custom-call | flops 8000000000 | bytes 4194304 | tf_op jit(solution)/shard_map/pallas_call | solution.py:356
  198.3 12.9 %all-to-all-done.5 = f32[256,1,384]{2,1,0:T(1,128)S(1)} async-done(((f32[256,1,384]{2,1,0:T(1,128)}), f32[256,1,384]{2,1,0:T(1,128)S(1)}, u32[]{:S(2)}, u32[]{:S(2)}) %all-to-all-start.5) | async-done | bytes 393248 | tf_op jit(solution)/shard_map/all_to_all | solution.py:369
  211.2 0.6 slice.23
  211.9 0.1 slice.21
  212.0 0.7 pad_maximum_fusion.1
  (57 shorter events, 0.2 us)
Async XLA Ops:
  1.4 0.7 copy-start
  2.1 1.1 copy-start.1
  3.2 1.0 copy-start.4
  4.2 0.7 copy-start.7
  4.8 0.7 copy-start.12
  5.5 0.7 copy-start.14
  6.2 0.9 copy-start.21
  54.1 1.9 copy-start.16
  54.1 1.9 copy-start.19
  54.1 1.9 copy-start.20
  54.2 1.8 collective-permute-start
  56.1 11.2 %copy-start.5 = (f32[128,640]{1,0:T(8,128)S(1)}, f32[128,640]{1,0:T(8,128)}, u32[]{:S(2)}) copy-start(f32[128,640]{1,0:T(8,128)} %weight.7) | copy-start | bytes 983044
  59.3 1.0 copy-start.25
  60.4 0.8 copy-start.27
  61.2 6.1 %copy-start.2 = (f32[18,72,128]{2,1,0:T(8,128)S(1)}, f32[18,72,128]{2,1,0:T(8,128)}, u32[]{:S(2)}) copy-start(f32[18,72,128]{2,1,0:T(8,128)} %param.16) | copy-start | bytes 1990660
  61.2 6.1 %copy-start.3 = (f32[18,72,128]{2,1,0:T(8,128)S(1)}, f32[18,72,128]{2,1,0:T(8,128)}, u32[]{:S(2)}) copy-start(f32[18,72,128]{2,1,0:T(8,128)} %param.17) | copy-start | bytes 1990660
  61.2 6.1 %copy-start.6 = (f32[128,128]{1,0:T(8,128)S(1)}, f32[128,128]{1,0:T(8,128)}, u32[]{:S(2)}) copy-start(f32[128,128]{1,0:T(8,128)} %out_weight.3) | copy-start | bytes 196612
  61.2 6.1 %copy-start.8 = (f32[640]{0:T(1024)S(1)}, f32[640]{0:T(1024)}, u32[]{:S(2)}) copy-start(f32[640]{0:T(1024)} %param.22) | copy-start | bytes 7684
  61.2 6.1 %copy-start.9 = (f32[128]{0:T(128)S(1)}, f32[128]{0:T(128)}, u32[]{:S(2)}) copy-start(f32[128]{0:T(128)} %param.23) | copy-start | bytes 1540
  61.2 6.1 %copy-start.13 = (f32[128]{0:T(128)S(1)}, f32[128]{0:T(128)}, u32[]{:S(2)}) copy-start(f32[128]{0:T(128)} %param.20) | copy-start | bytes 1540
  61.2 6.1 %copy-start.15 = (f32[128]{0:T(128)S(1)}, f32[128]{0:T(128)}, u32[]{:S(2)}) copy-start(f32[128]{0:T(128)} %param.19) | copy-start | bytes 1540
  62.1 23.8 %all-to-all-start.1 = ((bf16[256,2,384]{2,1,0:T(2,128)(2,1)}), bf16[256,2,384]{2,1,0:T(2,128)(2,1)S(1)}, u32[]{:S(2)}, u32[]{:S(2)}) async-start(bf16[256,2,384]{2,1,0:T(2,128)(2,1)} %reshape.78), calls=%async_computation.1 | async-start | bytes 786432 | tf_op jit(solution)/shard_map/all_to_all | solution.py:369
  67.3 18.6 %copy-start.18 = (bf16[256,256]{1,0:T(8,128)(2,1)S(1)}, bf16[256,256]{1,0:T(8,128)(2,1)}, u32[]{:S(2)}) copy-start(bf16[256,256]{1,0:T(8,128)(2,1)} %constant.36.clone.by_half) | copy-start | bytes 393220
  67.3 18.6 %copy-start.22 = (bf16[256,256]{1,0:T(8,128)(2,1)S(1)}, bf16[256,256]{1,0:T(8,128)(2,1)}, u32[]{:S(2)}) copy-start(bf16[256,256]{1,0:T(8,128)(2,1)} %constant.37.clone.by_channel) | copy-start | bytes 393220
  74.4 0.9 copy-start.31
  75.3 0.9 copy-start.35
  76.2 0.9 copy-start.37
  85.9 1.1 copy-start.32
  88.4 0.9 copy-start.29
  89.3 25.4 %copy-start.17 = (bf16[576,1024]{1,0:T(8,128)(2,1)S(1)}, bf16[576,1024]{1,0:T(8,128)(2,1)}, u32[]{:S(2)}) copy-start(bf16[576,1024]{1,0:T(8,128)(2,1)} %constant.38.clone.spread) | copy-start | bytes 3538948
  90.1 24.5 %copy-start.26 = (bf16[576,1024]{1,0:T(8,128)(2,1)S(1)}, bf16[576,1024]{1,0:T(8,128)(2,1)}, u32[]{:S(2)}) copy-start(bf16[576,1024]{1,0:T(8,128)(2,1)} %copy-done.25) | copy-start | bytes 3538948
  114.6 1.1 copy-start.28
  119.6 1.8 collective-permute-start.1
  123.3 6.8 %copy-start.10 = (f32[128]{0:T(128)S(1)}, f32[128]{0:T(128)}, u32[]{:S(2)}) copy-start(f32[128]{0:T(128)} %param.24) | copy-start | bytes 1540
  123.3 6.8 %copy-start.11 = (f32[128]{0:T(128)S(1)}, f32[128]{0:T(128)}, u32[]{:S(2)}) copy-start(f32[128]{0:T(128)} %param.26) | copy-start | bytes 1540
  123.3 6.8 %copy-start.30 = (f32[128,1536]{1,0:T(8,128)S(1)}, f32[128,1536]{1,0:T(8,128)}, u32[]{:S(2)}) copy-start(f32[128,1536]{1,0:T(8,128)} %copy-done.29) | copy-start | bytes 2359300
  123.3 33.0 %all-to-all-start.3 = ((bf16[256,2,768]{2,1,0:T(2,128)(2,1)}), bf16[256,2,768]{2,1,0:T(2,128)(2,1)}, u32[]{:S(2)}, u32[]{:S(2)}) async-start(bf16[256,2,768]{2,1,0:T(2,128)(2,1)} %copy.21), calls=%async_computation.3 | async-start | bytes 1572864 | tf_op jit(solution)/shard_map/all_to_all | solution.py:369
  130.2 1.1 copy-start.36
  131.3 1.1 copy-start.38
  137.1 0.9 copy-start.33
  157.6 1.9 copy-start.23
  162.9 29.7 %copy-start.34 = (f32[128,1536]{1,0:T(8,128)S(1)}, f32[128,1536]{1,0:T(8,128)}, u32[]{:S(2)}) copy-start(f32[128,1536]{1,0:T(8,128)} %copy-done.33) | copy-start | bytes 2359300
  187.4 23.8 %all-to-all-start.5 = ((f32[256,1,384]{2,1,0:T(1,128)}), f32[256,1,384]{2,1,0:T(1,128)S(1)}, u32[]{:S(2)}, u32[]{:S(2)}) async-start(f32[256,1,384]{2,1,0:T(1,128)} %broadcast_in_dim.2), calls=%async_computation.5 | async-start | bytes 786432 | tf_op jit(solution)/shard_map/all_to_all | solution.py:369
  192.6 1.9 copy-start.24

commit v2 on v1

--- a/solution.py
+++ b/solution.py
@@ -117,28 +117,31 @@
     return pl.ds(pl.multiple_of(step * STEP, STEP), STEP)
 
 
-def build_mask(place, valid_s, valid_v, mask):
-    values = jnp.concatenate([valid_v[...].astype(F32), jnp.zeros((1, WIRE - TOTAL), F32)], axis=1)
+def build_mask(place, valid, mask):
+    values = jnp.concatenate([valid[...].astype(F32), jnp.zeros((1, WIRE - TOTAL), F32)], axis=1)
     values = jnp.broadcast_to(values, (8, WIRE))
-    shift = place[1] * COLS
-    values = pltpu.roll(values, jnp.where(shift == 0, 0, WIRE - shift), 1)
     lane = lax.broadcasted_iota(jnp.int32, (8, WIRE), 1)
-    values = jnp.where(lane < COLS, values, 0.0)
-    shifted = [values] + [pltpu.roll(values, i * COLS, 1) for i in range(1, HALF)]
+
+    def window(start):
+        return pltpu.roll(values, jnp.where(start == 0, 0, WIRE - start), 1)
+
+    cols = jnp.where(lane < COLS, window(place[1] * COLS), 0.0)
+    rows = window(place[0] * ROWS)
+    shifted = [cols] + [pltpu.roll(cols, i * COLS, 1) for i in range(1, HALF)]
     for half in range(2):
         total = jnp.zeros((8, WIRE), F32)
         for i in range(HALF):
-            row = valid_s[place[0] * ROWS + half * HALF + i].astype(F32)
-            total = total + row * shifted[i]
+            row = half * HALF + i
+            total = total + rows[:, row : row + 1] * shifted[i]
         mask[:, half * WIRE : (half + 1) * WIRE] = total[:1]
 
 
 def project_kernel(
-    place, valid_s, valid_v, pair, weight, bias, gain, shift, by_channel,
+    place, valid, pair, weight, bias, gain, shift, by_channel,
     wire, mask,
     padded, left_s, right_s,
 ):
-    build_mask(place, valid_s, valid_v, mask)
+    build_mask(place, valid, mask)
     fill(padded, pair)
     gain_c, shift_c = column(gain), column(shift)
     bias_c = jnp.concatenate(columns(bias)[:4], axis=0)
@@ -324,10 +327,10 @@
         normed = split(hat[:, lanes_of(step)] * gain_c + shift_c)
         total[...] += fine(normed, d_hidden, LAST)
 
-    grads[:WIDTH, :] = total[:, : 3 * WIDTH]
-    grads[WIDTH:, :WIDTH] = total[:, 3 * WIDTH :]
-    grads[WIDTH:, WIDTH : 2 * WIDTH] = grad_gate[...]
-    grads[WIDTH:, 2 * WIDTH :] = grad_out[...]
+    grads[:WIDTH, :] = total[:, : 3 * WIDTH].astype(BF16)
+    grads[WIDTH:, :WIDTH] = total[:, 3 * WIDTH :].astype(BF16)
+    grads[WIDTH:, WIDTH : 2 * WIDTH] = grad_gate[...].astype(BF16)
+    grads[WIDTH:, 2 * WIDTH :] = grad_out[...].astype(BF16)
 
 
 def pair_kernel(
@@ -350,7 +353,7 @@
     drain(grad_pair, padded)
 
 
-def call(kernel, outs, scratch, *args, smem=0, work=2e9):
+def call(kernel, outs, scratch, *args, smem=0, work=2e9, room=48):
     whole = lambda shape: pl.BlockSpec(shape, lambda i: (0,) * len(shape))
     scalars = [pl.BlockSpec(memory_space=pltpu.SMEM)] * smem
     return pl.pallas_call(
@@ -360,9 +363,53 @@
         in_specs=scalars + [whole(a.shape) for a in args[smem:]],
         out_specs=[whole(o[0]) for o in outs],
         scratch_shapes=[pltpu.VMEM(*s) for s in scratch],
-        compiler_params=pltpu.CompilerParams(vmem_limit_bytes=48 * 2**20),
+        compiler_params=pltpu.CompilerParams(vmem_limit_bytes=room * 2**20),
         cost_estimate=pl.CostEstimate(flops=int(work), bytes_accessed=4 * 2**20, transcendentals=0),
     )(*args)
+
+
+def spin(step, count, inner):
+    size = 32 if inner != 2 else 8
+    return [
+        (i, i - (i // inner % count) * inner + ((i // inner + step) % count) * inner)
+        for i in range(size)
+    ]
+
+
+def meet(value, axis, count, inner):
+    value = lax.optimization_barrier(value.astype(BF16))
+    others = [lax.ppermute(value, axis, spin(k, count, inner)) for k in range(1, count)]
+    own = value.astype(F32)
+    if count == 2:
+        return own + others[0].astype(F32)
+    one, two, three = (o.astype(F32) for o in others)
+    return (own + two) + (one + three)
+
+
+def sum_over_devices(grads, row, col, beside):
+    core, x = col % 2, row % 4
+    pick = lambda a, i: lax.dynamic_index_in_dim(a, i, 0, keepdims=False)
+    pairs = grads.reshape(2, WIDTH, 3 * WIDTH)
+    taken = lax.ppermute(pick(pairs, 1 - core), "col", SWAP)
+    total = pick(pairs, core).astype(F32) + taken.astype(F32)
+    total = total.astype(BF16).reshape(4, WIDTH // 4, 3 * WIDTH)
+    taken = [
+        lax.ppermute(pick(total, (x + k) % 4), "row", spin(k, 4, 1)).astype(F32) for k in (1, 2, 3)
+    ]
+    total = (pick(total, x).astype(F32) + taken[0]) + (taken[1] + taken[2])
+    total = meet(total, "row", 4, 8)
+    total = meet(total, "col", 4, 2)
+    total, beside = lax.optimization_barrier((meet(total, "row", 2, 4).astype(BF16), beside))
+    parts = jnp.zeros((4, WIDTH // 4, 3 * WIDTH), BF16)
+    parts = lax.dynamic_update_index_in_dim(parts, total, x, 0)
+    for k in (1, 2, 3):
+        taken = lax.ppermute(total, "row", spin(k, 4, 1))
+        parts = lax.dynamic_update_index_in_dim(parts, taken, (x + 4 - k) % 4, 0)
+    parts = parts.reshape(WIDTH, 3 * WIDTH)
+    other = lax.ppermute(parts, "col", SWAP)
+    first = core == 0
+    upper, lower = jnp.where(first, parts, other), jnp.where(first, other, parts)
+    return upper.astype(F32), lower.astype(F32), beside
 
 
 def exchange(chunks):
@@ -401,9 +448,9 @@
         project_kernel,
         [((DEVICES, LANES), BF16), ((1, LANES), F32)],
         [whole, halves(BF16), halves(BF16)],
-        place, residue_mask, residue_mask.reshape(1, TOTAL), pair, proj_weight, bias, gain, shift,
-        by_channel,
-        smem=2,
+        place, residue_mask.reshape(1, TOTAL), pair, proj_weight, bias, gain, shift, by_channel,
+        smem=1,
+        room=62,
     )
     got = exchange(wire.reshape(DEVICES, 2, WIRE)).reshape(DEVICES, LANES)
     hat, scale, factors, opened, d_result, d_hat = call(
@@ -449,11 +496,10 @@
     got = exchange(jnp.stack([left_wire, right_wire], axis=1)).reshape(DEVICES, LANES)
     (grads,) = call(
         weight_kernel,
-        [((DEVICES, 3 * WIDTH), F32)],
+        [((DEVICES, 3 * WIDTH), BF16)],
         [halves(F32), halves(F32), ((WIDTH, 4 * WIDTH), F32)],
         got, factors, hat, gain, shift, grad_gate, grad_out, by_half,
     )
-    pieces = exchange(grads)
     (grad_pair,) = call(
         pair_kernel,
         [((places, WIDTH), F32)],
@@ -461,10 +507,9 @@
         got, factors, hat, scale, d_normed, proj_weight, gain, by_half,
         work=8e9,
     )
-    summed = jnp.sum(pieces, axis=0, keepdims=True)
-    grads = exchange(jnp.broadcast_to(summed, pieces.shape))
-    grad_proj = jnp.concatenate([grads[:WIDTH], grads[WIDTH:, : 2 * WIDTH]], axis=1)
-    return update.reshape(shape), grad_pair.reshape(shape), grad_proj, grads[WIDTH:, 2 * WIDTH :]
+    upper, lower, grad_pair = sum_over_devices(grads, row, col, grad_pair)
+    grad_proj = jnp.concatenate([upper, lower[:, : 2 * WIDTH]], axis=1)
+    return update.reshape(shape), grad_pair.reshape(shape), grad_proj, lower[:, 2 * WIDTH :]
 
 
 def solution(mesh):

time: 214 us -> 203 us (0.949)
  blocking collectives: 90.1 us -> 66.6 us
  starting transfers between devices: 17.5 us -> 33.4 us
  local copies, waits for them, and re-layouts: 28 us -> 24 us
    all_to_all x3 -> x2, blocking collectives: 90.1 us -> 66.6 us  [exchange(): return lax.all_to_all(chunks, BOTH, 0, 0, tiled=True)]
    ppermute x0 -> x15, starting transfers between devices: none -> 21.1 us  [the longest x7 7.89 us: meet(): lax.ppermute(value, axis, spin(k, count, inner))]
    all_to_all x3 -> x2, waiting for transfers between devices: 40.1 us -> 27.1 us  [exchange(): return lax.all_to_all(chunks, BOTH, 0, 0, tiled=True)]
    ppermute x0 -> x15, waiting for transfers between devices: none -> 11.9 us  [the longest x7 4.79 us: meet(): lax.ppermute(value, axis, spin(k, count, inner))]
    all_to_all x3 -> x2, starting transfers between devices: 17.1 us -> 12 us  [exchange(): return lax.all_to_all(chunks, BOTH, 0, 0, tiled=True)]
    unnamed x84 -> x78, local copies, waits for them, and re-layouts: 21.7 us -> 17.1 us
  transfers between devices with their start and end apart: 5 -> 19, of which waited for: 5 -> 16; matrix products, arithmetic and copies ran while one was open for 0% -> 0% of each run, Pallas kernels for 7% -> 8%
where the time goes in v2:
time: 203 us; the launch traced here: 202 us
  blocking collectives  66.6 us (33%)
  waiting for transfers between devices  42.3 us (21%)
  starting transfers between devices  33.4 us (16%)
  Pallas kernels  33.2 us (16%)
  local copies, waits for them, and re-layouts  24 us (12%)
    all_to_all x2, blocking collectives, exchange(): return lax.all_to_all(chunks, BOTH, 0, 0, tiled=True)  66.6 us
    pallas_call x8, Pallas kernels, call(): pl.pallas_call(kernel, grid=(1,), out_shape=[jax.ShapeDtypeStruct(*o) for...  33.2 us
    all_to_all x2, waiting for transfers between devices, exchange(): return lax.all_to_all(chunks, BOTH, 0, 0, tiled=True)  27.1 us
    unnamed x78, local copies, waits for them, and re-layouts  17.1 us
    all_to_all x2, starting transfers between devices, exchange(): return lax.all_to_all(chunks, BOTH, 0, 0, tiled=True)  12 us
    ppermute x7, starting transfers between devices, meet(): lax.ppermute(value, axis, spin(k, count, inner))  7.89 us
    ppermute x1, starting transfers between devices, sum_over_devices(): other = lax.ppermute(parts, 'col', SWAP)  6.92 us
    ppermute x7, waiting for transfers between devices, meet(): lax.ppermute(value, axis, spin(k, count, inner))  4.79 us
  transfers between devices with their start and end apart: 19, of which 16 were waited for; matrix products, arithmetic and copies ran while one was open for 0% of the time, Pallas kernels for 8%

profile of v2, /device:TPU:1, one launch (start us, length us, event | category | flops | bytes accessed | tf_op | source)
XLA Modules:
  0.0 202.3 jit_solution(9312714195566629691)
XLA Ops:
  0.6 1.3 reshape.75.valid
  1.9 0.6 pad_add_fusion.place
  2.5 6.2 %shard_map.183 = (bf16[256,1536]{1,0:T(8,128)(2,1)}, f32[1,1536]{1,0:T(1,128)}) custom-call(s32[3]{0:T(128)} %pad_add_fusion.place, s32[1,576]{1,0:T(1,128)} %reshape.75.valid, f32[1296,128]{1,0:T(8,128)} %bitcast.60, f32[128,640]{1,0:T(8,128)} %weight.7, f32[5,128]{1,0:T(8,128)} %bitcast.63, f32[1,128]{1,0:T(1,128)} %bitcast.73, f32[1,128]{1,0:T(1,128)} %bitcast.69, ...), custom_call_target="tpu_custom_call" | custom-call | flops 2000000000 | bytes 4194304 | tf_op jit(solution)/shard_map/pallas_call | solution.py:359
  8.7 2.3 %reshape.80 = bf16[256,2,768]{2,1,0:T(2,128)(2,1)S(1)} reshape(bf16[256,1536]{1,0:T(8,128)(2,1)} %get-tuple-element.26) | data formatting | bytes 1572864 | tf_op jit(solution)/shard_map/reshape | solution.py:455
  11.0 42.4 %all_to_all.20 = bf16[256,2,768]{2,1,0:T(2,128)(2,1)S(1)} all-to-all(bf16[256,2,768]{2,1,0:T(2,128)(2,1)S(1)} %reshape.80), channel_id=1, replica_groups=mesh['row'=32,'col'=8] {'row','col'}, dimensions={0} | all-to-all | bytes 1572864 | tf_op jit(solution)/shard_map/all_to_all | solution.py:416
  53.4 0.1 collective-permute-start
  53.5 1.7 collective-permute-done.other_w
  55.3 3.2 %shard_map.184 = (bf16[256,768]{1,0:T(8,128)(2,1)S(1)}, bf16[288,1024]{1,0:T(8,128)(2,1)S(1)}, bf16[576,1024]{1,0:T(8,128)(2,1)S(1)}) custom-call(s32[3]{0:T(128)S(1)} %copy-done, bf16[256,1536]{1,0:T(8,128)(2,1)S(1)} %bitcast.52, bf16[256,768]{1,0:T(8,128)(2,1)S(1)} %collective-permute-done.other_w, bf16[256,256]{1,0:T(8,128)(2,1)S(1)} %copy-done.13, ...), custom_call_target="tpu_custom_call" | custom-call | flops 2000000000 | bytes 4194304 | tf_op jit(solution)/shard_map/pallas_call | solution.py:359
  58.5 1.0 copy-done.22
  59.6 0.8 copy-done.24
  60.4 0.8 reshape.82
  61.3 5.2 %all-to-all-start.1 = ((bf16[256,2,384]{2,1,0:T(2,128)(2,1)}), bf16[256,2,384]{2,1,0:T(2,128)(2,1)S(1)}, u32[]{:S(2)}, u32[]{:S(2)}) async-start(bf16[256,2,384]{2,1,0:T(2,128)(2,1)} %reshape.82), calls=%async_computation.1 | async-start | bytes 786432 | tf_op jit(solution)/shard_map/all_to_all | solution.py:416
  66.5 7.0 %shard_map.185 = (f32[128,1536]{1,0:T(8,128)S(1)}, f32[1,1536]{1,0:T(1,128)S(1)}, f32[512,1536]{1,0:T(8,128)}, f32[128,1536]{1,0:T(8,128)S(1)}, f32[128,1536]{1,0:T(8,128)S(1)}, /*index=5*/f32[128,1536]{1,0:T(8,128)S(1)}) custom-call(f32[1,1536]{1,0:T(1,128)S(1)} %copy-done.36, f32[1296,128]{1,0:T(8,128)S(1)} %bitcast.61, f32[1296,128]{1,0:T(8,128)S(1)} %bitcast.62, ...), custom_call_target="tpu_custom_call" | custom-call | flops 10000000000 | bytes 4194304 | tf_op jit(solution)/shard_map/pallas_call | solution.py:359
  73.6 0.9 copy-done.20
  74.5 0.9 copy-done.28
  75.4 0.9 copy-done.32
  76.3 0.9 copy-done.34
  77.2 7.9 %all-to-all-done.1 = bf16[256,2,384]{2,1,0:T(2,128)(2,1)S(1)} async-done(((bf16[256,2,384]{2,1,0:T(2,128)(2,1)}), bf16[256,2,384]{2,1,0:T(2,128)(2,1)S(1)}, u32[]{:S(2)}, u32[]{:S(2)}) %all-to-all-start.1) | async-done | bytes 393248 | tf_op jit(solution)/shard_map/all_to_all | solution.py:416
  85.1 0.9 copy-done.17
  86.0 1.1 copy-done.29
  87.2 1.3 shard_map.186
  88.5 0.9 copy-done.26
  89.5 24.3 %all_to_all.21 = bf16[256,2,384]{2,1,0:T(2,128)(2,1)S(1)} all-to-all(bf16[256,2,384]{2,1,0:T(2,128)(2,1)S(1)} %reshape.89), channel_id=1, replica_groups=mesh['row'=32,'col'=8] {'row','col'}, dimensions={0} | all-to-all | bytes 786432 | tf_op jit(solution)/shard_map/all_to_all | solution.py:416
  113.9 3.9 %shard_map.188 = (bf16[256,768]{1,0:T(8,128)(2,1)S(1)}, bf16[256,768]{1,0:T(8,128)(2,1)S(1)}, bf16[256,768]{1,0:T(8,128)(2,1)S(1)}) custom-call(s32[3]{0:T(128)S(1)} %copy-done, bf16[256,768]{1,0:T(8,128)(2,1)S(1)} %bitcast.55, bf16[288,1024]{1,0:T(8,128)(2,1)S(1)} %copy-done.25, bf16[576,1024]{1,0:T(8,128)(2,1)S(1)} %copy-done.23, ...), custom_call_target="tpu_custom_call" | custom-call | flops 2000000000 | bytes 4194304 | tf_op jit(solution)/shard_map/pallas_call | solution.py:359
  117.8 0.2 collective-permute-start.1
  118.0 1.6 collective-permute-done.1
  119.6 0.1 fusion
  119.8 1.7 copy.21
  121.5 6.8 %all-to-all-start.3 = ((bf16[256,2,768]{2,1,0:T(2,128)(2,1)}), bf16[256,2,768]{2,1,0:T(2,128)(2,1)}, u32[]{:S(2)}, u32[]{:S(2)}) async-start(bf16[256,2,768]{2,1,0:T(2,128)(2,1)} %copy.21), calls=%async_computation.3 | async-start | bytes 1572864 | tf_op jit(solution)/shard_map/all_to_all | solution.py:416
  128.4 1.1 copy-done.33
  129.5 1.1 copy-done.35
  130.7 4.7 %shard_map.187 = (f32[1296,128]{1,0:T(8,128)}, f32[128,128]{1,0:T(8,128)S(1)}, f32[128,128]{1,0:T(8,128)S(1)}, f32[128,1536]{1,0:T(8,128)S(1)}) custom-call(f32[128,1536]{1,0:T(8,128)S(1)} %copy-done.27, f32[128,1536]{1,0:T(8,128)S(1)} %copy-done.33, f32[128,1536]{1,0:T(8,128)S(1)} %copy-done.35, f32[128,1536]{1,0:T(8,128)S(1)} %copy-done.21, ...), custom_call_target="tpu_custom_call" | custom-call | flops 8000000000 | bytes 4194304 | tf_op jit(solution)/shard_map/pallas_call | solution.py:359
  135.3 19.2 %all-to-all-done.3 = bf16[256,2,768]{2,1,0:T(2,128)(2,1)} async-done(((bf16[256,2,768]{2,1,0:T(2,128)(2,1)}), bf16[256,2,768]{2,1,0:T(2,128)(2,1)}, u32[]{:S(2)}, u32[]{:S(2)}) %all-to-all-start.3) | async-done | bytes 786464 | tf_op jit(solution)/shard_map/all_to_all | solution.py:416
  154.5 1.2 copy.25
  155.7 1.9 copy-done.18
  157.6 3.0 %shard_map.189 = bf16[256,384]{1,0:T(8,128)(2,1)S(1)} custom-call(bf16[256,1536]{1,0:T(8,128)(2,1)S(1)} %bitcast.53, f32[512,1536]{1,0:T(8,128)S(1)} %copy-done.18, f32[128,1536]{1,0:T(8,128)S(1)} %copy-done.21, f32[1,128]{1,0:T(1,128)S(1)} %bitcast.76, f32[1,128]{1,0:T(1,128)S(1)} %bitcast.72, f32[128,128]{1,0:T(8,128)S(1)} %get-tuple-element.42.grad_gate, ...), custom_call_target="tpu_custom_call" | custom-call | flops 2000000000 | bytes 4194304 | tf_op jit(solution)/shard_map/pallas_call | solution.py:359
  160.9 1.2 collective-permute-done.2
  162.2 1.1 collective-permute-start.4
  163.3 1.5 collective-permute-start.5
  164.9 1.2 collective-permute-done.3
  166.1 0.4 collective-permute-done.4
  166.5 0.7 collective-permute-done.5
  167.2 0.7 collective-permute-start.6
  167.9 0.8 collective-permute-start.7
  168.7 1.9 collective-permute-start.8
  170.6 0.9 collective-permute-done.6
  171.5 0.3 collective-permute-done.7
  171.8 1.2 collective-permute-start.10
  173.0 2.4 %collective-permute-start.11 = (bf16[32,384]{1,0:T(8,128)(2,1)S(1)}, bf16[32,384]{1,0:T(8,128)(2,1)S(1)}, u32[]{:S(2)}, u32[]{:S(2)}) collective-permute-start(bf16[32,384]{1,0:T(8,128)(2,1)S(1)} %add_convert_fusion.3), channel_id=1, source_target_pairs={{0,6},{1,7},{2,0},{3,1},{4,2},{5,3},{6,4},{7,5},{8,14},{9,15},{10,... | collective-permute-start | bytes 73736 | tf_op jit(solution)/shard_map/ppermute | solution.py:381
  175.4 1.2 collective-permute-done.10
  176.6 2.4 %collective-permute-done.9 = bf16[32,384]{1,0:T(8,128)(2,1)S(1)} collective-permute-done((bf16[32,384]{1,0:T(8,128)(2,1)S(1)}, bf16[32,384]{1,0:T(8,128)(2,1)S(1)}, u32[]{:S(2)}, u32[]{:S(2)}) %collective-permute-start.9) | collective-permute-done | bytes 24608 | tf_op jit(solution)/shard_map/ppermute | solution.py:381
  179.0 1.0 collective-permute-start.12
  180.0 1.9 copy-done.19
  181.9 1.1 copy-done.31
  183.0 3.9 %shard_map.190 = f32[1296,128]{1,0:T(8,128)} custom-call(bf16[256,1536]{1,0:T(8,128)(2,1)S(1)} %bitcast.54, f32[512,1536]{1,0:T(8,128)S(1)} %copy-done.19, f32[128,1536]{1,0:T(8,128)S(1)} %copy-done.21, f32[1,1536]{1,0:T(1,128)S(1)} %get-tuple-element.44.scale, f32[128,1536]{1,0:T(8,128)S(1)} %copy-done.31, f32[128,640]{1,0:T(8,128)S(1)} %copy-done.3, ...), custom_call_target="tpu_custom_call" | custom-call | flops 8000000000 | bytes 4194304 | tf_op jit(solution)/shard_map/pallas_call | solution.py:359
  186.9 0.9 collective-permute-start.13
  187.8 2.5 %collective-permute-start.14 = (bf16[32,384]{1,0:T(8,128)(2,1)S(1)}, bf16[32,384]{1,0:T(8,128)(2,1)S(1)}, u32[]{:S(2)}, u32[]{:S(2)}) collective-permute-start(bf16[32,384]{1,0:T(8,128)(2,1)S(1)} %add_convert_fusion.1), channel_id=1, source_target_pairs={{0,16},{8,24},{16,0},{24,8},{32,48},{40,56},{48,32},{56,40},{64,80... | collective-permute-start | bytes 73736 | tf_op jit(solution)/shard_map/ppermute | solution.py:406
  190.4 0.7 collective-permute-done.13
  191.1 1.0 collective-permute-done.14
  192.0 1.0 collective-permute-done.15
  193.0 6.9 %collective-permute-start.16 = (bf16[128,384]{1,0:T(8,128)(2,1)S(1)}, bf16[128,384]{1,0:T(8,128)(2,1)S(1)}, u32[]{:S(2)}, u32[]{:S(2)}) collective-permute-start(bf16[128,384]{1,0:T(8,128)(2,1)S(1)} %bitcast.83), channel_id=1, source_target_pairs={{0,1},{1,0},{2,3},{3,2},{4,5},{5,4},{6,7},{7,6},{8,9},{9,8},{10,11... | collective-permute-start | bytes 294920 | tf_op jit(solution)/shard_map/ppermute | solution.py:409
  199.9 0.9 collective-permute-done.16
  200.9 0.6 slice.14
  201.6 0.7 pad_maximum_fusion.1
  (87 shorter events, 0.9 us)
Async XLA Ops:
  53.3 2.0 copy-start
  53.3 2.0 copy-start.11
  53.3 2.0 copy-start.13
  53.3 2.0 copy-start.15
  53.4 1.8 collective-permute-start
  55.3 11.2 %copy-start.3 = (f32[128,640]{1,0:T(8,128)S(1)}, f32[128,640]{1,0:T(8,128)}, u32[]{:S(2)}) copy-start(f32[128,640]{1,0:T(8,128)} %weight.7) | copy-start | bytes 983044
  58.5 1.0 copy-start.22
  59.6 0.8 copy-start.24
  60.4 6.1 %copy-start.1 = (f32[18,72,128]{2,1,0:T(8,128)S(1)}, f32[18,72,128]{2,1,0:T(8,128)}, u32[]{:S(2)}) copy-start(f32[18,72,128]{2,1,0:T(8,128)} %param.16) | copy-start | bytes 1990660
  60.4 6.1 %copy-start.2 = (f32[18,72,128]{2,1,0:T(8,128)S(1)}, f32[18,72,128]{2,1,0:T(8,128)}, u32[]{:S(2)}) copy-start(f32[18,72,128]{2,1,0:T(8,128)} %param.17) | copy-start | bytes 1990660
  60.4 6.1 %copy-start.4 = (f32[128,128]{1,0:T(8,128)S(1)}, f32[128,128]{1,0:T(8,128)}, u32[]{:S(2)}) copy-start(f32[128,128]{1,0:T(8,128)} %out_weight.3) | copy-start | bytes 196612
  60.4 6.1 %copy-start.5 = (f32[640]{0:T(1024)S(1)}, f32[640]{0:T(1024)}, u32[]{:S(2)}) copy-start(f32[640]{0:T(1024)} %param.22) | copy-start | bytes 7684
  60.4 6.1 %copy-start.6 = (f32[128]{0:T(128)S(1)}, f32[128]{0:T(128)}, u32[]{:S(2)}) copy-start(f32[128]{0:T(128)} %param.23) | copy-start | bytes 1540
  60.4 6.1 %copy-start.9 = (f32[128]{0:T(128)S(1)}, f32[128]{0:T(128)}, u32[]{:S(2)}) copy-start(f32[128]{0:T(128)} %param.20) | copy-start | bytes 1540
  60.4 6.1 %copy-start.10 = (f32[128]{0:T(128)S(1)}, f32[128]{0:T(128)}, u32[]{:S(2)}) copy-start(f32[128]{0:T(128)} %param.19) | copy-start | bytes 1540
  60.4 6.1 %copy-start.36 = (f32[1,1536]{1,0:T(1,128)S(1)}, f32[1,1536]{1,0:T(1,128)}, u32[]{:S(2)}) copy-start(f32[1,1536]{1,0:T(1,128)} %get-tuple-element.28.mask) | copy-start | bytes 18436
  61.3 23.8 %all-to-all-start.1 = ((bf16[256,2,384]{2,1,0:T(2,128)(2,1)}), bf16[256,2,384]{2,1,0:T(2,128)(2,1)S(1)}, u32[]{:S(2)}, u32[]{:S(2)}) async-start(bf16[256,2,384]{2,1,0:T(2,128)(2,1)} %reshape.82), calls=%async_computation.1 | async-start | bytes 786432 | tf_op jit(solution)/shard_map/all_to_all | solution.py:416
  66.5 18.6 %copy-start.12 = (bf16[256,256]{1,0:T(8,128)(2,1)S(1)}, bf16[256,256]{1,0:T(8,128)(2,1)}, u32[]{:S(2)}) copy-start(bf16[256,256]{1,0:T(8,128)(2,1)} %constant.108.clone.by_half) | copy-start | bytes 393220
  73.6 0.9 copy-start.20
  74.5 0.9 copy-start.28
  75.4 0.9 copy-start.32
  76.3 0.9 copy-start.34
  85.1 0.9 copy-start.17
  86.0 1.1 copy-start.29
  88.5 0.9 copy-start.26
  89.4 24.4 %copy-start.14 = (bf16[256,256]{1,0:T(8,128)(2,1)S(1)}, bf16[256,256]{1,0:T(8,128)(2,1)}, u32[]{:S(2)}) copy-start(bf16[256,256]{1,0:T(8,128)(2,1)} %constant.106.clone.by_col) | copy-start | bytes 393220
  89.4 24.4 %copy-start.16 = (bf16[256,256]{1,0:T(8,128)(2,1)S(1)}, bf16[256,256]{1,0:T(8,128)(2,1)}, u32[]{:S(2)}) copy-start(bf16[256,256]{1,0:T(8,128)(2,1)} %constant.107.clone.by_row) | copy-start | bytes 393220
  89.4 24.4 %copy-start.25 = (bf16[288,1024]{1,0:T(8,128)(2,1)S(1)}, bf16[288,1024]{1,0:T(8,128)(2,1)}, u32[]{:S(2)}) copy-start(bf16[288,1024]{1,0:T(8,128)(2,1)} %copy-done.24) | copy-start | bytes 1769476
  89.5 24.4 %copy-start.23 = (bf16[576,1024]{1,0:T(8,128)(2,1)S(1)}, bf16[576,1024]{1,0:T(8,128)(2,1)}, u32[]{:S(2)}) copy-start(bf16[576,1024]{1,0:T(8,128)(2,1)} %copy-done.22) | copy-start | bytes 3538948
  117.8 1.8 collective-permute-start.1
  121.5 6.9 %copy-start.7 = (f32[128]{0:T(128)S(1)}, f32[128]{0:T(128)}, u32[]{:S(2)}) copy-start(f32[128]{0:T(128)} %param.24) | copy-start | bytes 1540
  121.5 6.9 %copy-start.8 = (f32[128]{0:T(128)S(1)}, f32[128]{0:T(128)}, u32[]{:S(2)}) copy-start(f32[128]{0:T(128)} %param.26) | copy-start | bytes 1540
  121.5 6.9 %copy-start.21 = (f32[128,1536]{1,0:T(8,128)S(1)}, f32[128,1536]{1,0:T(8,128)}, u32[]{:S(2)}) copy-start(f32[128,1536]{1,0:T(8,128)} %copy-done.20) | copy-start | bytes 2359300
  121.5 6.9 %copy-start.27 = (f32[128,1536]{1,0:T(8,128)S(1)}, f32[128,1536]{1,0:T(8,128)}, u32[]{:S(2)}) copy-start(f32[128,1536]{1,0:T(8,128)} %copy-done.26) | copy-start | bytes 2359300
  121.5 33.0 %all-to-all-start.3 = ((bf16[256,2,768]{2,1,0:T(2,128)(2,1)}), bf16[256,2,768]{2,1,0:T(2,128)(2,1)}, u32[]{:S(2)}, u32[]{:S(2)}) async-start(bf16[256,2,768]{2,1,0:T(2,128)(2,1)} %copy.21), calls=%async_computation.3 | async-start | bytes 1572864 | tf_op jit(solution)/shard_map/all_to_all | solution.py:416
  128.4 1.1 copy-start.33
  129.5 1.1 copy-start.35
  135.3 20.4 %copy-start.30 = (f32[128,1536]{1,0:T(8,128)}, f32[128,1536]{1,0:T(8,128)S(1)}, u32[]{:S(2)}) copy-start(f32[128,1536]{1,0:T(8,128)S(1)} %get-tuple-element.45.d_normed) | copy-start | bytes 2359300
  155.7 1.9 copy-start.18
  160.7 1.4 collective-permute-start.2
  162.1 4.0 %collective-permute-start.3 = (bf16[32,384]{1,0:T(8,128)(2,1)S(1)}, bf16[32,384]{1,0:T(8,128)(2,1)S(1)}, u32[]{:S(2)}, u32[]{:S(2)}) collective-permute-start(bf16[32,384]{1,0:T(8,128)(2,1)S(1)} %get-tuple-element.50), channel_id=1, source_target_pairs={{0,8},{8,16},{16,24},{24,0},{32,40},{40,48},{48,56},{56,32},{64,72... | collective-permute-start | bytes 73736 | tf_op jit(solution)/shard_map/ppermute | solution.py:397
  162.2 4.3 %collective-permute-start.4 = (bf16[32,384]{1,0:T(8,128)(2,1)S(1)}, bf16[32,384]{1,0:T(8,128)(2,1)S(1)}, u32[]{:S(2)}, u32[]{:S(2)}) collective-permute-start(bf16[32,384]{1,0:T(8,128)(2,1)S(1)} %get-tuple-element.52), channel_id=1, source_target_pairs={{0,16},{8,24},{16,0},{24,8},{32,48},{40,56},{48,32},{56,40},{64,80... | collective-permute-start | bytes 73736 | tf_op jit(solution)/shard_map/ppermute | solution.py:397
  163.3 3.9 %collective-permute-start.5 = (bf16[32,384]{1,0:T(8,128)(2,1)S(1)}, bf16[32,384]{1,0:T(8,128)(2,1)S(1)}, u32[]{:S(2)}, u32[]{:S(2)}) collective-permute-start(bf16[32,384]{1,0:T(8,128)(2,1)S(1)} %get-tuple-element.51), channel_id=1, source_target_pairs={{0,24},{8,0},{16,8},{24,16},{32,56},{40,32},{48,40},{56,48},{64,88... | collective-permute-start | bytes 73736 | tf_op jit(solution)/shard_map/ppermute | solution.py:397
  167.2 4.3 %collective-permute-start.6 = (bf16[32,384]{1,0:T(8,128)(2,1)S(1)}, bf16[32,384]{1,0:T(8,128)(2,1)S(1)}, u32[]{:S(2)}, u32[]{:S(2)}) collective-permute-start(bf16[32,384]{1,0:T(8,128)(2,1)S(1)} %fusion.3), channel_id=1, source_target_pairs={{0,128},{8,136},{16,144},{24,152},{32,160},{40,168},{48,176},{56,1... | collective-permute-start | bytes 73736 | tf_op jit(solution)/shard_map/ppermute | solution.py:381
  167.9 3.9 %collective-permute-start.7 = (bf16[32,384]{1,0:T(8,128)(2,1)S(1)}, bf16[32,384]{1,0:T(8,128)(2,1)S(1)}, u32[]{:S(2)}, u32[]{:S(2)}) collective-permute-start(bf16[32,384]{1,0:T(8,128)(2,1)S(1)} %fusion.3), channel_id=1, source_target_pairs={{0,64},{8,72},{16,80},{24,88},{32,96},{40,104},{48,112},{56,120},{... | collective-permute-start | bytes 73736 | tf_op jit(solution)/shard_map/ppermute | solution.py:381
  168.7 3.1 %collective-permute-start.8 = (bf16[32,384]{1,0:T(8,128)(2,1)S(1)}, bf16[32,384]{1,0:T(8,128)(2,1)S(1)}, u32[]{:S(2)}, u32[]{:S(2)}) collective-permute-start(bf16[32,384]{1,0:T(8,128)(2,1)S(1)} %fusion.3), channel_id=1, source_target_pairs={{0,192},{8,200},{16,208},{24,216},{32,224},{40,232},{48,240},{56,2... | collective-permute-start | bytes 73736 | tf_op jit(solution)/shard_map/ppermute | solution.py:381
  171.8 4.8 %collective-permute-start.10 = (bf16[32,384]{1,0:T(8,128)(2,1)S(1)}, bf16[32,384]{1,0:T(8,128)(2,1)S(1)}, u32[]{:S(2)}, u32[]{:S(2)}) collective-permute-start(bf16[32,384]{1,0:T(8,128)(2,1)S(1)} %add_convert_fusion.3), channel_id=1, source_target_pairs={{0,2},{1,3},{2,4},{3,5},{4,6},{5,7},{6,0},{7,1},{8,10},{9,11},{10,... | collective-permute-start | bytes 73736 | tf_op jit(solution)/shard_map/ppermute | solution.py:381
  173.0 3.6 %collective-permute-start.11 = (bf16[32,384]{1,0:T(8,128)(2,1)S(1)}, bf16[32,384]{1,0:T(8,128)(2,1)S(1)}, u32[]{:S(2)}, u32[]{:S(2)}) collective-permute-start(bf16[32,384]{1,0:T(8,128)(2,1)S(1)} %add_convert_fusion.3), channel_id=1, source_target_pairs={{0,6},{1,7},{2,0},{3,1},{4,2},{5,3},{6,4},{7,5},{8,14},{9,15},{10,... | collective-permute-start | bytes 73736 | tf_op jit(solution)/shard_map/ppermute | solution.py:381
  175.4 3.6 %collective-permute-start.9 = (bf16[32,384]{1,0:T(8,128)(2,1)S(1)}, bf16[32,384]{1,0:T(8,128)(2,1)S(1)}, u32[]{:S(2)}, u32[]{:S(2)}) collective-permute-start(bf16[32,384]{1,0:T(8,128)(2,1)S(1)} %add_convert_fusion.3), channel_id=1, source_target_pairs={{0,4},{1,5},{2,6},{3,7},{4,0},{5,1},{6,2},{7,3},{8,12},{9,13},{10,... | collective-permute-start | bytes 73736 | tf_op jit(solution)/shard_map/ppermute | solution.py:381
  179.0 7.9 %collective-permute-start.12 = (bf16[32,384]{1,0:T(8,128)(2,1)S(1)}, bf16[32,384]{1,0:T(8,128)(2,1)S(1)}, u32[]{:S(2)}, u32[]{:S(2)}) collective-permute-start(bf16[32,384]{1,0:T(8,128)(2,1)S(1)} %add_convert_fusion.2), channel_id=1, source_target_pairs={{0,32},{8,40},{16,48},{24,56},{32,0},{40,8},{48,16},{56,24},{64,96... | collective-permute-start | bytes 73736 | tf_op jit(solution)/shard_map/ppermute | solution.py:381
  180.0 1.9 copy-start.19
  181.9 1.1 copy-start.31
  186.9 4.1 %collective-permute-start.13 = (bf16[32,384]{1,0:T(8,128)(2,1)S(1)}, bf16[32,384]{1,0:T(8,128)(2,1)S(1)}, u32[]{:S(2)}, u32[]{:S(2)}) collective-permute-start(bf16[32,384]{1,0:T(8,128)(2,1)S(1)} %add_convert_fusion.1), channel_id=1, source_target_pairs={{0,8},{8,16},{16,24},{24,0},{32,40},{40,48},{48,56},{56,32},{64,72... | collective-permute-start | bytes 73736 | tf_op jit(solution)/shard_map/ppermute | solution.py:406
  187.8 4.2 %collective-permute-start.14 = (bf16[32,384]{1,0:T(8,128)(2,1)S(1)}, bf16[32,384]{1,0:T(8,128)(2,1)S(1)}, u32[]{:S(2)}, u32[]{:S(2)}) collective-permute-start(bf16[32,384]{1,0:T(8,128)(2,1)S(1)} %add_convert_fusion.1), channel_id=1, source_target_pairs={{0,16},{8,24},{16,0},{24,8},{32,48},{40,56},{48,32},{56,40},{64,80... | collective-permute-start | bytes 73736 | tf_op jit(solution)/shard_map/ppermute | solution.py:406
  190.3 2.7 %collective-permute-start.15 = (bf16[32,384]{1,0:T(8,128)(2,1)S(1)}, bf16[32,384]{1,0:T(8,128)(2,1)S(1)}, u32[]{:S(2)}, u32[]{:S(2)}) collective-permute-start(bf16[32,384]{1,0:T(8,128)(2,1)S(1)} %add_convert_fusion.1), channel_id=1, source_target_pairs={{0,24},{8,0},{16,8},{24,16},{32,56},{40,32},{48,40},{56,48},{64,88... | collective-permute-start | bytes 73736 | tf_op jit(solution)/shard_map/ppermute | solution.py:406
  193.0 7.9 %collective-permute-start.16 = (bf16[128,384]{1,0:T(8,128)(2,1)S(1)}, bf16[128,384]{1,0:T(8,128)(2,1)S(1)}, u32[]{:S(2)}, u32[]{:S(2)}) collective-permute-start(bf16[128,384]{1,0:T(8,128)(2,1)S(1)} %bitcast.83), channel_id=1, source_target_pairs={{0,1},{1,0},{2,3},{3,2},{4,5},{5,4},{6,7},{7,6},{8,9},{9,8},{10,11... | collective-permute-start | bytes 294920 | tf_op jit(solution)/shard_map/ppermute | solution.py:409

commit v3 on v2

v3 whole, which is shorter than its diff:
```python
import jax
import jax.numpy as jnp
import numpy as np
from jax import lax
from jax.experimental import pallas as pl
from jax.experimental.pallas import tpu as pltpu
from jax.sharding import PartitionSpec as P

BOTH = ("row", "col")
SWAP = [(0, 1), (1, 0), (2, 3), (3, 2), (4, 5), (5, 4), (6, 7), (7, 6)]
ROWS, COLS, WIDTH = 18, 72, 128
ROW_N, COL_N = 32, 8
DEVICES = ROW_N * COL_N
HALF = ROWS // 2
PIECE = HALF * COLS
WIRE = 768
LANES = 2 * WIRE
TOTAL = ROW_N * ROWS
GROUP = ROW_N // COL_N
STEP = 256
STEPS = LANES // STEP
F32, BF16 = jnp.float32, jnp.bfloat16


def one_hot(targets, length):
    table = np.zeros((len(targets), length), np.float32)
    table[np.arange(len(targets)), targets] = 1
    return jnp.asarray(table, BF16)


def spread_table():
    place, row = np.divmod(np.arange(TOTAL), ROW_N)
    col, part = np.divmod(row, GROUP)
    return one_hot(col * 128 + part * ROWS + place, COL_N * 128)


HAT, OPEN, GIVEN, D_HAT, SAVED = 512, 640, 768, 896, 1024
LEFT_ROWS, KEPT_ROWS, KEPT = 288, 864, 3072
BY_COL, BY_ROW, BY_HALF, BY_CHANNEL = 5, 3, 7, 1


def order(bits):
    n = lax.broadcasted_iota(jnp.int32, (DEVICES, DEVICES), 0)
    target = ((n & ((1 << bits) - 1)) << (8 - bits)) + (n >> bits)
    other = lax.broadcasted_iota(jnp.int32, (DEVICES, DEVICES), 1)
    return jnp.where(other == target, 1.0, 0.0).astype(BF16)


PLAIN = ((1,), (0,))
LAST = ((1,), (1,))


def dot(a, b, contract=PLAIN):
    return lax.dot_general(a, b, (contract, ((), ())), preferred_element_type=F32)


def split(x):
    high = x.astype(BF16)
    return high, (x - high.astype(F32)).astype(BF16)


def fine(a, b, contract=PLAIN):
    return dot(a[0], b[0], contract) + (dot(a[0], b[1], contract) + dot(a[1], b[0], contract))


def move(bits, values):
    return dot(order(bits), values)


def sigmoid(x):
    return 0.5 * jnp.tanh(0.5 * x) + 0.5


def normalise(values):
    centred = values - jnp.mean(values, axis=0, keepdims=True)
    spread = jnp.mean(centred * centred, axis=0, keepdims=True)
    scale = lax.rsqrt(spread + 1e-05)
    return centred * scale, scale


def normalise_back(d_hat, hat, scale):
    return scale * (
        d_hat
        - jnp.mean(d_hat, axis=0, keepdims=True)
        - hat * jnp.mean(d_hat * hat, axis=0, keepdims=True)
    )


def column(ref):
    return jnp.broadcast_to(ref[...], (8, WIDTH)).T[:, :1]


def columns(ref):
    table = jnp.concatenate([ref[...], jnp.zeros((3, WIDTH), F32)], axis=0).T
    return [table[:, i : i + 1] for i in range(5)]


def fill(padded, block):
    for half in range(2):
        padded[pl.ds(half * WIRE, PIECE), :] = block[pl.ds(half * PIECE, PIECE), :]
        padded[pl.ds(half * WIRE + PIECE, WIRE - PIECE), :] = jnp.zeros(
            (WIRE - PIECE, WIDTH), F32
        )


def drain(block, padded):
    for half in range(2):
        block[pl.ds(half * PIECE, PIECE), :] = padded[pl.ds(half * WIRE, PIECE), :]


def place_of(step):
    per = WIRE // STEP
    half = step // per
    return (
        pl.ds(pl.multiple_of(half * WIDTH, WIDTH), WIDTH),
        pl.ds(pl.multiple_of((step - half * per) * STEP, STEP), STEP),
    )


def lanes_of(step):
    return pl.ds(pl.multiple_of(step * STEP, STEP), STEP)


def build_mask(row, col, valid, mask):
    lane = lax.broadcasted_iota(jnp.int32, (8, 128), 1)
    cols = jnp.zeros((8, 128), F32)
    for k in range(COLS):
        cols = jnp.where(lane == k, valid[col * COLS + k].astype(F32), cols)
    cols = jnp.concatenate([cols, jnp.zeros((8, WIRE - 128), F32)], axis=1)
    shifted = [cols] + [pltpu.roll(cols, i * COLS, 1) for i in range(1, HALF)]
    for half in range(2):
        total = jnp.zeros((8, WIRE), F32)
        for i in range(HALF):
            total = total + valid[row * ROWS + half * HALF + i].astype(F32) * shifted[i]
        mask[:, half * WIRE : (half + 1) * WIRE] = total[:1]


def project_kernel(
    valid, pair, weight, bias, gain, shift,
    wire, mask,
    padded, left_s, right_s,
):
    build_mask(lax.axis_index("row"), lax.axis_index("col"), valid, mask)
    fill(padded, pair)
    gain_c, shift_c = column(gain), column(shift)
    bias_c = jnp.concatenate(columns(bias)[:4], axis=0)
    weight_t = split(weight[:, : 4 * WIDTH].T)

    @pl.loop(0, STEPS)
    def _(step):
        lanes = lanes_of(step)
        hat, _ = normalise(padded[lanes, :].T)
        hidden = fine(weight_t, split(hat * gain_c + shift_c)) + bias_c
        valid = mask[:, lanes]
        rows, cols = place_of(step)
        left = valid * sigmoid(hidden[WIDTH : 2 * WIDTH]) * hidden[:WIDTH]
        left_s[rows, cols] = left.astype(BF16)
        right = valid * sigmoid(hidden[3 * WIDTH : 4 * WIDTH]) * hidden[2 * WIDTH : 3 * WIDTH]
        right_s[rows, cols] = right.astype(BF16)

    wire[:, :WIRE] = move(BY_CHANNEL, left_s[...]).astype(BF16)
    wire[:, WIRE:] = move(BY_CHANNEL, right_s[...]).astype(BF16)


def prepare_kernel(
    mask, pair, cotangent, weight, bias, gain, shift, out_gain, out_weight,
    scale_o, saved,
    padded, padded_c, held, sems,
):
    fill(padded, pair)
    fill(padded_c, cotangent)
    gain_c, shift_c, out_gain_c = column(gain), column(shift), column(out_gain)
    bias_c = jnp.concatenate(columns(bias), axis=0)
    weight_t = split(weight[...].T)
    out_w = split(out_weight[...])

    def leave(step):
        lanes = lanes_of(step)
        return pltpu.make_async_copy(held.at[:, lanes], saved.at[:, lanes], sems.at[step])

    @pl.loop(0, STEPS)
    def _(step):
        lanes = lanes_of(step)
        hat, scale = normalise(padded[lanes, :].T)
        held[HAT:OPEN, lanes] = hat
        scale_o[:, lanes] = scale
        hidden = fine(weight_t, split(hat * gain_c + shift_c)) + bias_c
        valid = mask[:, lanes]
        for i in range(2):
            opened = sigmoid(hidden[(2 * i + 1) * WIDTH : (2 * i + 2) * WIDTH])
            factor = valid * opened
            held[2 * i * WIDTH : (2 * i + 1) * WIDTH, lanes] = factor
            held[(2 * i + 1) * WIDTH : (2 * i + 2) * WIDTH, lanes] = (
                factor * (1.0 - opened) * hidden[2 * i * WIDTH : (2 * i + 1) * WIDTH]
            )
        opened = sigmoid(hidden[4 * WIDTH :])
        held[OPEN:GIVEN, lanes] = opened
        d_result = padded_c[lanes, :].T * opened
        held[GIVEN:D_HAT, lanes] = d_result
        held[D_HAT:SAVED, lanes] = fine(out_w, split(d_result)) * out_gain_c
        leave(step).start()

    @pl.loop(0, STEPS)
    def _(step):
        leave(step).wait()


def unpack(values, out, base):
    keep = lax.broadcasted_iota(jnp.int32, (DEVICES, 128), 1) < COLS
    for i in range(HALF):
        tile, offset = divmod(i * COLS, 128)
        part = values[:, tile * 128 : tile * 128 + 256]
        if offset:
            part = pltpu.roll(part, 256 - offset, 1)
        part = jnp.where(keep, part[:, :128], 0.0).astype(BF16)
        for q in range(COL_N):
            out[pl.ds(base + i * ROW_N, ROW_N), q * 128 : (q + 1) * 128] = part[
                q * ROW_N : (q + 1) * ROW_N
            ]


def pack(values, out):
    out[...] = jnp.zeros_like(out)
    for i in range(HALF):
        tile, offset = divmod(i * COLS, 128)
        part = jnp.concatenate(
            [
                values[i * ROW_N : (i + 1) * ROW_N, q * 128 : (q + 1) * 128]
                for q in range(COL_N)
            ],
            axis=0,
        )
        part = jnp.concatenate([part, jnp.zeros_like(part)], axis=1)
        if offset:
            part = pltpu.roll(part, offset, 1)
        out[:, tile * 128 : tile * 128 + 256] += part


def mix_kernel(both_w, other_w, spread, wire, kept, left_m, right_m, packed, sems):
    own = lax.axis_index("col") % 2 * (TOTAL // 2)
    away = (TOTAL // 2) - own
    keep_left = pltpu.make_async_copy(left_m, kept.at[:LEFT_ROWS, :], sems.at[0])
    keep_right = pltpu.make_async_copy(right_m, kept.at[LEFT_ROWS:KEPT_ROWS, :], sems.at[1])
    by_col = order(BY_COL)
    unpack(dot(by_col, both_w[:, :WIRE]), left_m, 0)
    keep_left.start()
    unpack(dot(by_col, both_w[:, WIRE:]), right_m, pl.multiple_of(own, 32))
    unpack(dot(by_col, other_w[...]), right_m, pl.multiple_of(away, 32))
    keep_right.start()
    mixed = dot(left_m[...], right_m[...], LAST).astype(BF16)
    pack(dot(mixed, spread[...]), packed)
    wire[...] = move(BY_ROW, packed[...].astype(BF16)).astype(BF16)
    keep_left.wait()
    keep_right.wait()


def turn_kernel(mixed_w, saved, wire, mixed_s, d_mixed_s, d_hat, sem):
    fetch = pltpu.make_async_copy(saved.at[D_HAT:SAVED, :], d_hat, sem)
    fetch.start()
    mixed_s[...] = move(BY_HALF, mixed_w[...])
    fetch.wait()

    @pl.loop(0, STEPS)
    def _(step):
        rows, cols = place_of(step)
        hat, scale = normalise(mixed_s[rows, cols])
        d_mixed_s[rows, cols] = normalise_back(d_hat[:, lanes_of(step)], hat, scale).astype(BF16)

    wire[...] = move(BY_CHANNEL, d_mixed_s[...]).astype(BF16)


def update_kernel(
    mixed_w, saved, weight, gain, shift, out_gain, out_shift, out_weight, out_bias,
    update, grad_out, grad_gate, d_normed,
    padded, mixed_s, held, sem,
):
    fetch = pltpu.make_async_copy(saved.at[HAT:D_HAT, :], held, sem)
    fetch.start()
    mixed_s[...] = move(BY_HALF, mixed_w[...])
    gain_c, shift_c = column(gain), column(shift)
    out_gain_c, out_shift_c, out_bias_c = column(out_gain), column(out_shift), column(out_bias)
    out_t = split(out_weight[...].T)
    gate_w = split(weight[:, 4 * WIDTH :])
    grad_out[...] = jnp.zeros_like(grad_out)
    grad_gate[...] = jnp.zeros_like(grad_gate)
    fetch.wait()

    @pl.loop(0, STEPS)
    def _(step):
        lanes = lanes_of(step)
        rows, cols = place_of(step)
        hat_m, _ = normalise(mixed_s[rows, cols])
        normed = split(hat_m * out_gain_c + out_shift_c)
        result = fine(out_t, normed) + out_bias_c
        is_open = held[OPEN - HAT : GIVEN - HAT, lanes]
        padded[lanes, :] = (is_open * result).T
        given = held[GIVEN - HAT :, lanes]
        grad_out[...] += fine(normed, split(given), LAST)
        d_gate = split(given * result * (1.0 - is_open))
        grad_gate[...] += fine(
            split(held[: OPEN - HAT, lanes] * gain_c + shift_c), d_gate, LAST
        )
        d_normed[:, lanes] = fine(gate_w, d_gate)

    drain(update, padded)


def unmix_kernel(
    d_w, kept, spread,
    left_wire, own_wire, away_wire,
    d_mixed_m, terms, packed, left_m, right_m, sems,
):
    own = lax.axis_index("col") % 2 * (TOTAL // 2)
    away = (TOTAL // 2) - own
    get_left = pltpu.make_async_copy(kept.at[:LEFT_ROWS, :], left_m, sems.at[0])
    get_right = pltpu.make_async_copy(kept.at[LEFT_ROWS:KEPT_ROWS, :], right_m, sems.at[1])
    get_left.start()
    get_right.start()
    by_row = order(BY_ROW)
    send = lambda: dot(by_row, packed[...].astype(BF16)).astype(BF16)
    unpack(move(BY_COL, d_w[...]), d_mixed_m, 0)
    d_mixed = dot(d_mixed_m[...], spread[...], LAST).astype(BF16)
    get_left.wait()
    terms[...] = dot(d_mixed, left_m[...], ((0,), (0,)))
    pack(terms[pl.ds(pl.multiple_of(away, 32), TOTAL // 2), :], packed)
    away_wire[...] = send()
    pack(terms[pl.ds(pl.multiple_of(own, 32), TOTAL // 2), :], packed)
    own_wire[...] = send()
    get_right.wait()
    pack(dot(d_mixed, right_m[...]), packed)
    left_wire[...] = send()


def d_hidden_of(d_left_s, d_right_s, factors, step):
    rows, cols = place_of(step)
    lanes = lanes_of(step)
    parts = []
    for i, ref in enumerate((d_left_s, d_right_s)):
        given = ref[rows, cols]
        for j in range(2):
            start = (2 * i + j) * WIDTH
            parts.append(given * factors[start : start + WIDTH, lanes])
    return split(jnp.concatenate(parts, axis=0))


def fetch_saved(saved, held, sems, step):
    lanes = lanes_of(step)
    return pltpu.make_async_copy(saved.at[:OPEN, lanes], held.at[:, lanes], sems.at[step])


def weight_kernel(
    both_w, saved, gain, shift, grad_gate, grad_out,
    grads,
    d_left_s, d_right_s, total, held, sems,
):
    for step in range(STEPS):
        fetch_saved(saved, held, sems, step).start()
    by_half = order(BY_HALF)
    d_left_s[...] = dot(by_half, both_w[:, :WIRE])
    d_right_s[...] = dot(by_half, both_w[:, WIRE:])
    gain_c, shift_c = column(gain), column(shift)
    total[...] = jnp.zeros_like(total)

    @pl.loop(0, STEPS)
    def _(step):
        fetch_saved(saved, held, sems, step).wait()
        d_hidden = d_hidden_of(d_left_s, d_right_s, held, step)
        normed = split(held[HAT:OPEN, lanes_of(step)] * gain_c + shift_c)
        total[...] += fine(normed, d_hidden, LAST)

    grads[:WIDTH, :] = total[:, : 3 * WIDTH]
    grads[WIDTH:, :WIDTH] = total[:, 3 * WIDTH :]
    grads[WIDTH:, WIDTH : 2 * WIDTH] = grad_gate[...]
    grads[WIDTH:, 2 * WIDTH :] = grad_out[...]


def pair_kernel(
    both_w, saved, scale, d_normed, weight, gain,
    grad_pair,
    d_left_s, d_right_s, padded, held, sems,
):
    for step in range(STEPS):
        fetch_saved(saved, held, sems, step).start()
    by_half = order(BY_HALF)
    d_left_s[...] = dot(by_half, both_w[:, :WIRE])
    d_right_s[...] = dot(by_half, both_w[:, WIRE:])
    gain_c = column(gain)
    weight_s = split(weight[:, : 4 * WIDTH])

    @pl.loop(0, STEPS)
    def _(step):
        fetch_saved(saved, held, sems, step).wait()
        lanes = lanes_of(step)
        d_hidden = d_hidden_of(d_left_s, d_right_s, held, step)
        d_hat = (fine(weight_s, d_hidden) + d_normed[:, lanes]) * gain_c
        padded[lanes, :] = normalise_back(d_hat, held[HAT:OPEN, lanes], scale[:, lanes]).T

    drain(grad_pair, padded)


class Raw:
    def __init__(self, value):
        self.value = value


def call(kernel, outs, scratch, *args, smem=0, work=2e9, room=48):
    operands = [a.value if isinstance(a, Raw) else a for a in args]
    results = [jax.ShapeDtypeStruct(*(o.value if isinstance(o, Raw) else o)) for o in outs]

    def spec(value, raw):
        if raw:
            return pl.BlockSpec(memory_space=pl.ANY)
        return pl.BlockSpec(value.shape, lambda i: (0,) * len(value.shape))

    specs = [spec(v, isinstance(w, Raw)) for v, w in zip([*operands, *results], [*args, *outs])]
    specs[:smem] = [pl.BlockSpec(memory_space=pltpu.SMEM)] * smem
    return pl.pallas_call(
        kernel,
        grid=(1,),
        out_shape=results,
        in_specs=specs[: len(args)],
        out_specs=specs[len(args) :],
        scratch_shapes=[pltpu.VMEM(*s) if isinstance(s, tuple) else s for s in scratch],
        compiler_params=pltpu.CompilerParams(vmem_limit_bytes=room * 2**20),
        cost_estimate=pl.CostEstimate(flops=int(work), bytes_accessed=4 * 2**20, transcendentals=0),
    )(*operands)


def spin(step, count, inner):
    size = 32 if inner != 2 else 8
    return [
        (i, i - (i // inner % count) * inner + ((i // inner + step) % count) * inner)
        for i in range(size)
    ]


def meet(value, axis, count, inner):
    others = [lax.ppermute(value, axis, spin(k, count, inner)) for k in range(1, count)]
    if count == 2:
        return value + others[0]
    one, two, three = others
    return (value + two) + (one + three)


def sum_over_devices(grads, row, col, beside):
    core, x = col % 2, row % 4
    pick = lambda a, i: lax.dynamic_index_in_dim(a, i, 0, keepdims=False)
    pairs = grads.reshape(2, WIDTH, 3 * WIDTH)
    taken = lax.ppermute(pick(pairs, 1 - core), "col", SWAP)
    total = pick(pairs, core) + taken
    total = total.astype(BF16).reshape(4, WIDTH // 4, 3 * WIDTH)
    taken = [
        lax.ppermute(pick(total, (x + k) % 4), "row", spin(k, 4, 1)).astype(F32) for k in (1, 2, 3)
    ]
    total = (pick(total, x).astype(F32) + taken[0]) + (taken[1] + taken[2])
    total = meet(total, "row", 4, 8)
    total = meet(total, "col", 4, 2)
    total, beside = lax.optimization_barrier((meet(total, "row", 2, 4).astype(BF16), beside))
    parts = jnp.zeros((4, WIDTH // 4, 3 * WIDTH), BF16)
    parts = lax.dynamic_update_index_in_dim(parts, total, x, 0)
    for k in (1, 2, 3):
        taken = lax.ppermute(total, "row", spin(k, 4, 1))
        parts = lax.dynamic_update_index_in_dim(parts, taken, (x + 4 - k) % 4, 0)
    parts = parts.reshape(WIDTH, 3 * WIDTH)
    other = lax.ppermute(parts, "col", SWAP)
    first = core == 0
    upper, lower = jnp.where(first, parts, other), jnp.where(first, other, parts)
    return upper.astype(F32), lower.astype(F32), beside


def exchange(chunks):
    return lax.all_to_all(chunks, BOTH, 0, 0, tiled=True)


def shards(
    pair,
    cotangent,
    residue_mask,
    ln_gain,
    ln_bias,
    proj_weight,
    proj_bias,
    norm_gain,
    norm_bias,
    out_weight,
    out_bias,
):
    spread = spread_table()
    shape = pair.shape
    places = ROWS * COLS
    row, col = lax.axis_index("row"), lax.axis_index("col")
    pair = pair.reshape(places, WIDTH)
    cotangent = cotangent.reshape(places, WIDTH)
    line = lambda v: v.reshape(-1, WIDTH)
    gain, shift, bias = line(ln_gain), line(ln_bias), line(proj_bias)
    out_gain, out_shift, out_bias = line(norm_gain), line(norm_bias), line(out_bias)
    whole = ((LANES, WIDTH), F32)
    turned = ((WIDTH, LANES), F32)
    square = ((WIDTH, WIDTH), F32)
    halves = lambda kind: ((DEVICES, WIRE), kind)

    wire, mask = call(
        project_kernel,
        [((DEVICES, LANES), BF16), ((1, LANES), F32)],
        [whole, halves(BF16), halves(BF16)],
        residue_mask, pair, proj_weight, bias, gain, shift,
        smem=1,
        room=62,
    )
    got = exchange(wire.reshape(DEVICES, 2, WIRE)).reshape(DEVICES, LANES)
    dma = pltpu.SemaphoreType.DMA
    scale, saved = call(
        prepare_kernel,
        [((1, LANES), F32), Raw(((SAVED, LANES), F32))],
        [whole, whole, ((SAVED, LANES), F32), dma((STEPS,))],
        mask, pair, cotangent, proj_weight, bias, gain, shift, out_gain, out_weight,
        work=1e10,
    )
    other_w = lax.ppermute(got[:, WIRE:], "col", SWAP)
    left_s, right_s = ((LEFT_ROWS, COL_N * 128), BF16), ((TOTAL, COL_N * 128), BF16)
    wire, kept = call(
        mix_kernel,
        [halves(BF16), Raw(((KEPT, COL_N * 128), BF16))],
        [left_s, right_s, halves(F32), dma((2,))],
        got, other_w, spread,
    )
    mixed_w = exchange(wire.reshape(DEVICES, 2, WIRE // 2)).reshape(DEVICES, WIRE)
    (wire,) = call(
        turn_kernel,
        [halves(BF16)],
        [halves(F32), halves(BF16), turned, dma],
        mixed_w, Raw(saved),
    )
    got = exchange(wire.reshape(DEVICES, 2, WIRE // 2)).reshape(DEVICES, WIRE)
    update, grad_out, grad_gate, d_normed = call(
        update_kernel,
        [((places, WIDTH), F32), square, square, turned],
        [whole, halves(F32), ((D_HAT - HAT, LANES), F32), dma],
        mixed_w, Raw(saved), proj_weight, gain, shift, out_gain, out_shift, out_weight, out_bias,
        work=8e9,
    )
    left_wire, own_wire, away_wire = call(
        unmix_kernel,
        [halves(BF16)] * 3,
        [left_s, ((TOTAL, COL_N * 128), F32), halves(F32), left_s, right_s, dma((2,))],
        got, Raw(kept), spread,
    )
    other_wire = lax.ppermute(away_wire, "col", SWAP)
    right_wire = (own_wire.astype(F32) + other_wire.astype(F32)).astype(BF16)
    got = exchange(jnp.stack([left_wire, right_wire], axis=1)).reshape(DEVICES, LANES)
    held = ((OPEN, LANES), F32)
    (grads,) = call(
        weight_kernel,
        [((DEVICES, 3 * WIDTH), F32)],
        [halves(F32), halves(F32), ((WIDTH, 4 * WIDTH), F32), held, dma((STEPS,))],
        got, Raw(saved), gain, shift, grad_gate, grad_out,
    )
    (grad_pair,) = call(
        pair_kernel,
        [((places, WIDTH), F32)],
        [halves(F32), halves(F32), whole, held, dma((STEPS,))],
        got, Raw(saved), scale, d_normed, proj_weight, gain,
        work=8e9,
    )
    upper, lower, grad_pair = sum_over_devices(grads, row, col, grad_pair)
    grad_proj = jnp.concatenate([upper, lower[:, : 2 * WIDTH]], axis=1)
    return update.reshape(shape), grad_pair.reshape(shape), grad_proj, lower[:, 2 * WIDTH :]


def solution(mesh):
    in_specs = (P("row", "col", None), P("row", "col", None)) + (P(),) * 9
    out_specs = (P("row", "col", None), P("row", "col", None), P(), P())
    return jax.shard_map(shards, mesh=mesh, in_specs=in_specs, out_specs=out_specs, check_vma=False)
```

time: 203 us -> 196 us (0.966)
  local copies, waits for them, and re-layouts: 24 us -> 8.83 us
  waiting for transfers between devices: 42.3 us -> 47.6 us
  Pallas kernels: 33.2 us -> 36.7 us
    unnamed x78 -> x30, local copies, waits for them, and re-layouts: 17.1 us -> 2.44 us
    all_to_all x2, waiting for transfers between devices: 27.1 us -> 30.6 us  [exchange(): return lax.all_to_all(chunks, BOTH, 0, 0, tiled=True)]
    pallas_call x8, Pallas kernels: 33.2 us -> 36.7 us  [call(): pl.pallas_call(kernel, grid=(1,), out_shape=results, in_specs=specs[:len(...]
    ppermute x7, waiting for transfers between devices: 4.79 us -> 7.02 us  [meet(): lax.ppermute(value, axis, spin(k, count, inner))]
  transfers between devices with their start and end apart: 19 -> 19, of which waited for: 16 -> 17; matrix products, arithmetic and copies ran while one was open for 0% -> 0% of each run, Pallas kernels for 8% -> 9%
where the time goes in v3:
time: 196 us
  blocking collectives  66 us (34%)
  waiting for transfers between devices  47.6 us (24%)
  Pallas kernels  36.7 us (19%)
  starting transfers between devices  34.7 us (18%)
  local copies, waits for them, and re-layouts  8.83 us (5%)
    all_to_all x2, blocking collectives, exchange(): return lax.all_to_all(chunks, BOTH, 0, 0, tiled=True)  66 us
    pallas_call x8, Pallas kernels, call(): pl.pallas_call(kernel, grid=(1,), out_shape=results, in_specs=specs[:len(...  36.7 us
    all_to_all x2, waiting for transfers between devices, exchange(): return lax.all_to_all(chunks, BOTH, 0, 0, tiled=True)  30.6 us
    all_to_all x2, starting transfers between devices, exchange(): return lax.all_to_all(chunks, BOTH, 0, 0, tiled=True)  11.9 us
    ppermute x1, starting transfers between devices, sum_over_devices(): other = lax.ppermute(parts, 'col', SWAP)  8.39 us
    ppermute x7, starting transfers between devices, meet(): lax.ppermute(value, axis, spin(k, count, inner))  7.7 us
    ppermute x7, waiting for transfers between devices, meet(): lax.ppermute(value, axis, spin(k, count, inner))  7.02 us
  transfers between devices with their start and end apart: 19, of which 17 were waited for; matrix products, arithmetic and copies ran while one was open for 0% of the time, Pallas kernels for 9%

profile of v3, /device:TPU:1, one launch (start us, length us, event | category | flops | bytes accessed | tf_op | source)
XLA Modules:
  0.0 196.0 jit_solution(8091150302818853959)
XLA Ops:
  0.6 0.0 copy-start
  0.6 6.1 %shard_map.147 = (bf16[256,1536]{1,0:T(8,128)(2,1)}, f32[1,1536]{1,0:T(1,128)}) custom-call(s32[576]{0:T(1024)} %valid.1, f32[1296,128]{1,0:T(8,128)} %bitcast.68, f32[128,640]{1,0:T(8,128)} %weight.7, f32[5,128]{1,0:T(8,128)} %bitcast.71, f32[1,128]{1,0:T(1,128)} %bitcast.63, f32[1,128]{1,0:T(1,128)} %bitcast.59), custom_call_target="tpu_custom_call" | custom-call | flops 2000000000 | bytes 4194304 | tf_op jit(solution)/shard_map/pallas_call | solution.py:417
  6.8 3.0 %reshape.74 = bf16[256,2,768]{2,1,0:T(2,128)(2,1)} reshape(bf16[256,1536]{1,0:T(8,128)(2,1)} %get-tuple-element.19) | data formatting | bytes 1572864 | tf_op jit(solution)/shard_map/reshape | solution.py:510
  9.7 0.0 copy-start.7
  9.8 0.0 copy-start.12
  9.8 42.6 %all_to_all.20 = bf16[256,2,768]{2,1,0:T(2,128)(2,1)S(1)} all-to-all(bf16[256,2,768]{2,1,0:T(2,128)(2,1)} %reshape.74), channel_id=1, replica_groups=mesh['row'=32,'col'=8] {'row','col'}, dimensions={0} | all-to-all | bytes 1572864 | tf_op jit(solution)/shard_map/all_to_all | solution.py:472
  52.3 0.1 copy.18
  52.5 0.1 collective-permute-start
  52.6 1.7 collective-permute-done.other_w
  54.3 2.6 %shard_map.148 = (bf16[256,768]{1,0:T(8,128)(2,1)S(1)}, bf16[3072,1024]{1,0:T(8,128)(2,1)}) custom-call(bf16[256,1536]{1,0:T(8,128)(2,1)S(1)} %bitcast.52, bf16[256,768]{1,0:T(8,128)(2,1)S(1)} %collective-permute-done.other_w, bf16[576,1024]{1,0:T(8,128)(2,1)S(1)} %copy-done), custom_call_target="tpu_custom_call" | custom-call | flops 2000000000 | bytes 4194304 | tf_op jit(solution)/shard_map/pallas_call | solution.py:417
  56.9 0.8 reshape.76
  57.7 5.2 %all-to-all-start.1 = ((bf16[256,2,384]{2,1,0:T(2,128)(2,1)}), bf16[256,2,384]{2,1,0:T(2,128)(2,1)S(1)}, u32[]{:S(2)}, u32[]{:S(2)}) async-start(bf16[256,2,384]{2,1,0:T(2,128)(2,1)} %reshape.76), calls=%async_computation.1 | async-start | bytes 786432 | tf_op jit(solution)/shard_map/all_to_all | solution.py:472
  63.0 0.0 copy-start.5
  63.0 1.0 copy-done.5
  64.0 6.7 %shard_map.149 = (f32[1,1536]{1,0:T(1,128)S(1)}, f32[1024,1536]{1,0:T(8,128)}) custom-call(f32[1,1536]{1,0:T(1,128)S(1)} %copy-done.12, f32[1296,128]{1,0:T(8,128)S(1)} %bitcast.69, f32[1296,128]{1,0:T(8,128)S(1)} %bitcast.70, f32[128,640]{1,0:T(8,128)S(1)} %copy-done.5, f32[5,128]{1,0:T(8,128)S(1)} %bitcast.72, f32[1,128]{1,0:T(1,128)S(1)} %bitcast.64, ...), custom_call_target="tpu_custom_call" | custom-call | flops 10000000000 | bytes 4194304 | tf_op jit(solution)/shard_map/pallas_call | solution.py:417
  70.7 10.8 %all-to-all-done.1 = bf16[256,2,384]{2,1,0:T(2,128)(2,1)S(1)} async-done(((bf16[256,2,384]{2,1,0:T(2,128)(2,1)}), bf16[256,2,384]{2,1,0:T(2,128)(2,1)S(1)}, u32[]{:S(2)}, u32[]{:S(2)}) %all-to-all-start.1) | async-done | bytes 393248 | tf_op jit(solution)/shard_map/all_to_all | solution.py:472
  81.6 0.1 copy.19
  81.6 2.2 %shard_map.151 = bf16[256,768]{1,0:T(8,128)(2,1)S(1)} custom-call(bf16[256,768]{1,0:T(8,128)(2,1)S(1)} %bitcast.56, f32[1024,1536]{1,0:T(8,128)} %get-tuple-element.22.saved), custom_call_target="tpu_custom_call" | custom-call | flops 2000000000 | bytes 4194304 | tf_op jit(solution)/shard_map/pallas_call | solution.py:417
  83.8 0.1 reshape.83
  83.9 23.5 %all_to_all.21 = bf16[256,2,384]{2,1,0:T(2,128)(2,1)S(1)} all-to-all(bf16[256,2,384]{2,1,0:T(2,128)(2,1)S(1)} %reshape.83), channel_id=1, replica_groups=mesh['row'=32,'col'=8] {'row','col'}, dimensions={0} | all-to-all | bytes 786432 | tf_op jit(solution)/shard_map/all_to_all | solution.py:472
  107.3 0.1 copy.20
  107.4 0.0 copy-start.6
  107.4 0.0 copy-start.11
  107.4 4.1 %shard_map.152 = (bf16[256,768]{1,0:T(8,128)(2,1)S(1)}, bf16[256,768]{1,0:T(8,128)(2,1)S(1)}, bf16[256,768]{1,0:T(8,128)(2,1)S(1)}) custom-call(bf16[256,768]{1,0:T(8,128)(2,1)S(1)} %bitcast.55, bf16[3072,1024]{1,0:T(8,128)(2,1)} %get-tuple-element.24.kept, bf16[576,1024]{1,0:T(8,128)(2,1)S(1)} %copy-done), custom_call_target="tpu_custom_call" | custom-call | flops 2000000000 | bytes 4194304 | tf_op jit(solution)/shard_map/pallas_call | solution.py:417
  111.6 0.2 collective-permute-start.1
  111.8 1.6 collective-permute-done.1
  113.4 0.1 fusion
  113.5 0.1 pad_maximum_fusion
  113.6 1.7 copy.17
  115.3 6.7 %all-to-all-start.3 = ((bf16[256,2,768]{2,1,0:T(2,128)(2,1)}), bf16[256,2,768]{2,1,0:T(2,128)(2,1)}, u32[]{:S(2)}, u32[]{:S(2)}) async-start(bf16[256,2,768]{2,1,0:T(2,128)(2,1)} %copy.17), calls=%async_computation.3 | async-start | bytes 1572864 | tf_op jit(solution)/shard_map/all_to_all | solution.py:472
  122.0 6.4 %shard_map.150 = (f32[1296,128]{1,0:T(8,128)}, f32[128,128]{1,0:T(8,128)S(1)}, f32[128,128]{1,0:T(8,128)S(1)}, f32[128,1536]{1,0:T(8,128)S(1)}) custom-call(bf16[256,768]{1,0:T(8,128)(2,1)S(1)} %bitcast.57, f32[1024,1536]{1,0:T(8,128)} %get-tuple-element.22.saved, f32[128,640]{1,0:T(8,128)S(1)} %copy-done.6, f32[1,128]{1,0:T(1,128)S(1)} %bitcast.65, ...), custom_call_target="tpu_custom_call" | custom-call | flops 8000000000 | bytes 4194304 | tf_op jit(solution)/shard_map/pallas_call | solution.py:417
  128.4 19.7 %all-to-all-done.3 = bf16[256,2,768]{2,1,0:T(2,128)(2,1)} async-done(((bf16[256,2,768]{2,1,0:T(2,128)(2,1)}), bf16[256,2,768]{2,1,0:T(2,128)(2,1)}, u32[]{:S(2)}, u32[]{:S(2)}) %all-to-all-start.3) | async-done | bytes 786464 | tf_op jit(solution)/shard_map/all_to_all | solution.py:472
  148.2 1.2 copy.21
  149.4 3.8 %shard_map.153 = f32[256,384]{1,0:T(8,128)S(1)} custom-call(bf16[256,1536]{1,0:T(8,128)(2,1)S(1)} %bitcast.49, f32[1024,1536]{1,0:T(8,128)} %get-tuple-element.22.saved, f32[1,128]{1,0:T(1,128)S(1)} %bitcast.66, f32[1,128]{1,0:T(1,128)S(1)} %bitcast.62, f32[128,128]{1,0:T(8,128)S(1)} %get-tuple-element.28.grad_gate, f32[128,128]{1,0:T(8,128)S(1)} %get-tuple-element.29.grad_out), custom_call_target="tpu_custom_call" | custom-call | flops 2000000000 | bytes 4194304 | tf_op jit(solution)/shard_map/pallas_call | solution.py:417
  153.3 0.1 collective-permute-start.2
  153.4 1.4 collective-permute-done.2
  154.9 0.1 collective-permute-start.3
  154.9 1.1 collective-permute-start.4
  156.1 1.5 collective-permute-start.5
  157.6 1.2 collective-permute-done.3
  158.8 0.4 collective-permute-done.4
  159.2 0.7 collective-permute-done.5
  160.0 0.7 collective-permute-start.6
  160.6 0.8 collective-permute-start.7
  161.5 1.8 collective-permute-start.8
  163.3 1.2 collective-permute-done.6
  164.5 0.5 collective-permute-done.7
  165.1 1.0 collective-permute-start.10
  166.1 2.6 %collective-permute-start.11 = (f32[32,384]{1,0:T(8,128)S(1)}, f32[32,384]{1,0:T(8,128)S(1)}, u32[]{:S(2)}, u32[]{:S(2)}) collective-permute-start(f32[32,384]{1,0:T(8,128)S(1)} %add_add_fusion.1), channel_id=1, source_target_pairs={{0,6},{1,7},{2,0},{3,1},{4,2},{5,3},{6,4},{7,5},{8,14},{9,15},{10,... | collective-permute-start | bytes 147464 | tf_op jit(solution)/shard_map/ppermute | solution.py:438
  168.6 1.5 collective-permute-done.10
  170.1 2.4 %collective-permute-done.9 = f32[32,384]{1,0:T(8,128)S(1)} collective-permute-done((f32[32,384]{1,0:T(8,128)S(1)}, f32[32,384]{1,0:T(8,128)S(1)}, u32[]{:S(2)}, u32[]{:S(2)}) %collective-permute-start.9) | collective-permute-done | bytes 49184 | tf_op jit(solution)/shard_map/ppermute | solution.py:438
  172.5 0.8 collective-permute-start.12
  173.3 4.7 %shard_map.154 = f32[1296,128]{1,0:T(8,128)} custom-call(bf16[256,1536]{1,0:T(8,128)(2,1)S(1)} %bitcast.50, f32[1024,1536]{1,0:T(8,128)} %get-tuple-element.22.saved, f32[1,1536]{1,0:T(1,128)S(1)} %get-tuple-element.30.scale, f32[128,1536]{1,0:T(8,128)S(1)} %get-tuple-element.31.d_normed, f32[128,640]{1,0:T(8,128)S(1)} %copy-done.6, f32[1,128]{1,0:T(1,128)S(1)} %bitcast.67), custom_call_target="tpu_custom_call" | custom-call | flops 8000000000 | bytes 4194304 | tf_op jit(solution)/shard_map/pallas_call | solution.py:417
  178.0 1.4 collective-permute-done.12
  179.5 1.2 collective-permute-start.13
  180.6 1.9 collective-permute-start.14
  182.5 0.6 collective-permute-start.15
  183.1 0.6 collective-permute-done.13
  183.7 1.1 collective-permute-done.14
  184.8 0.4 collective-permute-done.15
  185.2 8.4 %collective-permute-start.16 = (bf16[128,384]{1,0:T(8,128)(2,1)S(1)}, bf16[128,384]{1,0:T(8,128)(2,1)S(1)}, u32[]{:S(2)}, u32[]{:S(2)}) collective-permute-start(bf16[128,384]{1,0:T(8,128)(2,1)S(1)} %bitcast.82), channel_id=1, source_target_pairs={{0,1},{1,0},{2,3},{3,2},{4,5},{5,4},{6,7},{7,6},{8,9},{9,8},{10,11... | collective-permute-start | bytes 294920 | tf_op jit(solution)/shard_map/ppermute | solution.py:465
  193.6 0.9 collective-permute-done.16
  194.6 0.6 slice.14
  195.3 0.7 pad_maximum_fusion.1
  (37 shorter events, 0.3 us)
Async XLA Ops:
  0.6 53.7 %copy-start = (bf16[576,1024]{1,0:T(8,128)(2,1)S(1)}, bf16[576,1024]{1,0:T(8,128)(2,1)}, u32[]{:S(2)}) copy-start(bf16[576,1024]{1,0:T(8,128)(2,1)} %constant.96.clone.spread) | copy-start | bytes 3538948
  9.7 53.2 %copy-start.1 = (f32[128]{0:T(128)S(1)}, f32[128]{0:T(128)}, u32[]{:S(2)}) copy-start(f32[128]{0:T(128)} %param.16) | copy-start | bytes 1540
  9.7 53.2 %copy-start.2 = (f32[128]{0:T(128)S(1)}, f32[128]{0:T(128)}, u32[]{:S(2)}) copy-start(f32[128]{0:T(128)} %param.15) | copy-start | bytes 1540
  9.7 53.2 %copy-start.3 = (f32[18,72,128]{2,1,0:T(8,128)S(1)}, f32[18,72,128]{2,1,0:T(8,128)}, u32[]{:S(2)}) copy-start(f32[18,72,128]{2,1,0:T(8,128)} %param.12) | copy-start | bytes 1990660
  9.7 53.2 %copy-start.4 = (f32[18,72,128]{2,1,0:T(8,128)S(1)}, f32[18,72,128]{2,1,0:T(8,128)}, u32[]{:S(2)}) copy-start(f32[18,72,128]{2,1,0:T(8,128)} %param.13) | copy-start | bytes 1990660
  9.7 53.2 %copy-start.7 = (f32[128,128]{1,0:T(8,128)S(1)}, f32[128,128]{1,0:T(8,128)}, u32[]{:S(2)}) copy-start(f32[128,128]{1,0:T(8,128)} %out_weight.3) | copy-start | bytes 196612
  9.7 53.2 %copy-start.8 = (f32[640]{0:T(1024)S(1)}, f32[640]{0:T(1024)}, u32[]{:S(2)}) copy-start(f32[640]{0:T(1024)} %param.18) | copy-start | bytes 7684
  9.8 53.2 %copy-start.9 = (f32[128]{0:T(128)S(1)}, f32[128]{0:T(128)}, u32[]{:S(2)}) copy-start(f32[128]{0:T(128)} %param.19) | copy-start | bytes 1540
  9.8 53.2 %copy-start.12 = (f32[1,1536]{1,0:T(1,128)S(1)}, f32[1,1536]{1,0:T(1,128)}, u32[]{:S(2)}) copy-start(f32[1,1536]{1,0:T(1,128)} %get-tuple-element.21.mask) | copy-start | bytes 18436
  52.5 1.8 collective-permute-start
  57.7 23.8 %all-to-all-start.1 = ((bf16[256,2,384]{2,1,0:T(2,128)(2,1)}), bf16[256,2,384]{2,1,0:T(2,128)(2,1)S(1)}, u32[]{:S(2)}, u32[]{:S(2)}) async-start(bf16[256,2,384]{2,1,0:T(2,128)(2,1)} %reshape.76), calls=%async_computation.1 | async-start | bytes 786432 | tf_op jit(solution)/shard_map/all_to_all | solution.py:472
  63.0 1.0 copy-start.5
  107.4 14.6 %copy-start.6 = (f32[128,640]{1,0:T(8,128)S(1)}, f32[128,640]{1,0:T(8,128)}, u32[]{:S(2)}) copy-start(f32[128,640]{1,0:T(8,128)} %weight.7) | copy-start | bytes 983044
  107.4 14.6 %copy-start.10 = (f32[128]{0:T(128)S(1)}, f32[128]{0:T(128)}, u32[]{:S(2)}) copy-start(f32[128]{0:T(128)} %param.20) | copy-start | bytes 1540
  107.4 14.6 %copy-start.11 = (f32[128]{0:T(128)S(1)}, f32[128]{0:T(128)}, u32[]{:S(2)}) copy-start(f32[128]{0:T(128)} %param.22) | copy-start | bytes 1540
  111.6 1.8 collective-permute-start.1
  115.3 32.9 %all-to-all-start.3 = ((bf16[256,2,768]{2,1,0:T(2,128)(2,1)}), bf16[256,2,768]{2,1,0:T(2,128)(2,1)}, u32[]{:S(2)}, u32[]{:S(2)}) async-start(bf16[256,2,768]{2,1,0:T(2,128)(2,1)} %copy.17), calls=%async_computation.3 | async-start | bytes 1572864 | tf_op jit(solution)/shard_map/all_to_all | solution.py:472
  153.3 1.5 collective-permute-start.2
  154.9 4.0 %collective-permute-start.3 = (bf16[32,384]{1,0:T(8,128)(2,1)S(1)}, bf16[32,384]{1,0:T(8,128)(2,1)S(1)}, u32[]{:S(2)}, u32[]{:S(2)}) collective-permute-start(bf16[32,384]{1,0:T(8,128)(2,1)S(1)} %get-tuple-element.36), channel_id=1, source_target_pairs={{0,8},{8,16},{16,24},{24,0},{32,40},{40,48},{48,56},{56,32},{64,72... | collective-permute-start | bytes 73736 | tf_op jit(solution)/shard_map/ppermute | solution.py:453
  154.9 4.3 %collective-permute-start.4 = (bf16[32,384]{1,0:T(8,128)(2,1)S(1)}, bf16[32,384]{1,0:T(8,128)(2,1)S(1)}, u32[]{:S(2)}, u32[]{:S(2)}) collective-permute-start(bf16[32,384]{1,0:T(8,128)(2,1)S(1)} %get-tuple-element.38), channel_id=1, source_target_pairs={{0,16},{8,24},{16,0},{24,8},{32,48},{40,56},{48,32},{56,40},{64,80... | collective-permute-start | bytes 73736 | tf_op jit(solution)/shard_map/ppermute | solution.py:453
  156.1 3.9 %collective-permute-start.5 = (bf16[32,384]{1,0:T(8,128)(2,1)S(1)}, bf16[32,384]{1,0:T(8,128)(2,1)S(1)}, u32[]{:S(2)}, u32[]{:S(2)}) collective-permute-start(bf16[32,384]{1,0:T(8,128)(2,1)S(1)} %get-tuple-element.37), channel_id=1, source_target_pairs={{0,24},{8,0},{16,8},{24,16},{32,56},{40,32},{48,40},{56,48},{64,88... | collective-permute-start | bytes 73736 | tf_op jit(solution)/shard_map/ppermute | solution.py:453
  160.0 4.6 %collective-permute-start.6 = (f32[32,384]{1,0:T(8,128)S(1)}, f32[32,384]{1,0:T(8,128)S(1)}, u32[]{:S(2)}, u32[]{:S(2)}) collective-permute-start(f32[32,384]{1,0:T(8,128)S(1)} %fusion.2), channel_id=1, source_target_pairs={{0,128},{8,136},{16,144},{24,152},{32,160},{40,168},{48,176},{56,1... | collective-permute-start | bytes 147464 | tf_op jit(solution)/shard_map/ppermute | solution.py:438
  160.6 4.4 %collective-permute-start.7 = (f32[32,384]{1,0:T(8,128)S(1)}, f32[32,384]{1,0:T(8,128)S(1)}, u32[]{:S(2)}, u32[]{:S(2)}) collective-permute-start(f32[32,384]{1,0:T(8,128)S(1)} %fusion.2), channel_id=1, source_target_pairs={{0,64},{8,72},{16,80},{24,88},{32,96},{40,104},{48,112},{56,120},{... | collective-permute-start | bytes 147464 | tf_op jit(solution)/shard_map/ppermute | solution.py:438
  161.5 3.6 %collective-permute-start.8 = (f32[32,384]{1,0:T(8,128)S(1)}, f32[32,384]{1,0:T(8,128)S(1)}, u32[]{:S(2)}, u32[]{:S(2)}) collective-permute-start(f32[32,384]{1,0:T(8,128)S(1)} %fusion.2), channel_id=1, source_target_pairs={{0,192},{8,200},{16,208},{24,216},{32,224},{40,232},{48,240},{56,2... | collective-permute-start | bytes 147464 | tf_op jit(solution)/shard_map/ppermute | solution.py:438
  165.1 5.0 %collective-permute-start.10 = (f32[32,384]{1,0:T(8,128)S(1)}, f32[32,384]{1,0:T(8,128)S(1)}, u32[]{:S(2)}, u32[]{:S(2)}) collective-permute-start(f32[32,384]{1,0:T(8,128)S(1)} %add_add_fusion.1), channel_id=1, source_target_pairs={{0,2},{1,3},{2,4},{3,5},{4,6},{5,7},{6,0},{7,1},{8,10},{9,11},{10,... | collective-permute-start | bytes 147464 | tf_op jit(solution)/shard_map/ppermute | solution.py:438
  166.1 4.0 %collective-permute-start.11 = (f32[32,384]{1,0:T(8,128)S(1)}, f32[32,384]{1,0:T(8,128)S(1)}, u32[]{:S(2)}, u32[]{:S(2)}) collective-permute-start(f32[32,384]{1,0:T(8,128)S(1)} %add_add_fusion.1), channel_id=1, source_target_pairs={{0,6},{1,7},{2,0},{3,1},{4,2},{5,3},{6,4},{7,5},{8,14},{9,15},{10,... | collective-permute-start | bytes 147464 | tf_op jit(solution)/shard_map/ppermute | solution.py:438
  168.6 3.9 %collective-permute-start.9 = (f32[32,384]{1,0:T(8,128)S(1)}, f32[32,384]{1,0:T(8,128)S(1)}, u32[]{:S(2)}, u32[]{:S(2)}) collective-permute-start(f32[32,384]{1,0:T(8,128)S(1)} %add_add_fusion.1), channel_id=1, source_target_pairs={{0,4},{1,5},{2,6},{3,7},{4,0},{5,1},{6,2},{7,3},{8,12},{9,13},{10,... | collective-permute-start | bytes 147464 | tf_op jit(solution)/shard_map/ppermute | solution.py:438
  172.5 7.0 %collective-permute-start.12 = (f32[32,384]{1,0:T(8,128)S(1)}, f32[32,384]{1,0:T(8,128)S(1)}, u32[]{:S(2)}, u32[]{:S(2)}) collective-permute-start(f32[32,384]{1,0:T(8,128)S(1)} %add_add_fusion), channel_id=1, source_target_pairs={{0,32},{8,40},{16,48},{24,56},{32,0},{40,8},{48,16},{56,24},{64,96... | collective-permute-start | bytes 147464 | tf_op jit(solution)/shard_map/ppermute | solution.py:438
  179.5 4.3 %collective-permute-start.13 = (bf16[32,384]{1,0:T(8,128)(2,1)S(1)}, bf16[32,384]{1,0:T(8,128)(2,1)S(1)}, u32[]{:S(2)}, u32[]{:S(2)}) collective-permute-start(bf16[32,384]{1,0:T(8,128)(2,1)S(1)} %add_convert_fusion.1), channel_id=1, source_target_pairs={{0,8},{8,16},{16,24},{24,0},{32,40},{40,48},{48,56},{56,32},{64,72... | collective-permute-start | bytes 73736 | tf_op jit(solution)/shard_map/ppermute | solution.py:462
  180.6 4.2 %collective-permute-start.14 = (bf16[32,384]{1,0:T(8,128)(2,1)S(1)}, bf16[32,384]{1,0:T(8,128)(2,1)S(1)}, u32[]{:S(2)}, u32[]{:S(2)}) collective-permute-start(bf16[32,384]{1,0:T(8,128)(2,1)S(1)} %add_convert_fusion.1), channel_id=1, source_target_pairs={{0,16},{8,24},{16,0},{24,8},{32,48},{40,56},{48,32},{56,40},{64,80... | collective-permute-start | bytes 73736 | tf_op jit(solution)/shard_map/ppermute | solution.py:462
  182.5 2.7 %collective-permute-start.15 = (bf16[32,384]{1,0:T(8,128)(2,1)S(1)}, bf16[32,384]{1,0:T(8,128)(2,1)S(1)}, u32[]{:S(2)}, u32[]{:S(2)}) collective-permute-start(bf16[32,384]{1,0:T(8,128)(2,1)S(1)} %add_convert_fusion.1), channel_id=1, source_target_pairs={{0,24},{8,0},{16,8},{24,16},{32,56},{40,32},{48,40},{56,48},{64,88... | collective-permute-start | bytes 73736 | tf_op jit(solution)/shard_map/ppermute | solution.py:462
  185.2 9.3 %collective-permute-start.16 = (bf16[128,384]{1,0:T(8,128)(2,1)S(1)}, bf16[128,384]{1,0:T(8,128)(2,1)S(1)}, u32[]{:S(2)}, u32[]{:S(2)}) collective-permute-start(bf16[128,384]{1,0:T(8,128)(2,1)S(1)} %bitcast.82), channel_id=1, source_target_pairs={{0,1},{1,0},{2,3},{3,2},{4,5},{5,4},{6,7},{7,6},{8,9},{9,8},{10,11... | collective-permute-start | bytes 294920 | tf_op jit(solution)/shard_map/ppermute | solution.py:465

commit v4 on v3

--- a/solution.py
+++ b/solution.py
@@ -305,30 +305,33 @@
     drain(update, padded)
 
 
-def unmix_kernel(
+def unmix_right_kernel(
     d_w, kept, spread,
-    left_wire, own_wire, away_wire,
-    d_mixed_m, terms, packed, left_m, right_m, sems,
+    d_mixed, own_wire, away_wire,
+    d_mixed_m, terms, packed, left_m, sem,
 ):
     own = lax.axis_index("col") % 2 * (TOTAL // 2)
     away = (TOTAL // 2) - own
-    get_left = pltpu.make_async_copy(kept.at[:LEFT_ROWS, :], left_m, sems.at[0])
-    get_right = pltpu.make_async_copy(kept.at[LEFT_ROWS:KEPT_ROWS, :], right_m, sems.at[1])
+    get_left = pltpu.make_async_copy(kept.at[:LEFT_ROWS, :], left_m, sem)
     get_left.start()
+    by_row = order(BY_ROW)
+    unpack(move(BY_COL, d_w[...]), d_mixed_m, 0)
+    d_mixed[...] = dot(d_mixed_m[...], spread[...], LAST).astype(BF16)
+    get_left.wait()
+    terms[...] = dot(d_mixed[...], left_m[...], ((0,), (0,)))
+    pack(terms[pl.ds(pl.multiple_of(away, 32), TOTAL // 2), :], packed)
+    away_wire[...] = dot(by_row, packed[...].astype(BF16)).astype(BF16)
+    pack(terms[pl.ds(pl.multiple_of(own, 32), TOTAL // 2), :], packed)
+    own_wire[...] = dot(by_row, packed[...].astype(BF16)).astype(BF16)
+
+
+def unmix_left_kernel(d_mixed, kept, left_wire, packed, right_m, sem):
+    get_right = pltpu.make_async_copy(kept.at[LEFT_ROWS:KEPT_ROWS, :], right_m, sem)
     get_right.start()
     by_row = order(BY_ROW)
-    send = lambda: dot(by_row, packed[...].astype(BF16)).astype(BF16)
-    unpack(move(BY_COL, d_w[...]), d_mixed_m, 0)
-    d_mixed = dot(d_mixed_m[...], spread[...], LAST).astype(BF16)
-    get_left.wait()
-    terms[...] = dot(d_mixed, left_m[...], ((0,), (0,)))
-    pack(terms[pl.ds(pl.multiple_of(away, 32), TOTAL // 2), :], packed)
-    away_wire[...] = send()
-    pack(terms[pl.ds(pl.multiple_of(own, 32), TOTAL // 2), :], packed)
-    own_wire[...] = send()
     get_right.wait()
-    pack(dot(d_mixed, right_m[...]), packed)
-    left_wire[...] = send()
+    pack(dot(d_mixed[...], right_m[...]), packed)
+    left_wire[...] = dot(by_row, packed[...].astype(BF16)).astype(BF16)
 
 
 def d_hidden_of(d_left_s, d_right_s, factors, step):
@@ -398,6 +401,15 @@
     drain(grad_pair, padded)
 
 
+def join_kernel(own, other, grad_proj, grad_out):
+    first = lax.axis_index("col") % 2 == 0
+    own, other = own[...].astype(F32), other[...].astype(F32)
+    upper, lower = jnp.where(first, own, other), jnp.where(first, other, own)
+    grad_proj[:, : 3 * WIDTH] = upper
+    grad_proj[:, 3 * WIDTH :] = lower[:, : 2 * WIDTH]
+    grad_out[...] = lower[:, 2 * WIDTH :]
+
+
 class Raw:
     def __init__(self, value):
         self.value = value
@@ -434,6 +446,14 @@
     ]
 
 
+LINES = [
+    [(y * 8 + high * 4 + x) * COL_N + low * 2 + core for high in range(2) for low in range(4)]
+    for y in range(4)
+    for x in range(4)
+    for core in range(2)
+]
+
+
 def meet(value, axis, count, inner):
     others = [lax.ppermute(value, axis, spin(k, count, inner)) for k in range(1, count)]
     if count == 2:
@@ -448,14 +468,16 @@
     pairs = grads.reshape(2, WIDTH, 3 * WIDTH)
     taken = lax.ppermute(pick(pairs, 1 - core), "col", SWAP)
     total = pick(pairs, core) + taken
-    total = total.astype(BF16).reshape(4, WIDTH // 4, 3 * WIDTH)
+    total = total.reshape(4, WIDTH // 4, 3 * WIDTH)
     taken = [
-        lax.ppermute(pick(total, (x + k) % 4), "row", spin(k, 4, 1)).astype(F32) for k in (1, 2, 3)
+        lax.ppermute(pick(total, (x + k) % 4), "row", spin(k, 4, 1)) for k in (1, 2, 3)
     ]
-    total = (pick(total, x).astype(F32) + taken[0]) + (taken[1] + taken[2])
+    total = (pick(total, x) + taken[0]) + (taken[1] + taken[2])
     total = meet(total, "row", 4, 8)
-    total = meet(total, "col", 4, 2)
-    total, beside = lax.optimization_barrier((meet(total, "row", 2, 4).astype(BF16), beside))
+    total = jnp.broadcast_to(total.astype(BF16)[None], (8,) + total.shape)
+    total = lax.all_to_all(total, BOTH, 0, 0, axis_index_groups=LINES, tiled=True)
+    total = jnp.sum(total.astype(F32), axis=0).astype(BF16)
+    total, beside = lax.optimization_barrier((total, beside))
     parts = jnp.zeros((4, WIDTH // 4, 3 * WIDTH), BF16)
     parts = lax.dynamic_update_index_in_dim(parts, total, x, 0)
     for k in (1, 2, 3):
@@ -463,9 +485,7 @@
         parts = lax.dynamic_update_index_in_dim(parts, taken, (x + 4 - k) % 4, 0)
     parts = parts.reshape(WIDTH, 3 * WIDTH)
     other = lax.ppermute(parts, "col", SWAP)
-    first = core == 0
-    upper, lower = jnp.where(first, parts, other), jnp.where(first, other, parts)
-    return upper.astype(F32), lower.astype(F32), beside
+    return parts, other, beside
 
 
 def exchange(chunks):
@@ -539,13 +559,19 @@
         mixed_w, Raw(saved), proj_weight, gain, shift, out_gain, out_shift, out_weight, out_bias,
         work=8e9,
     )
-    left_wire, own_wire, away_wire = call(
-        unmix_kernel,
-        [halves(BF16)] * 3,
-        [left_s, ((TOTAL, COL_N * 128), F32), halves(F32), left_s, right_s, dma((2,))],
+    d_mixed, own_wire, away_wire = call(
+        unmix_right_kernel,
+        [((LEFT_ROWS, TOTAL), BF16), halves(BF16), halves(BF16)],
+        [left_s, ((TOTAL, COL_N * 128), F32), halves(F32), left_s, dma],
         got, Raw(kept), spread,
     )
     other_wire = lax.ppermute(away_wire, "col", SWAP)
+    (left_wire,) = call(
+        unmix_left_kernel,
+        [halves(BF16)],
+        [halves(F32), right_s, dma],
+        d_mixed, Raw(kept),
+    )
     right_wire = (own_wire.astype(F32) + other_wire.astype(F32)).astype(BF16)
     got = exchange(jnp.stack([left_wire, right_wire], axis=1)).reshape(DEVICES, LANES)
     held = ((OPEN, LANES), F32)
@@ -562,9 +588,11 @@
         got, Raw(saved), scale, d_normed, proj_weight, gain,
         work=8e9,
     )
-    upper, lower, grad_pair = sum_over_devices(grads, row, col, grad_pair)
-    grad_proj = jnp.concatenate([upper, lower[:, : 2 * WIDTH]], axis=1)
-    return update.reshape(shape), grad_pair.reshape(shape), grad_proj, lower[:, 2 * WIDTH :]
+    own, other, grad_pair = sum_over_devices(grads, row, col, grad_pair)
+    grad_proj, grad_out = call(
+        join_kernel, [((WIDTH, 5 * WIDTH), F32), square], [], own, other, work=1e8
+    )
+    return update.reshape(shape), grad_pair.reshape(shape), grad_proj, grad_out
 
 
 def solution(mesh):

time: 196 us -> 192 us (0.980)
  starting transfers between devices: 34.7 us -> 30.9 us
    ppermute x7 -> x3, waiting for transfers between devices: 7.02 us -> 1.9 us  [meet(): lax.ppermute(value, axis, spin(k, count, inner))]
    ppermute x7 -> x3, starting transfers between devices: 7.7 us -> 3.15 us  [meet(): lax.ppermute(value, axis, spin(k, count, inner))]
    all_to_all x0 -> x1, waiting for transfers between devices: none -> 3.85 us  [sum_over_devices(): lax.all_to_all(total, BOTH, 0, 0, axis_index_groups=LINES, tiled=True)]
    all_to_all x0 -> x1, starting transfers between devices: none -> 3.39 us  [sum_over_devices(): lax.all_to_all(total, BOTH, 0, 0, axis_index_groups=LINES, tiled=True)]
    ppermute x1, starting transfers between devices: 8.39 us -> 5.7 us  [sum_over_devices(): other = lax.ppermute(parts, 'col', SWAP)]
    pallas_call x8 -> x10, Pallas kernels: 36.7 us -> 38.6 us  [call(): pl.pallas_call(kernel, grid=(1,), out_shape=results, in_specs=specs[:len(...]
  transfers between devices with their start and end apart: 19 -> 16, of which waited for: 17 -> 13; matrix products, arithmetic and copies ran while one was open for 0% -> 0% of each run, Pallas kernels for 9% -> 10%
where the time goes in v4:
time: 192 us
  blocking collectives  66 us (34%)
  waiting for transfers between devices  46 us (24%)
  Pallas kernels  38.6 us (20%)
  starting transfers between devices  30.9 us (16%)
  local copies, waits for them, and re-layouts  8.67 us (5%)
    all_to_all x2, blocking collectives, exchange(): return lax.all_to_all(chunks, BOTH, 0, 0, tiled=True)  66 us
    pallas_call x10, Pallas kernels, call(): pl.pallas_call(kernel, grid=(1,), out_shape=results, in_specs=specs[:len(...  38.6 us
    all_to_all x2, waiting for transfers between devices, exchange(): return lax.all_to_all(chunks, BOTH, 0, 0, tiled=True)  30.6 us
    all_to_all x2, starting transfers between devices, exchange(): return lax.all_to_all(chunks, BOTH, 0, 0, tiled=True)  12.1 us
    ppermute x1, starting transfers between devices, sum_over_devices(): other = lax.ppermute(parts, 'col', SWAP)  5.7 us
    all_to_all x1, waiting for transfers between devices, sum_over_devices(): lax.all_to_all(total, BOTH, 0, 0, axis_index_groups=LINES, tiled=True)  3.85 us
  transfers between devices with their start and end apart: 16, of which 13 were waited for; matrix products, arithmetic and copies ran while one was open for 0% of the time, Pallas kernels for 10%

profile of v4, /device:TPU:1, one launch (start us, length us, event | category | flops | bytes accessed | tf_op | source)
XLA Modules:
  0.0 191.5 jit_solution(13028085830061221135)
XLA Ops:
  0.6 0.0 copy-start
  0.6 6.1 %shard_map.147 = (bf16[256,1536]{1,0:T(8,128)(2,1)}, f32[1,1536]{1,0:T(1,128)}) custom-call(s32[576]{0:T(1024)} %valid.1, f32[1296,128]{1,0:T(8,128)} %bitcast.67, f32[128,640]{1,0:T(8,128)} %weight.7, f32[5,128]{1,0:T(8,128)} %bitcast.70, f32[1,128]{1,0:T(1,128)} %bitcast.62, f32[1,128]{1,0:T(1,128)} %bitcast.58), custom_call_target="tpu_custom_call" | custom-call | flops 2000000000 | bytes 4194304 | tf_op jit(solution)/shard_map/pallas_call | solution.py:429
  6.7 2.9 %reshape.73 = bf16[256,2,768]{2,1,0:T(2,128)(2,1)} reshape(bf16[256,1536]{1,0:T(8,128)(2,1)} %get-tuple-element.21) | data formatting | bytes 1572864 | tf_op jit(solution)/shard_map/reshape | solution.py:530
  9.7 0.0 copy-start.7
  9.7 0.0 copy-start.8
  9.7 0.0 copy-start.9
  9.7 0.0 copy-start.12
  9.7 42.6 %all_to_all.25 = bf16[256,2,768]{2,1,0:T(2,128)(2,1)S(1)} all-to-all(bf16[256,2,768]{2,1,0:T(2,128)(2,1)} %reshape.73), channel_id=1, replica_groups=mesh['row'=32,'col'=8] {'row','col'}, dimensions={0} | all-to-all | bytes 1572864 | tf_op jit(solution)/shard_map/all_to_all | solution.py:492
  52.3 0.1 copy.19
  52.4 0.1 collective-permute-start
  52.5 1.7 collective-permute-done.other_w
  54.2 0.0 copy-done
  54.2 2.6 %shard_map.148 = (bf16[256,768]{1,0:T(8,128)(2,1)S(1)}, bf16[3072,1024]{1,0:T(8,128)(2,1)}) custom-call(bf16[256,1536]{1,0:T(8,128)(2,1)S(1)} %bitcast.49, bf16[256,768]{1,0:T(8,128)(2,1)S(1)} %collective-permute-done.other_w, bf16[576,1024]{1,0:T(8,128)(2,1)S(1)} %copy-done), custom_call_target="tpu_custom_call" | custom-call | flops 2000000000 | bytes 4194304 | tf_op jit(solution)/shard_map/pallas_call | solution.py:429
  56.9 0.8 reshape.75
  57.7 6.7 %all-to-all-start.1 = ((bf16[256,2,384]{2,1,0:T(2,128)(2,1)}), bf16[256,2,384]{2,1,0:T(2,128)(2,1)}, u32[]{:S(2)}, u32[]{:S(2)}) async-start(bf16[256,2,384]{2,1,0:T(2,128)(2,1)} %reshape.75), calls=%async_computation.1 | async-start | bytes 786432 | tf_op jit(solution)/shard_map/all_to_all | solution.py:492
  64.4 0.0 copy-done.1
  64.5 0.0 copy-start.5
  64.5 1.0 copy-done.5
  65.5 6.7 %shard_map.149 = (f32[1,1536]{1,0:T(1,128)S(1)}, f32[1024,1536]{1,0:T(8,128)}) custom-call(f32[1,1536]{1,0:T(1,128)S(1)} %copy-done.12, f32[1296,128]{1,0:T(8,128)S(1)} %bitcast.68, f32[1296,128]{1,0:T(8,128)S(1)} %bitcast.69, f32[128,640]{1,0:T(8,128)S(1)} %copy-done.5, f32[5,128]{1,0:T(8,128)S(1)} %bitcast.71, f32[1,128]{1,0:T(1,128)S(1)} %bitcast.63, ...), custom_call_target="tpu_custom_call" | custom-call | flops 10000000000 | bytes 4194304 | tf_op jit(solution)/shard_map/pallas_call | solution.py:429
  72.2 10.0 %all-to-all-done.1 = bf16[256,2,384]{2,1,0:T(2,128)(2,1)} async-done(((bf16[256,2,384]{2,1,0:T(2,128)(2,1)}), bf16[256,2,384]{2,1,0:T(2,128)(2,1)}, u32[]{:S(2)}, u32[]{:S(2)}) %all-to-all-start.1) | async-done | bytes 393248 | tf_op jit(solution)/shard_map/all_to_all | solution.py:492
  82.2 1.0 copy.20
  83.3 2.2 %shard_map.151 = bf16[256,768]{1,0:T(8,128)(2,1)S(1)} custom-call(bf16[256,768]{1,0:T(8,128)(2,1)S(1)} %bitcast.53, f32[1024,1536]{1,0:T(8,128)} %get-tuple-element.24.saved), custom_call_target="tpu_custom_call" | custom-call | flops 2000000000 | bytes 4194304 | tf_op jit(solution)/shard_map/pallas_call | solution.py:429
  85.4 0.1 reshape.82
  85.5 23.5 %all_to_all.26 = bf16[256,2,384]{2,1,0:T(2,128)(2,1)S(1)} all-to-all(bf16[256,2,384]{2,1,0:T(2,128)(2,1)S(1)} %reshape.82), channel_id=1, replica_groups=mesh['row'=32,'col'=8] {'row','col'}, dimensions={0} | all-to-all | bytes 786432 | tf_op jit(solution)/shard_map/all_to_all | solution.py:492
  109.0 0.1 copy.21
  109.0 3.1 %shard_map.152 = (bf16[288,576]{1,0:T(8,128)(2,1)S(1)}, bf16[256,768]{1,0:T(8,128)(2,1)S(1)}, bf16[256,768]{1,0:T(8,128)(2,1)S(1)}) custom-call(bf16[256,768]{1,0:T(8,128)(2,1)S(1)} %bitcast.52, bf16[3072,1024]{1,0:T(8,128)(2,1)} %get-tuple-element.26.kept, bf16[576,1024]{1,0:T(8,128)(2,1)S(1)} %copy-done), custom_call_target="tpu_custom_call" | custom-call | flops 2000000000 | bytes 4194304 | tf_op jit(solution)/shard_map/pallas_call | solution.py:429
  112.1 0.2 collective-permute-start.1
  112.3 2.3 %shard_map.153 = bf16[256,768]{1,0:T(8,128)(2,1)S(1)} custom-call(bf16[288,576]{1,0:T(8,128)(2,1)S(1)} %get-tuple-element.27.d_mixed, bf16[3072,1024]{1,0:T(8,128)(2,1)} %get-tuple-element.26.kept), custom_call_target="tpu_custom_call" | custom-call | flops 2000000000 | bytes 4194304 | tf_op jit(solution)/shard_map/pallas_call | solution.py:429
  114.6 0.0 collective-permute-done.1
  114.6 0.1 fusion
  114.7 0.1 pad_maximum_fusion
  114.8 1.7 copy.18
  116.5 5.4 %all-to-all-start.3 = ((bf16[256,2,768]{2,1,0:T(2,128)(2,1)}), bf16[256,2,768]{2,1,0:T(2,128)(2,1)S(1)}, u32[]{:S(2)}, u32[]{:S(2)}) async-start(bf16[256,2,768]{2,1,0:T(2,128)(2,1)} %copy.18), calls=%async_computation.3 | async-start | bytes 1572864 | tf_op jit(solution)/shard_map/all_to_all | solution.py:492
  122.0 6.3 %shard_map.150 = (f32[1296,128]{1,0:T(8,128)}, f32[128,128]{1,0:T(8,128)S(1)}, f32[128,128]{1,0:T(8,128)S(1)}, f32[128,1536]{1,0:T(8,128)S(1)}) custom-call(bf16[256,768]{1,0:T(8,128)(2,1)S(1)} %bitcast.54, f32[1024,1536]{1,0:T(8,128)} %get-tuple-element.24.saved, f32[128,640]{1,0:T(8,128)S(1)} %copy-done.6, f32[1,128]{1,0:T(1,128)S(1)} %bitcast.64, ...), custom_call_target="tpu_custom_call" | custom-call | flops 8000000000 | bytes 4194304 | tf_op jit(solution)/shard_map/pallas_call | solution.py:429
  128.3 20.6 %all-to-all-done.3 = bf16[256,2,768]{2,1,0:T(2,128)(2,1)S(1)} async-done(((bf16[256,2,768]{2,1,0:T(2,128)(2,1)}), bf16[256,2,768]{2,1,0:T(2,128)(2,1)S(1)}, u32[]{:S(2)}, u32[]{:S(2)}) %all-to-all-start.3) | async-done | bytes 786464 | tf_op jit(solution)/shard_map/all_to_all | solution.py:492
  149.0 0.1 copy.22
  149.1 3.8 %shard_map.154 = f32[256,384]{1,0:T(8,128)S(1)} custom-call(bf16[256,1536]{1,0:T(8,128)(2,1)S(1)} %bitcast.46, f32[1024,1536]{1,0:T(8,128)} %get-tuple-element.24.saved, f32[1,128]{1,0:T(1,128)S(1)} %bitcast.65, f32[1,128]{1,0:T(1,128)S(1)} %bitcast.61, f32[128,128]{1,0:T(8,128)S(1)} %get-tuple-element.30.grad_gate, f32[128,128]{1,0:T(8,128)S(1)} %get-tuple-element.31.grad_out), custom_call_target="tpu_custom_call" | custom-call | flops 2000000000 | bytes 4194304 | tf_op jit(solution)/shard_map/pallas_call | solution.py:429
  152.9 0.1 collective-permute-start.2
  153.1 1.4 collective-permute-done.2
  154.5 0.1 collective-permute-start.3
  154.6 1.1 collective-permute-start.4
  155.7 1.5 collective-permute-start.5
  157.3 2.4 %collective-permute-done.3 = f32[32,384]{1,0:T(8,128)S(1)} collective-permute-done((f32[32,384]{1,0:T(8,128)S(1)}, f32[32,384]{1,0:T(8,128)S(1)}, u32[]{:S(2)}, u32[]{:S(2)}) %collective-permute-start.3) | collective-permute-done | bytes 49184 | tf_op jit(solution)/shard_map/ppermute | solution.py:473
  159.7 0.0 collective-permute-done.4
  159.7 0.7 collective-permute-done.5
  160.3 0.5 collective-permute-start.6
  160.8 1.0 collective-permute-start.7
  161.8 1.7 collective-permute-start.8
  163.5 1.4 collective-permute-done.6
  164.9 0.5 collective-permute-done.7
  165.4 0.0 collective-permute-done.8
  165.4 0.7 broadcast_in_dim.22
  166.1 3.4 %all-to-all-start.4 = ((bf16[8,32,384]{2,1,0:T(8,128)(2,1)}), bf16[8,32,384]{2,1,0:T(8,128)(2,1)S(1)}, u32[]{:S(2)}, u32[]{:S(2)}) async-start(bf16[8,32,384]{2,1,0:T(8,128)(2,1)} %broadcast_in_dim.22), calls=%async_computation.4 | async-start | bytes 393216 | tf_op jit(solution)/shard_map/all_to_all | solution.py:478
  169.5 4.7 %shard_map.155 = f32[1296,128]{1,0:T(8,128)} custom-call(bf16[256,1536]{1,0:T(8,128)(2,1)S(1)} %bitcast.47, f32[1024,1536]{1,0:T(8,128)} %get-tuple-element.24.saved, f32[1,1536]{1,0:T(1,128)S(1)} %get-tuple-element.32.scale, f32[128,1536]{1,0:T(8,128)S(1)} %get-tuple-element.33.d_normed, f32[128,640]{1,0:T(8,128)S(1)} %copy-done.6, f32[1,128]{1,0:T(1,128)S(1)} %bitcast.66), custom_call_target="tpu_custom_call" | custom-call | flops 8000000000 | bytes 4194304 | tf_op jit(solution)/shard_map/pallas_call | solution.py:429
  174.2 3.9 %all-to-all-done.4 = bf16[8,32,384]{2,1,0:T(8,128)(2,1)S(1)} async-done(((bf16[8,32,384]{2,1,0:T(8,128)(2,1)}), bf16[8,32,384]{2,1,0:T(8,128)(2,1)S(1)}, u32[]{:S(2)}, u32[]{:S(2)}) %all-to-all-start.4) | async-done | bytes 196640 | tf_op jit(solution)/shard_map/all_to_all | solution.py:478
  178.1 0.9 collective-permute-start.9
  179.0 2.4 %collective-permute-start.10 = (bf16[32,384]{1,0:T(8,128)(2,1)S(1)}, bf16[32,384]{1,0:T(8,128)(2,1)S(1)}, u32[]{:S(2)}, u32[]{:S(2)}) collective-permute-start(bf16[32,384]{1,0:T(8,128)(2,1)S(1)} %reduce_sum.12), channel_id=1, source_target_pairs={{0,16},{8,24},{16,0},{24,8},{32,48},{40,56},{48,32},{56,40},{64,80... | collective-permute-start | bytes 73736 | tf_op jit(solution)/shard_map/ppermute | solution.py:484
  181.4 0.1 collective-permute-start.11
  181.5 0.5 collective-permute-done.9
  182.1 1.1 collective-permute-done.10
  183.2 0.9 collective-permute-done.11
  184.1 5.7 %collective-permute-start.12 = (bf16[128,384]{1,0:T(8,128)(2,1)S(1)}, bf16[128,384]{1,0:T(8,128)(2,1)S(1)}, u32[]{:S(2)}, u32[]{:S(2)}) collective-permute-start(bf16[128,384]{1,0:T(8,128)(2,1)S(1)} %bitcast.56), channel_id=1, source_target_pairs={{0,1},{1,0},{2,3},{3,2},{4,5},{5,4},{6,7},{7,6},{8,9},{9,8},{10,11... | collective-permute-start | bytes 294920 | tf_op jit(solution)/shard_map/ppermute | solution.py:487
  189.8 0.9 collective-permute-done.12.other
  190.8 0.8 shard_map.156
  (29 shorter events, 0.2 us)
Async XLA Ops:
  0.6 53.6 %copy-start = (bf16[576,1024]{1,0:T(8,128)(2,1)S(1)}, bf16[576,1024]{1,0:T(8,128)(2,1)}, u32[]{:S(2)}) copy-start(bf16[576,1024]{1,0:T(8,128)(2,1)} %constant.97.clone.spread) | copy-start | bytes 3538948
  9.7 54.7 %copy-start.1 = (f32[128]{0:T(128)S(1)}, f32[128]{0:T(128)}, u32[]{:S(2)}) copy-start(f32[128]{0:T(128)} %param.16) | copy-start | bytes 1540
  9.7 54.7 %copy-start.2 = (f32[128]{0:T(128)S(1)}, f32[128]{0:T(128)}, u32[]{:S(2)}) copy-start(f32[128]{0:T(128)} %param.15) | copy-start | bytes 1540
  9.7 54.8 %copy-start.3 = (f32[18,72,128]{2,1,0:T(8,128)S(1)}, f32[18,72,128]{2,1,0:T(8,128)}, u32[]{:S(2)}) copy-start(f32[18,72,128]{2,1,0:T(8,128)} %param.12) | copy-start | bytes 1990660
  9.7 54.8 %copy-start.4 = (f32[18,72,128]{2,1,0:T(8,128)S(1)}, f32[18,72,128]{2,1,0:T(8,128)}, u32[]{:S(2)}) copy-start(f32[18,72,128]{2,1,0:T(8,128)} %param.13) | copy-start | bytes 1990660
  9.7 54.8 %copy-start.7 = (f32[128,128]{1,0:T(8,128)S(1)}, f32[128,128]{1,0:T(8,128)}, u32[]{:S(2)}) copy-start(f32[128,128]{1,0:T(8,128)} %out_weight.3) | copy-start | bytes 196612
  9.7 54.8 %copy-start.8 = (f32[640]{0:T(1024)S(1)}, f32[640]{0:T(1024)}, u32[]{:S(2)}) copy-start(f32[640]{0:T(1024)} %param.18) | copy-start | bytes 7684
  9.7 54.8 %copy-start.9 = (f32[128]{0:T(128)S(1)}, f32[128]{0:T(128)}, u32[]{:S(2)}) copy-start(f32[128]{0:T(128)} %param.19) | copy-start | bytes 1540
  9.7 54.8 %copy-start.12 = (f32[1,1536]{1,0:T(1,128)S(1)}, f32[1,1536]{1,0:T(1,128)}, u32[]{:S(2)}) copy-start(f32[1,1536]{1,0:T(1,128)} %get-tuple-element.23.mask) | copy-start | bytes 18436
  52.4 1.8 collective-permute-start
  57.7 24.5 %all-to-all-start.1 = ((bf16[256,2,384]{2,1,0:T(2,128)(2,1)}), bf16[256,2,384]{2,1,0:T(2,128)(2,1)}, u32[]{:S(2)}, u32[]{:S(2)}) async-start(bf16[256,2,384]{2,1,0:T(2,128)(2,1)} %reshape.75), calls=%async_computation.1 | async-start | bytes 786432 | tf_op jit(solution)/shard_map/all_to_all | solution.py:492
  64.5 1.0 copy-start.5
  112.1 2.5 %collective-permute-start.1 = (bf16[256,768]{1,0:T(8,128)(2,1)S(1)}, bf16[256,768]{1,0:T(8,128)(2,1)S(1)}, u32[]{:S(2)}, u32[]{:S(2)}) collective-permute-start(bf16[256,768]{1,0:T(8,128)(2,1)S(1)} %get-tuple-element.29), channel_id=1, source_target_pairs={{0,1},{1,0},{2,3},{3,2},{4,5},{5,4},{6,7},{7,6},{8,9},{9,8},{10,11... | collective-permute-start | bytes 1179656 | tf_op jit(solution)/shard_map/ppermute | solution.py:568
  112.3 9.7 %copy-start.6 = (f32[128,640]{1,0:T(8,128)S(1)}, f32[128,640]{1,0:T(8,128)}, u32[]{:S(2)}) copy-start(f32[128,640]{1,0:T(8,128)} %weight.7) | copy-start | bytes 983044
  112.3 9.7 %copy-start.10 = (f32[128]{0:T(128)S(1)}, f32[128]{0:T(128)}, u32[]{:S(2)}) copy-start(f32[128]{0:T(128)} %param.20) | copy-start | bytes 1540
  112.3 9.7 %copy-start.11 = (f32[128]{0:T(128)S(1)}, f32[128]{0:T(128)}, u32[]{:S(2)}) copy-start(f32[128]{0:T(128)} %param.22) | copy-start | bytes 1540
  116.5 32.5 %all-to-all-start.3 = ((bf16[256,2,768]{2,1,0:T(2,128)(2,1)}), bf16[256,2,768]{2,1,0:T(2,128)(2,1)S(1)}, u32[]{:S(2)}, u32[]{:S(2)}) async-start(bf16[256,2,768]{2,1,0:T(2,128)(2,1)} %copy.18), calls=%async_computation.3 | async-start | bytes 1572864 | tf_op jit(solution)/shard_map/all_to_all | solution.py:492
  152.9 1.5 collective-permute-start.2
  154.5 5.1 %collective-permute-start.3 = (f32[32,384]{1,0:T(8,128)S(1)}, f32[32,384]{1,0:T(8,128)S(1)}, u32[]{:S(2)}, u32[]{:S(2)}) collective-permute-start(f32[32,384]{1,0:T(8,128)S(1)} %get-tuple-element.40), channel_id=1, source_target_pairs={{0,8},{8,16},{16,24},{24,0},{32,40},{40,48},{48,56},{56,32},{64,72... | collective-permute-start | bytes 147464 | tf_op jit(solution)/shard_map/ppermute | solution.py:473
  154.6 5.0 %collective-permute-start.4 = (f32[32,384]{1,0:T(8,128)S(1)}, f32[32,384]{1,0:T(8,128)S(1)}, u32[]{:S(2)}, u32[]{:S(2)}) collective-permute-start(f32[32,384]{1,0:T(8,128)S(1)} %get-tuple-element.39), channel_id=1, source_target_pairs={{0,16},{8,24},{16,0},{24,8},{32,48},{40,56},{48,32},{56,40},{64,80... | collective-permute-start | bytes 147464 | tf_op jit(solution)/shard_map/ppermute | solution.py:473
  155.7 4.6 %collective-permute-start.5 = (f32[32,384]{1,0:T(8,128)S(1)}, f32[32,384]{1,0:T(8,128)S(1)}, u32[]{:S(2)}, u32[]{:S(2)}) collective-permute-start(f32[32,384]{1,0:T(8,128)S(1)} %get-tuple-element.38), channel_id=1, source_target_pairs={{0,24},{8,0},{16,8},{24,16},{32,56},{40,32},{48,40},{56,48},{64,88... | collective-permute-start | bytes 147464 | tf_op jit(solution)/shard_map/ppermute | solution.py:473
  160.3 4.6 %collective-permute-start.6 = (f32[32,384]{1,0:T(8,128)S(1)}, f32[32,384]{1,0:T(8,128)S(1)}, u32[]{:S(2)}, u32[]{:S(2)}) collective-permute-start(f32[32,384]{1,0:T(8,128)S(1)} %fusion.1), channel_id=1, source_target_pairs={{0,128},{8,136},{16,144},{24,152},{32,160},{40,168},{48,176},{56,1... | collective-permute-start | bytes 147464 | tf_op jit(solution)/shard_map/ppermute | solution.py:458
  160.8 4.6 %collective-permute-start.7 = (f32[32,384]{1,0:T(8,128)S(1)}, f32[32,384]{1,0:T(8,128)S(1)}, u32[]{:S(2)}, u32[]{:S(2)}) collective-permute-start(f32[32,384]{1,0:T(8,128)S(1)} %fusion.1), channel_id=1, source_target_pairs={{0,64},{8,72},{16,80},{24,88},{32,96},{40,104},{48,112},{56,120},{... | collective-permute-start | bytes 147464 | tf_op jit(solution)/shard_map/ppermute | solution.py:458
  161.8 3.6 %collective-permute-start.8 = (f32[32,384]{1,0:T(8,128)S(1)}, f32[32,384]{1,0:T(8,128)S(1)}, u32[]{:S(2)}, u32[]{:S(2)}) collective-permute-start(f32[32,384]{1,0:T(8,128)S(1)} %fusion.1), channel_id=1, source_target_pairs={{0,192},{8,200},{16,208},{24,216},{32,224},{40,232},{48,240},{56,2... | collective-permute-start | bytes 147464 | tf_op jit(solution)/shard_map/ppermute | solution.py:458
  166.1 12.0 %all-to-all-start.4 = ((bf16[8,32,384]{2,1,0:T(8,128)(2,1)}), bf16[8,32,384]{2,1,0:T(8,128)(2,1)S(1)}, u32[]{:S(2)}, u32[]{:S(2)}) async-start(bf16[8,32,384]{2,1,0:T(8,128)(2,1)} %broadcast_in_dim.22), calls=%async_computation.4 | async-start | bytes 393216 | tf_op jit(solution)/shard_map/all_to_all | solution.py:478
  178.1 4.0 %collective-permute-start.9 = (bf16[32,384]{1,0:T(8,128)(2,1)S(1)}, bf16[32,384]{1,0:T(8,128)(2,1)S(1)}, u32[]{:S(2)}, u32[]{:S(2)}) collective-permute-start(bf16[32,384]{1,0:T(8,128)(2,1)S(1)} %reduce_sum.12), channel_id=1, source_target_pairs={{0,8},{8,16},{16,24},{24,0},{32,40},{40,48},{48,56},{56,32},{64,72... | collective-permute-start | bytes 73736 | tf_op jit(solution)/shard_map/ppermute | solution.py:484
  179.0 4.2 %collective-permute-start.10 = (bf16[32,384]{1,0:T(8,128)(2,1)S(1)}, bf16[32,384]{1,0:T(8,128)(2,1)S(1)}, u32[]{:S(2)}, u32[]{:S(2)}) collective-permute-start(bf16[32,384]{1,0:T(8,128)(2,1)S(1)} %reduce_sum.12), channel_id=1, source_target_pairs={{0,16},{8,24},{16,0},{24,8},{32,48},{40,56},{48,32},{56,40},{64,80... | collective-permute-start | bytes 73736 | tf_op jit(solution)/shard_map/ppermute | solution.py:484
  181.4 2.7 %collective-permute-start.11 = (bf16[32,384]{1,0:T(8,128)(2,1)S(1)}, bf16[32,384]{1,0:T(8,128)(2,1)S(1)}, u32[]{:S(2)}, u32[]{:S(2)}) collective-permute-start(bf16[32,384]{1,0:T(8,128)(2,1)S(1)} %reduce_sum.12), channel_id=1, source_target_pairs={{0,24},{8,0},{16,8},{24,16},{32,56},{40,32},{48,40},{56,48},{64,88... | collective-permute-start | bytes 73736 | tf_op jit(solution)/shard_map/ppermute | solution.py:484
  184.1 6.6 %collective-permute-start.12 = (bf16[128,384]{1,0:T(8,128)(2,1)S(1)}, bf16[128,384]{1,0:T(8,128)(2,1)S(1)}, u32[]{:S(2)}, u32[]{:S(2)}) collective-permute-start(bf16[128,384]{1,0:T(8,128)(2,1)S(1)} %bitcast.56), channel_id=1, source_target_pairs={{0,1},{1,0},{2,3},{3,2},{4,5},{5,4},{6,7},{7,6},{8,9},{9,8},{10,11... | collective-permute-start | bytes 294920 | tf_op jit(solution)/shard_map/ppermute | solution.py:487

commit v5 on v4

--- a/solution.py
+++ b/solution.py
@@ -17,7 +17,7 @@
 LANES = 2 * WIRE
 TOTAL = ROW_N * ROWS
 GROUP = ROW_N // COL_N
-STEP = 256
+STEP = 768
 STEPS = LANES // STEP
 F32, BF16 = jnp.float32, jnp.bfloat16
 
@@ -138,28 +138,42 @@
 def project_kernel(
     valid, pair, weight, bias, gain, shift,
     wire, mask,
-    padded, left_s, right_s,
+    padded, by_channel, held, sems,
 ):
     build_mask(lax.axis_index("row"), lax.axis_index("col"), valid, mask)
     fill(padded, pair)
     gain_c, shift_c = column(gain), column(shift)
     bias_c = jnp.concatenate(columns(bias)[:4], axis=0)
     weight_t = split(weight[:, : 4 * WIDTH].T)
-
-    @pl.loop(0, STEPS)
-    def _(step):
-        lanes = lanes_of(step)
-        hat, _ = normalise(padded[lanes, :].T)
-        hidden = fine(weight_t, split(hat * gain_c + shift_c)) + bias_c
-        valid = mask[:, lanes]
-        rows, cols = place_of(step)
-        left = valid * sigmoid(hidden[WIDTH : 2 * WIDTH]) * hidden[:WIDTH]
-        left_s[rows, cols] = left.astype(BF16)
-        right = valid * sigmoid(hidden[3 * WIDTH : 4 * WIDTH]) * hidden[2 * WIDTH : 3 * WIDTH]
-        right_s[rows, cols] = right.astype(BF16)
-
-    wire[:, :WIRE] = move(BY_CHANNEL, left_s[...]).astype(BF16)
-    wire[:, WIRE:] = move(BY_CHANNEL, right_s[...]).astype(BF16)
+    by_channel[...] = order(BY_CHANNEL)
+
+    def leave(step, side):
+        lanes = pl.ds(pl.multiple_of(side * WIRE + step * STEP, STEP), STEP)
+        pieces = held.at[:, lanes], wire.at[:, lanes]
+        return lanes, pltpu.make_async_copy(*pieces, sems.at[2 * step + side])
+
+    @pl.loop(0, WIRE // STEP)
+    def _(step):
+        sides = [], []
+        for half in range(2):
+            lanes = pl.ds(pl.multiple_of(half * WIRE + step * STEP, STEP), STEP)
+            hat, _ = normalise(padded[lanes, :].T)
+            hidden = fine(weight_t, split(hat * gain_c + shift_c)) + bias_c
+            valid = mask[:, lanes]
+            for side in range(2):
+                value = hidden[2 * side * WIDTH : (2 * side + 1) * WIDTH]
+                opened = sigmoid(hidden[(2 * side + 1) * WIDTH : (2 * side + 2) * WIDTH])
+                sides[side].append((valid * opened * value).astype(BF16))
+        for side in range(2):
+            lanes, copy = leave(step, side)
+            both = jnp.concatenate(sides[side], axis=0)
+            held[:, lanes] = dot(by_channel[...], both).astype(BF16)
+            copy.start()
+
+    @pl.loop(0, WIRE // STEP)
+    def _(step):
+        for side in range(2):
+            leave(step, side)[1].wait()
 
 
 def prepare_kernel(
@@ -254,16 +268,21 @@
     keep_right.wait()
 
 
-def turn_kernel(mixed_w, saved, wire, mixed_s, d_mixed_s, d_hat, sem):
-    fetch = pltpu.make_async_copy(saved.at[D_HAT:SAVED, :], d_hat, sem)
-    fetch.start()
+def turn_kernel(mixed_w, saved, wire, mixed_s, d_mixed_s, d_hat, sems):
+    def fetch(step):
+        lanes = lanes_of(step)
+        pieces = saved.at[D_HAT:SAVED, lanes], d_hat.at[:, lanes]
+        return pltpu.make_async_copy(*pieces, sems.at[step])
+
+    for step in range(STEPS):
+        fetch(step).start()
     mixed_s[...] = move(BY_HALF, mixed_w[...])
-    fetch.wait()
 
     @pl.loop(0, STEPS)
     def _(step):
         rows, cols = place_of(step)
         hat, scale = normalise(mixed_s[rows, cols])
+        fetch(step).wait()
         d_mixed_s[rows, cols] = normalise_back(d_hat[:, lanes_of(step)], hat, scale).astype(BF16)
 
     wire[...] = move(BY_CHANNEL, d_mixed_s[...]).astype(BF16)
@@ -519,16 +538,16 @@
     square = ((WIDTH, WIDTH), F32)
     halves = lambda kind: ((DEVICES, WIRE), kind)
 
+    dma = pltpu.SemaphoreType.DMA
     wire, mask = call(
         project_kernel,
-        [((DEVICES, LANES), BF16), ((1, LANES), F32)],
-        [whole, halves(BF16), halves(BF16)],
+        [Raw(((DEVICES, LANES), BF16)), ((1, LANES), F32)],
+        [whole, ((DEVICES, DEVICES), BF16), ((DEVICES, LANES), BF16), dma((STEPS,))],
         residue_mask, pair, proj_weight, bias, gain, shift,
         smem=1,
         room=62,
     )
     got = exchange(wire.reshape(DEVICES, 2, WIRE)).reshape(DEVICES, LANES)
-    dma = pltpu.SemaphoreType.DMA
     scale, saved = call(
         prepare_kernel,
         [((1, LANES), F32), Raw(((SAVED, LANES), F32))],
@@ -548,7 +567,7 @@
     (wire,) = call(
         turn_kernel,
         [halves(BF16)],
-        [halves(F32), halves(BF16), turned, dma],
+        [halves(F32), halves(BF16), turned, dma((STEPS,))],
         mixed_w, Raw(saved),
     )
     got = exchange(wire.reshape(DEVICES, 2, WIRE // 2)).reshape(DEVICES, WIRE)

time: 192 us -> 190 us (0.990)
  Pallas kernels: 38.6 us -> 33.3 us
  waiting for transfers between devices: 46 us -> 49.5 us
    pallas_call x10, Pallas kernels: 38.6 us -> 33.3 us  [call(): pl.pallas_call(kernel, grid=(1,), out_shape=results, in_specs=specs[:len(...]
    all_to_all x2, waiting for transfers between devices: 30.6 us -> 33.5 us  [exchange(): return lax.all_to_all(chunks, BOTH, 0, 0, tiled=True)]
  transfers between devices with their start and end apart: 16 -> 16, of which waited for: 13 -> 13; matrix products, arithmetic and copies ran while one was open for 0% -> 0% of each run, Pallas kernels for 10% -> 9%
where the time goes in v5:
time: 190 us
  blocking collectives  66.2 us (35%)
  waiting for transfers between devices  49.5 us (26%)
  Pallas kernels  33.3 us (18%)
  starting transfers between devices  30.9 us (16%)
  local copies, waits for them, and re-layouts  8.68 us (5%)
    all_to_all x2, blocking collectives, exchange(): return lax.all_to_all(chunks, BOTH, 0, 0, tiled=True)  66.2 us
    all_to_all x2, waiting for transfers between devices, exchange(): return lax.all_to_all(chunks, BOTH, 0, 0, tiled=True)  33.5 us
    pallas_call x10, Pallas kernels, call(): pl.pallas_call(kernel, grid=(1,), out_shape=results, in_specs=specs[:len(...  33.3 us
    all_to_all x2, starting transfers between devices, exchange(): return lax.all_to_all(chunks, BOTH, 0, 0, tiled=True)  12.1 us
    ppermute x1, starting transfers between devices, sum_over_devices(): other = lax.ppermute(parts, 'col', SWAP)  5.69 us
    all_to_all x1, waiting for transfers between devices, sum_over_devices(): lax.all_to_all(total, BOTH, 0, 0, axis_index_groups=LINES, tiled=True)  4.5 us
  transfers between devices with their start and end apart: 16, of which 13 were waited for; matrix products, arithmetic and copies ran while one was open for 0% of the time, Pallas kernels for 9%

profile of v5, /device:TPU:1, one launch (start us, length us, event | category | flops | bytes accessed | tf_op | source)
XLA Modules:
  0.0 189.9 jit_solution(10839461498770303072)
XLA Ops:
  0.6 0.0 copy-start
  0.6 4.9 %shard_map.147 = (bf16[256,1536]{1,0:T(8,128)(2,1)}, f32[1,1536]{1,0:T(1,128)}) custom-call(s32[576]{0:T(1024)} %valid.1, f32[1296,128]{1,0:T(8,128)} %bitcast.67, f32[128,640]{1,0:T(8,128)} %weight.7, f32[5,128]{1,0:T(8,128)} %bitcast.70, f32[1,128]{1,0:T(1,128)} %bitcast.62, f32[1,128]{1,0:T(1,128)} %bitcast.58), custom_call_target="tpu_custom_call" | custom-call | flops 2000000000 | bytes 4194304 | tf_op jit(solution)/shard_map/pallas_call | solution.py:448
  5.6 2.9 %reshape.73 = bf16[256,2,768]{2,1,0:T(2,128)(2,1)} reshape(bf16[256,1536]{1,0:T(8,128)(2,1)} %get-tuple-element.21) | data formatting | bytes 1572864 | tf_op jit(solution)/shard_map/reshape | solution.py:550
  8.6 0.0 copy-start.7
  8.6 0.0 copy-start.8
  8.6 0.0 copy-start.9
  8.6 0.0 copy-start.12
  8.6 42.6 %all_to_all.25 = bf16[256,2,768]{2,1,0:T(2,128)(2,1)S(1)} all-to-all(bf16[256,2,768]{2,1,0:T(2,128)(2,1)} %reshape.73), channel_id=1, replica_groups=mesh['row'=32,'col'=8] {'row','col'}, dimensions={0} | all-to-all | bytes 1572864 | tf_op jit(solution)/shard_map/all_to_all | solution.py:511
  51.2 0.1 copy.19
  51.3 0.1 collective-permute-start
  51.4 1.7 collective-permute-done.other_w
  53.1 2.6 %shard_map.148 = (bf16[256,768]{1,0:T(8,128)(2,1)S(1)}, bf16[3072,1024]{1,0:T(8,128)(2,1)}) custom-call(bf16[256,1536]{1,0:T(8,128)(2,1)S(1)} %bitcast.49, bf16[256,768]{1,0:T(8,128)(2,1)S(1)} %collective-permute-done.other_w, bf16[576,1024]{1,0:T(8,128)(2,1)S(1)} %copy-done), custom_call_target="tpu_custom_call" | custom-call | flops 2000000000 | bytes 4194304 | tf_op jit(solution)/shard_map/pallas_call | solution.py:448
  55.7 0.8 reshape.75
  56.6 6.7 %all-to-all-start.1 = ((bf16[256,2,384]{2,1,0:T(2,128)(2,1)}), bf16[256,2,384]{2,1,0:T(2,128)(2,1)}, u32[]{:S(2)}, u32[]{:S(2)}) async-start(bf16[256,2,384]{2,1,0:T(2,128)(2,1)} %reshape.75), calls=%async_computation.1 | async-start | bytes 786432 | tf_op jit(solution)/shard_map/all_to_all | solution.py:511
  63.3 0.0 copy-done.1
  63.3 0.0 copy-done.2
  63.4 0.0 copy-start.5
  63.4 1.0 copy-done.5
  64.3 5.6 %shard_map.149 = (f32[1,1536]{1,0:T(1,128)S(1)}, f32[1024,1536]{1,0:T(8,128)}) custom-call(f32[1,1536]{1,0:T(1,128)S(1)} %copy-done.12, f32[1296,128]{1,0:T(8,128)S(1)} %bitcast.68, f32[1296,128]{1,0:T(8,128)S(1)} %bitcast.69, f32[128,640]{1,0:T(8,128)S(1)} %copy-done.5, f32[5,128]{1,0:T(8,128)S(1)} %bitcast.71, f32[1,128]{1,0:T(1,128)S(1)} %bitcast.63, ...), custom_call_target="tpu_custom_call" | custom-call | flops 10000000000 | bytes 4194304 | tf_op jit(solution)/shard_map/pallas_call | solution.py:448
  70.0 11.1 %all-to-all-done.1 = bf16[256,2,384]{2,1,0:T(2,128)(2,1)} async-done(((bf16[256,2,384]{2,1,0:T(2,128)(2,1)}), bf16[256,2,384]{2,1,0:T(2,128)(2,1)}, u32[]{:S(2)}, u32[]{:S(2)}) %all-to-all-start.1) | async-done | bytes 393248 | tf_op jit(solution)/shard_map/all_to_all | solution.py:511
  81.1 1.0 copy.20
  82.1 1.7 shard_map.151
  83.9 0.1 reshape.82
  84.0 23.6 %all_to_all.26 = bf16[256,2,384]{2,1,0:T(2,128)(2,1)S(1)} all-to-all(bf16[256,2,384]{2,1,0:T(2,128)(2,1)S(1)} %reshape.82), channel_id=1, replica_groups=mesh['row'=32,'col'=8] {'row','col'}, dimensions={0} | all-to-all | bytes 786432 | tf_op jit(solution)/shard_map/all_to_all | solution.py:511
  107.6 0.1 copy.21
  107.7 3.1 %shard_map.152 = (bf16[288,576]{1,0:T(8,128)(2,1)S(1)}, bf16[256,768]{1,0:T(8,128)(2,1)S(1)}, bf16[256,768]{1,0:T(8,128)(2,1)S(1)}) custom-call(bf16[256,768]{1,0:T(8,128)(2,1)S(1)} %bitcast.52, bf16[3072,1024]{1,0:T(8,128)(2,1)} %get-tuple-element.26.kept, bf16[576,1024]{1,0:T(8,128)(2,1)S(1)} %copy-done), custom_call_target="tpu_custom_call" | custom-call | flops 2000000000 | bytes 4194304 | tf_op jit(solution)/shard_map/pallas_call | solution.py:448
  110.8 0.2 collective-permute-start.1
  111.0 2.3 %shard_map.153 = bf16[256,768]{1,0:T(8,128)(2,1)S(1)} custom-call(bf16[288,576]{1,0:T(8,128)(2,1)S(1)} %get-tuple-element.27.d_mixed, bf16[3072,1024]{1,0:T(8,128)(2,1)} %get-tuple-element.26.kept), custom_call_target="tpu_custom_call" | custom-call | flops 2000000000 | bytes 4194304 | tf_op jit(solution)/shard_map/pallas_call | solution.py:448
  113.3 0.0 collective-permute-done.1
  113.3 0.1 fusion
  113.4 0.1 pad_maximum_fusion
  113.5 1.7 copy.18
  115.2 5.4 %all-to-all-start.3 = ((bf16[256,2,768]{2,1,0:T(2,128)(2,1)}), bf16[256,2,768]{2,1,0:T(2,128)(2,1)S(1)}, u32[]{:S(2)}, u32[]{:S(2)}) async-start(bf16[256,2,768]{2,1,0:T(2,128)(2,1)} %copy.18), calls=%async_computation.3 | async-start | bytes 1572864 | tf_op jit(solution)/shard_map/all_to_all | solution.py:511
  120.6 4.6 %shard_map.150 = (f32[1296,128]{1,0:T(8,128)}, f32[128,128]{1,0:T(8,128)S(1)}, f32[128,128]{1,0:T(8,128)S(1)}, f32[128,1536]{1,0:T(8,128)S(1)}) custom-call(bf16[256,768]{1,0:T(8,128)(2,1)S(1)} %bitcast.54, f32[1024,1536]{1,0:T(8,128)} %get-tuple-element.24.saved, f32[128,640]{1,0:T(8,128)S(1)} %copy-done.6, f32[1,128]{1,0:T(1,128)S(1)} %bitcast.64, ...), custom_call_target="tpu_custom_call" | custom-call | flops 8000000000 | bytes 4194304 | tf_op jit(solution)/shard_map/pallas_call | solution.py:448
  125.2 22.4 %all-to-all-done.3 = bf16[256,2,768]{2,1,0:T(2,128)(2,1)S(1)} async-done(((bf16[256,2,768]{2,1,0:T(2,128)(2,1)}), bf16[256,2,768]{2,1,0:T(2,128)(2,1)S(1)}, u32[]{:S(2)}, u32[]{:S(2)}) %all-to-all-start.3) | async-done | bytes 786464 | tf_op jit(solution)/shard_map/all_to_all | solution.py:511
  147.6 0.1 copy.22
  147.7 3.5 %shard_map.154 = f32[256,384]{1,0:T(8,128)S(1)} custom-call(bf16[256,1536]{1,0:T(8,128)(2,1)S(1)} %bitcast.46, f32[1024,1536]{1,0:T(8,128)} %get-tuple-element.24.saved, f32[1,128]{1,0:T(1,128)S(1)} %bitcast.65, f32[1,128]{1,0:T(1,128)S(1)} %bitcast.61, f32[128,128]{1,0:T(8,128)S(1)} %get-tuple-element.30.grad_gate, f32[128,128]{1,0:T(8,128)S(1)} %get-tuple-element.31.grad_out), custom_call_target="tpu_custom_call" | custom-call | flops 2000000000 | bytes 4194304 | tf_op jit(solution)/shard_map/pallas_call | solution.py:448
  151.3 0.1 collective-permute-start.2
  151.4 1.4 collective-permute-done.2
  152.9 0.1 collective-permute-start.3
  153.0 1.1 collective-permute-start.4
  154.1 1.5 collective-permute-start.5
  155.6 2.4 %collective-permute-done.3 = f32[32,384]{1,0:T(8,128)S(1)} collective-permute-done((f32[32,384]{1,0:T(8,128)S(1)}, f32[32,384]{1,0:T(8,128)S(1)}, u32[]{:S(2)}, u32[]{:S(2)}) %collective-permute-start.3) | collective-permute-done | bytes 49184 | tf_op jit(solution)/shard_map/ppermute | solution.py:492
  158.0 0.0 collective-permute-done.4
  158.0 0.7 collective-permute-done.5
  158.7 0.5 collective-permute-start.6
  159.1 1.0 collective-permute-start.7
  160.2 1.7 collective-permute-start.8
  161.8 1.4 collective-permute-done.6
  163.3 0.5 collective-permute-done.7
  163.7 0.0 collective-permute-done.8
  163.8 0.7 broadcast_in_dim.22
  164.5 3.4 %all-to-all-start.4 = ((bf16[8,32,384]{2,1,0:T(8,128)(2,1)}), bf16[8,32,384]{2,1,0:T(8,128)(2,1)S(1)}, u32[]{:S(2)}, u32[]{:S(2)}) async-start(bf16[8,32,384]{2,1,0:T(8,128)(2,1)} %broadcast_in_dim.22), calls=%async_computation.4 | async-start | bytes 393216 | tf_op jit(solution)/shard_map/all_to_all | solution.py:497
  167.9 4.1 %shard_map.155 = f32[1296,128]{1,0:T(8,128)} custom-call(bf16[256,1536]{1,0:T(8,128)(2,1)S(1)} %bitcast.47, f32[1024,1536]{1,0:T(8,128)} %get-tuple-element.24.saved, f32[1,1536]{1,0:T(1,128)S(1)} %get-tuple-element.32.scale, f32[128,1536]{1,0:T(8,128)S(1)} %get-tuple-element.33.d_normed, f32[128,640]{1,0:T(8,128)S(1)} %copy-done.6, f32[1,128]{1,0:T(1,128)S(1)} %bitcast.66), custom_call_target="tpu_custom_call" | custom-call | flops 8000000000 | bytes 4194304 | tf_op jit(solution)/shard_map/pallas_call | solution.py:448
  171.9 4.5 %all-to-all-done.4 = bf16[8,32,384]{2,1,0:T(8,128)(2,1)S(1)} async-done(((bf16[8,32,384]{2,1,0:T(8,128)(2,1)}), bf16[8,32,384]{2,1,0:T(8,128)(2,1)S(1)}, u32[]{:S(2)}, u32[]{:S(2)}) %all-to-all-start.4) | async-done | bytes 196640 | tf_op jit(solution)/shard_map/all_to_all | solution.py:497
  176.5 0.9 collective-permute-start.9
  177.3 2.4 %collective-permute-start.10 = (bf16[32,384]{1,0:T(8,128)(2,1)S(1)}, bf16[32,384]{1,0:T(8,128)(2,1)S(1)}, u32[]{:S(2)}, u32[]{:S(2)}) collective-permute-start(bf16[32,384]{1,0:T(8,128)(2,1)S(1)} %reduce_sum.12), channel_id=1, source_target_pairs={{0,16},{8,24},{16,0},{24,8},{32,48},{40,56},{48,32},{56,40},{64,80... | collective-permute-start | bytes 73736 | tf_op jit(solution)/shard_map/ppermute | solution.py:503
  179.8 0.1 collective-permute-start.11
  179.9 0.6 collective-permute-done.9
  180.4 1.1 collective-permute-done.10
  181.5 0.9 collective-permute-done.11
  182.5 5.7 %collective-permute-start.12 = (bf16[128,384]{1,0:T(8,128)(2,1)S(1)}, bf16[128,384]{1,0:T(8,128)(2,1)S(1)}, u32[]{:S(2)}, u32[]{:S(2)}) collective-permute-start(bf16[128,384]{1,0:T(8,128)(2,1)S(1)} %bitcast.56), channel_id=1, source_target_pairs={{0,1},{1,0},{2,3},{3,2},{4,5},{5,4},{6,7},{7,6},{8,9},{9,8},{10,11... | collective-permute-start | bytes 294920 | tf_op jit(solution)/shard_map/ppermute | solution.py:506
  188.1 0.9 collective-permute-done.12.other
  189.1 0.8 shard_map.156
  (29 shorter events, 0.2 us)
Async XLA Ops:
  0.6 52.5 %copy-start = (bf16[576,1024]{1,0:T(8,128)(2,1)S(1)}, bf16[576,1024]{1,0:T(8,128)(2,1)}, u32[]{:S(2)}) copy-start(bf16[576,1024]{1,0:T(8,128)(2,1)} %constant.97.clone.spread) | copy-start | bytes 3538948
  8.5 54.7 %copy-start.1 = (f32[128]{0:T(128)S(1)}, f32[128]{0:T(128)}, u32[]{:S(2)}) copy-start(f32[128]{0:T(128)} %param.16) | copy-start | bytes 1540
  8.5 54.7 %copy-start.2 = (f32[128]{0:T(128)S(1)}, f32[128]{0:T(128)}, u32[]{:S(2)}) copy-start(f32[128]{0:T(128)} %param.15) | copy-start | bytes 1540
  8.5 54.8 %copy-start.3 = (f32[18,72,128]{2,1,0:T(8,128)S(1)}, f32[18,72,128]{2,1,0:T(8,128)}, u32[]{:S(2)}) copy-start(f32[18,72,128]{2,1,0:T(8,128)} %param.12) | copy-start | bytes 1990660
  8.5 54.8 %copy-start.4 = (f32[18,72,128]{2,1,0:T(8,128)S(1)}, f32[18,72,128]{2,1,0:T(8,128)}, u32[]{:S(2)}) copy-start(f32[18,72,128]{2,1,0:T(8,128)} %param.13) | copy-start | bytes 1990660
  8.6 54.8 %copy-start.7 = (f32[128,128]{1,0:T(8,128)S(1)}, f32[128,128]{1,0:T(8,128)}, u32[]{:S(2)}) copy-start(f32[128,128]{1,0:T(8,128)} %out_weight.3) | copy-start | bytes 196612
  8.6 54.8 %copy-start.8 = (f32[640]{0:T(1024)S(1)}, f32[640]{0:T(1024)}, u32[]{:S(2)}) copy-start(f32[640]{0:T(1024)} %param.18) | copy-start | bytes 7684
  8.6 54.8 %copy-start.9 = (f32[128]{0:T(128)S(1)}, f32[128]{0:T(128)}, u32[]{:S(2)}) copy-start(f32[128]{0:T(128)} %param.19) | copy-start | bytes 1540
  8.6 54.8 %copy-start.12 = (f32[1,1536]{1,0:T(1,128)S(1)}, f32[1,1536]{1,0:T(1,128)}, u32[]{:S(2)}) copy-start(f32[1,1536]{1,0:T(1,128)} %get-tuple-element.23.mask) | copy-start | bytes 18436
  51.3 1.8 collective-permute-start
  56.6 24.5 %all-to-all-start.1 = ((bf16[256,2,384]{2,1,0:T(2,128)(2,1)}), bf16[256,2,384]{2,1,0:T(2,128)(2,1)}, u32[]{:S(2)}, u32[]{:S(2)}) async-start(bf16[256,2,384]{2,1,0:T(2,128)(2,1)} %reshape.75), calls=%async_computation.1 | async-start | bytes 786432 | tf_op jit(solution)/shard_map/all_to_all | solution.py:511
  63.4 1.0 copy-start.5
  110.8 2.5 %collective-permute-start.1 = (bf16[256,768]{1,0:T(8,128)(2,1)S(1)}, bf16[256,768]{1,0:T(8,128)(2,1)S(1)}, u32[]{:S(2)}, u32[]{:S(2)}) collective-permute-start(bf16[256,768]{1,0:T(8,128)(2,1)S(1)} %get-tuple-element.29), channel_id=1, source_target_pairs={{0,1},{1,0},{2,3},{3,2},{4,5},{5,4},{6,7},{7,6},{8,9},{9,8},{10,11... | collective-permute-start | bytes 1179656 | tf_op jit(solution)/shard_map/ppermute | solution.py:587
  111.0 9.6 %copy-start.6 = (f32[128,640]{1,0:T(8,128)S(1)}, f32[128,640]{1,0:T(8,128)}, u32[]{:S(2)}) copy-start(f32[128,640]{1,0:T(8,128)} %weight.7) | copy-start | bytes 983044
  111.0 9.6 %copy-start.10 = (f32[128]{0:T(128)S(1)}, f32[128]{0:T(128)}, u32[]{:S(2)}) copy-start(f32[128]{0:T(128)} %param.20) | copy-start | bytes 1540
  111.0 9.6 %copy-start.11 = (f32[128]{0:T(128)S(1)}, f32[128]{0:T(128)}, u32[]{:S(2)}) copy-start(f32[128]{0:T(128)} %param.22) | copy-start | bytes 1540
  115.2 32.5 %all-to-all-start.3 = ((bf16[256,2,768]{2,1,0:T(2,128)(2,1)}), bf16[256,2,768]{2,1,0:T(2,128)(2,1)S(1)}, u32[]{:S(2)}, u32[]{:S(2)}) async-start(bf16[256,2,768]{2,1,0:T(2,128)(2,1)} %copy.18), calls=%async_computation.3 | async-start | bytes 1572864 | tf_op jit(solution)/shard_map/all_to_all | solution.py:511
  151.3 1.5 collective-permute-start.2
  152.9 5.1 %collective-permute-start.3 = (f32[32,384]{1,0:T(8,128)S(1)}, f32[32,384]{1,0:T(8,128)S(1)}, u32[]{:S(2)}, u32[]{:S(2)}) collective-permute-start(f32[32,384]{1,0:T(8,128)S(1)} %get-tuple-element.40), channel_id=1, source_target_pairs={{0,8},{8,16},{16,24},{24,0},{32,40},{40,48},{48,56},{56,32},{64,72... | collective-permute-start | bytes 147464 | tf_op jit(solution)/shard_map/ppermute | solution.py:492
  153.0 5.0 %collective-permute-start.4 = (f32[32,384]{1,0:T(8,128)S(1)}, f32[32,384]{1,0:T(8,128)S(1)}, u32[]{:S(2)}, u32[]{:S(2)}) collective-permute-start(f32[32,384]{1,0:T(8,128)S(1)} %get-tuple-element.39), channel_id=1, source_target_pairs={{0,16},{8,24},{16,0},{24,8},{32,48},{40,56},{48,32},{56,40},{64,80... | collective-permute-start | bytes 147464 | tf_op jit(solution)/shard_map/ppermute | solution.py:492
  154.1 4.6 %collective-permute-start.5 = (f32[32,384]{1,0:T(8,128)S(1)}, f32[32,384]{1,0:T(8,128)S(1)}, u32[]{:S(2)}, u32[]{:S(2)}) collective-permute-start(f32[32,384]{1,0:T(8,128)S(1)} %get-tuple-element.38), channel_id=1, source_target_pairs={{0,24},{8,0},{16,8},{24,16},{32,56},{40,32},{48,40},{56,48},{64,88... | collective-permute-start | bytes 147464 | tf_op jit(solution)/shard_map/ppermute | solution.py:492
  158.7 4.6 %collective-permute-start.6 = (f32[32,384]{1,0:T(8,128)S(1)}, f32[32,384]{1,0:T(8,128)S(1)}, u32[]{:S(2)}, u32[]{:S(2)}) collective-permute-start(f32[32,384]{1,0:T(8,128)S(1)} %fusion.1), channel_id=1, source_target_pairs={{0,128},{8,136},{16,144},{24,152},{32,160},{40,168},{48,176},{56,1... | collective-permute-start | bytes 147464 | tf_op jit(solution)/shard_map/ppermute | solution.py:477
  159.1 4.6 %collective-permute-start.7 = (f32[32,384]{1,0:T(8,128)S(1)}, f32[32,384]{1,0:T(8,128)S(1)}, u32[]{:S(2)}, u32[]{:S(2)}) collective-permute-start(f32[32,384]{1,0:T(8,128)S(1)} %fusion.1), channel_id=1, source_target_pairs={{0,64},{8,72},{16,80},{24,88},{32,96},{40,104},{48,112},{56,120},{... | collective-permute-start | bytes 147464 | tf_op jit(solution)/shard_map/ppermute | solution.py:477
  160.2 3.6 %collective-permute-start.8 = (f32[32,384]{1,0:T(8,128)S(1)}, f32[32,384]{1,0:T(8,128)S(1)}, u32[]{:S(2)}, u32[]{:S(2)}) collective-permute-start(f32[32,384]{1,0:T(8,128)S(1)} %fusion.1), channel_id=1, source_target_pairs={{0,192},{8,200},{16,208},{24,216},{32,224},{40,232},{48,240},{56,2... | collective-permute-start | bytes 147464 | tf_op jit(solution)/shard_map/ppermute | solution.py:477
  164.5 12.0 %all-to-all-start.4 = ((bf16[8,32,384]{2,1,0:T(8,128)(2,1)}), bf16[8,32,384]{2,1,0:T(8,128)(2,1)S(1)}, u32[]{:S(2)}, u32[]{:S(2)}) async-start(bf16[8,32,384]{2,1,0:T(8,128)(2,1)} %broadcast_in_dim.22), calls=%async_computation.4 | async-start | bytes 393216 | tf_op jit(solution)/shard_map/all_to_all | solution.py:497
  176.5 4.0 %collective-permute-start.9 = (bf16[32,384]{1,0:T(8,128)(2,1)S(1)}, bf16[32,384]{1,0:T(8,128)(2,1)S(1)}, u32[]{:S(2)}, u32[]{:S(2)}) collective-permute-start(bf16[32,384]{1,0:T(8,128)(2,1)S(1)} %reduce_sum.12), channel_id=1, source_target_pairs={{0,8},{8,16},{16,24},{24,0},{32,40},{40,48},{48,56},{56,32},{64,72... | collective-permute-start | bytes 73736 | tf_op jit(solution)/shard_map/ppermute | solution.py:503
  177.3 4.2 %collective-permute-start.10 = (bf16[32,384]{1,0:T(8,128)(2,1)S(1)}, bf16[32,384]{1,0:T(8,128)(2,1)S(1)}, u32[]{:S(2)}, u32[]{:S(2)}) collective-permute-start(bf16[32,384]{1,0:T(8,128)(2,1)S(1)} %reduce_sum.12), channel_id=1, source_target_pairs={{0,16},{8,24},{16,0},{24,8},{32,48},{40,56},{48,32},{56,40},{64,80... | collective-permute-start | bytes 73736 | tf_op jit(solution)/shard_map/ppermute | solution.py:503
  179.8 2.7 %collective-permute-start.11 = (bf16[32,384]{1,0:T(8,128)(2,1)S(1)}, bf16[32,384]{1,0:T(8,128)(2,1)S(1)}, u32[]{:S(2)}, u32[]{:S(2)}) collective-permute-start(bf16[32,384]{1,0:T(8,128)(2,1)S(1)} %reduce_sum.12), channel_id=1, source_target_pairs={{0,24},{8,0},{16,8},{24,16},{32,56},{40,32},{48,40},{56,48},{64,88... | collective-permute-start | bytes 73736 | tf_op jit(solution)/shard_map/ppermute | solution.py:503
  182.5 6.6 %collective-permute-start.12 = (bf16[128,384]{1,0:T(8,128)(2,1)S(1)}, bf16[128,384]{1,0:T(8,128)(2,1)S(1)}, u32[]{:S(2)}, u32[]{:S(2)}) collective-permute-start(bf16[128,384]{1,0:T(8,128)(2,1)S(1)} %bitcast.56), channel_id=1, source_target_pairs={{0,1},{1,0},{2,3},{3,2},{4,5},{5,4},{6,7},{7,6},{8,9},{9,8},{10,11... | collective-permute-start | bytes 294920 | tf_op jit(solution)/shard_map/ppermute | solution.py:506

commit v6 on v5

--- a/solution.py
+++ b/solution.py
@@ -545,7 +545,7 @@
         [whole, ((DEVICES, DEVICES), BF16), ((DEVICES, LANES), BF16), dma((STEPS,))],
         residue_mask, pair, proj_weight, bias, gain, shift,
         smem=1,
-        room=62,
+        room=63,
     )
     got = exchange(wire.reshape(DEVICES, 2, WIRE)).reshape(DEVICES, LANES)
     scale, saved = call(

time: 190 us -> 191 us (level)
  no operation moved by 1% of the time
where the time goes in v6:
time: 191 us; the launch traced here: 190 us
  blocking collectives  66 us (35%)
  waiting for transfers between devices  50.5 us (26%)
  Pallas kernels  33.2 us (17%)
  starting transfers between devices  30.8 us (16%)
  local copies, waits for them, and re-layouts  8.48 us (4%)
    all_to_all x2, blocking collectives, exchange(): return lax.all_to_all(chunks, BOTH, 0, 0, tiled=True)  66 us
    all_to_all x2, waiting for transfers between devices, exchange(): return lax.all_to_all(chunks, BOTH, 0, 0, tiled=True)  34.5 us
    pallas_call x10, Pallas kernels, call(): pl.pallas_call(kernel, grid=(1,), out_shape=results, in_specs=specs[:len(...  33.2 us
    all_to_all x2, starting transfers between devices, exchange(): return lax.all_to_all(chunks, BOTH, 0, 0, tiled=True)  12 us
    ppermute x1, starting transfers between devices, sum_over_devices(): other = lax.ppermute(parts, 'col', SWAP)  5.69 us
    all_to_all x1, waiting for transfers between devices, sum_over_devices(): lax.all_to_all(total, BOTH, 0, 0, axis_index_groups=LINES, tiled=True)  4.49 us
  transfers between devices with their start and end apart: 16, of which 13 were waited for; matrix products, arithmetic and copies ran while one was open for 0% of the time, Pallas kernels for 9%

profile of v6, /device:TPU:1, one launch (start us, length us, event | category | flops | bytes accessed | tf_op | source)
XLA Modules:
  0.0 190.4 jit_solution(18085683302832675261)
XLA Ops:
  0.6 4.9 %shard_map.147 = (bf16[256,1536]{1,0:T(8,128)(2,1)}, f32[1,1536]{1,0:T(1,128)}) custom-call(s32[576]{0:T(1024)} %valid.1, f32[1296,128]{1,0:T(8,128)} %bitcast.67, f32[128,640]{1,0:T(8,128)} %weight.7, f32[5,128]{1,0:T(8,128)} %bitcast.70, f32[1,128]{1,0:T(1,128)} %bitcast.62, f32[1,128]{1,0:T(1,128)} %bitcast.58), custom_call_target="tpu_custom_call" | custom-call | flops 2000000000 | bytes 4194304 | tf_op jit(solution)/shard_map/pallas_call | solution.py:448
  5.5 2.3 %reshape.73 = bf16[256,2,768]{2,1,0:T(2,128)(2,1)S(1)} reshape(bf16[256,1536]{1,0:T(8,128)(2,1)} %get-tuple-element.21) | data formatting | bytes 1572864 | tf_op jit(solution)/shard_map/reshape | solution.py:550
  7.8 0.0 copy-start.2
  7.8 0.0 copy-start.3
  7.8 0.0 copy-start.4
  7.8 0.0 copy-start.5
  7.8 0.0 copy-start.6
  7.8 0.0 copy-start.7
  7.8 0.0 copy-start.8
  7.8 0.0 copy-start.9
  7.9 0.0 copy-start.12
  7.9 42.4 %all_to_all.25 = bf16[256,2,768]{2,1,0:T(2,128)(2,1)S(1)} all-to-all(bf16[256,2,768]{2,1,0:T(2,128)(2,1)S(1)} %reshape.73), channel_id=1, replica_groups=mesh['row'=32,'col'=8] {'row','col'}, dimensions={0} | all-to-all | bytes 1572864 | tf_op jit(solution)/shard_map/all_to_all | solution.py:511
  50.2 0.1 copy.19
  50.4 0.1 collective-permute-start
  50.5 1.7 collective-permute-done.other_w
  52.2 1.3 copy-done
  53.4 2.6 %shard_map.148 = (bf16[256,768]{1,0:T(8,128)(2,1)S(1)}, bf16[3072,1024]{1,0:T(8,128)(2,1)}) custom-call(bf16[256,1536]{1,0:T(8,128)(2,1)S(1)} %bitcast.49, bf16[256,768]{1,0:T(8,128)(2,1)S(1)} %collective-permute-done.other_w, bf16[576,1024]{1,0:T(8,128)(2,1)S(1)} %copy-done), custom_call_target="tpu_custom_call" | custom-call | flops 2000000000 | bytes 4194304 | tf_op jit(solution)/shard_map/pallas_call | solution.py:448
  56.1 0.8 reshape.75
  56.9 5.2 %all-to-all-start.1 = ((bf16[256,2,384]{2,1,0:T(2,128)(2,1)}), bf16[256,2,384]{2,1,0:T(2,128)(2,1)S(1)}, u32[]{:S(2)}, u32[]{:S(2)}) async-start(bf16[256,2,384]{2,1,0:T(2,128)(2,1)} %reshape.75), calls=%async_computation.1 | async-start | bytes 786432 | tf_op jit(solution)/shard_map/all_to_all | solution.py:511
  62.2 5.6 %shard_map.149 = (f32[1,1536]{1,0:T(1,128)S(1)}, f32[1024,1536]{1,0:T(8,128)}) custom-call(f32[1,1536]{1,0:T(1,128)S(1)} %copy-done.12, f32[1296,128]{1,0:T(8,128)S(1)} %bitcast.68, f32[1296,128]{1,0:T(8,128)S(1)} %bitcast.69, f32[128,640]{1,0:T(8,128)S(1)} %copy-done.6, f32[5,128]{1,0:T(8,128)S(1)} %bitcast.71, f32[1,128]{1,0:T(1,128)S(1)} %bitcast.63, ...), custom_call_target="tpu_custom_call" | custom-call | flops 10000000000 | bytes 4194304 | tf_op jit(solution)/shard_map/pallas_call | solution.py:448
  67.8 0.0 copy-start.1
  67.8 12.9 %all-to-all-done.1 = bf16[256,2,384]{2,1,0:T(2,128)(2,1)S(1)} async-done(((bf16[256,2,384]{2,1,0:T(2,128)(2,1)}), bf16[256,2,384]{2,1,0:T(2,128)(2,1)S(1)}, u32[]{:S(2)}, u32[]{:S(2)}) %all-to-all-start.1) | async-done | bytes 393248 | tf_op jit(solution)/shard_map/all_to_all | solution.py:511
  80.7 0.1 copy.20
  80.7 1.7 shard_map.151
  82.5 0.1 reshape.82
  82.6 23.7 %all_to_all.26 = bf16[256,2,384]{2,1,0:T(2,128)(2,1)S(1)} all-to-all(bf16[256,2,384]{2,1,0:T(2,128)(2,1)S(1)} %reshape.82), channel_id=1, replica_groups=mesh['row'=32,'col'=8] {'row','col'}, dimensions={0} | all-to-all | bytes 786432 | tf_op jit(solution)/shard_map/all_to_all | solution.py:511
  106.2 0.1 copy.21
  106.3 3.1 %shard_map.152 = (bf16[288,576]{1,0:T(8,128)(2,1)S(1)}, bf16[256,768]{1,0:T(8,128)(2,1)S(1)}, bf16[256,768]{1,0:T(8,128)(2,1)S(1)}) custom-call(bf16[256,768]{1,0:T(8,128)(2,1)S(1)} %bitcast.52, bf16[3072,1024]{1,0:T(8,128)(2,1)} %get-tuple-element.26.kept, bf16[576,1024]{1,0:T(8,128)(2,1)S(1)} %copy-done.1), custom_call_target="tpu_custom_call" | custom-call | flops 2000000000 | bytes 4194304 | tf_op jit(solution)/shard_map/pallas_call | solution.py:448
  109.4 0.2 collective-permute-start.1
  109.7 2.3 %shard_map.153 = bf16[256,768]{1,0:T(8,128)(2,1)S(1)} custom-call(bf16[288,576]{1,0:T(8,128)(2,1)S(1)} %get-tuple-element.27.d_mixed, bf16[3072,1024]{1,0:T(8,128)(2,1)} %get-tuple-element.26.kept), custom_call_target="tpu_custom_call" | custom-call | flops 2000000000 | bytes 4194304 | tf_op jit(solution)/shard_map/pallas_call | solution.py:448
  111.9 0.0 collective-permute-done.1
  111.9 0.1 fusion
  112.0 0.1 pad_maximum_fusion
  112.1 1.7 copy.18
  113.8 6.9 %all-to-all-start.3 = ((bf16[256,2,768]{2,1,0:T(2,128)(2,1)}), bf16[256,2,768]{2,1,0:T(2,128)(2,1)}, u32[]{:S(2)}, u32[]{:S(2)}) async-start(bf16[256,2,768]{2,1,0:T(2,128)(2,1)} %copy.18), calls=%async_computation.3 | async-start | bytes 1572864 | tf_op jit(solution)/shard_map/all_to_all | solution.py:511
  120.8 4.6 %shard_map.150 = (f32[1296,128]{1,0:T(8,128)}, f32[128,128]{1,0:T(8,128)S(1)}, f32[128,128]{1,0:T(8,128)S(1)}, f32[128,1536]{1,0:T(8,128)S(1)}) custom-call(bf16[256,768]{1,0:T(8,128)(2,1)S(1)} %bitcast.54, f32[1024,1536]{1,0:T(8,128)} %get-tuple-element.24.saved, f32[128,640]{1,0:T(8,128)S(1)} %copy-done.6, f32[1,128]{1,0:T(1,128)S(1)} %bitcast.64, ...), custom_call_target="tpu_custom_call" | custom-call | flops 8000000000 | bytes 4194304 | tf_op jit(solution)/shard_map/pallas_call | solution.py:448
  125.4 21.6 %all-to-all-done.3 = bf16[256,2,768]{2,1,0:T(2,128)(2,1)} async-done(((bf16[256,2,768]{2,1,0:T(2,128)(2,1)}), bf16[256,2,768]{2,1,0:T(2,128)(2,1)}, u32[]{:S(2)}, u32[]{:S(2)}) %all-to-all-start.3) | async-done | bytes 786464 | tf_op jit(solution)/shard_map/all_to_all | solution.py:511
  147.0 1.2 copy.22
  148.2 3.5 %shard_map.154 = f32[256,384]{1,0:T(8,128)S(1)} custom-call(bf16[256,1536]{1,0:T(8,128)(2,1)S(1)} %bitcast.46, f32[1024,1536]{1,0:T(8,128)} %get-tuple-element.24.saved, f32[1,128]{1,0:T(1,128)S(1)} %bitcast.65, f32[1,128]{1,0:T(1,128)S(1)} %bitcast.61, f32[128,128]{1,0:T(8,128)S(1)} %get-tuple-element.30.grad_gate, f32[128,128]{1,0:T(8,128)S(1)} %get-tuple-element.31.grad_out), custom_call_target="tpu_custom_call" | custom-call | flops 2000000000 | bytes 4194304 | tf_op jit(solution)/shard_map/pallas_call | solution.py:448
  151.8 0.1 collective-permute-start.2
  152.0 1.4 collective-permute-done.2
  153.4 0.1 collective-permute-start.3
  153.5 1.1 collective-permute-start.4
  154.6 1.5 collective-permute-start.5
  156.1 2.4 %collective-permute-done.3 = f32[32,384]{1,0:T(8,128)S(1)} collective-permute-done((f32[32,384]{1,0:T(8,128)S(1)}, f32[32,384]{1,0:T(8,128)S(1)}, u32[]{:S(2)}, u32[]{:S(2)}) %collective-permute-start.3) | collective-permute-done | bytes 49184 | tf_op jit(solution)/shard_map/ppermute | solution.py:492
  158.5 0.7 collective-permute-done.5
  159.2 0.5 collective-permute-start.6
  159.7 1.0 collective-permute-start.7
  160.7 1.7 collective-permute-start.8
  162.3 1.4 collective-permute-done.6
  163.8 0.5 collective-permute-done.7
  164.3 0.7 broadcast_in_dim.22
  165.0 3.4 %all-to-all-start.4 = ((bf16[8,32,384]{2,1,0:T(8,128)(2,1)}), bf16[8,32,384]{2,1,0:T(8,128)(2,1)S(1)}, u32[]{:S(2)}, u32[]{:S(2)}) async-start(bf16[8,32,384]{2,1,0:T(8,128)(2,1)} %broadcast_in_dim.22), calls=%async_computation.4 | async-start | bytes 393216 | tf_op jit(solution)/shard_map/all_to_all | solution.py:497
  168.4 4.1 %shard_map.155 = f32[1296,128]{1,0:T(8,128)} custom-call(bf16[256,1536]{1,0:T(8,128)(2,1)S(1)} %bitcast.47, f32[1024,1536]{1,0:T(8,128)} %get-tuple-element.24.saved, f32[1,1536]{1,0:T(1,128)S(1)} %get-tuple-element.32.scale, f32[128,1536]{1,0:T(8,128)S(1)} %get-tuple-element.33.d_normed, f32[128,640]{1,0:T(8,128)S(1)} %copy-done.6, f32[1,128]{1,0:T(1,128)S(1)} %bitcast.66), custom_call_target="tpu_custom_call" | custom-call | flops 8000000000 | bytes 4194304 | tf_op jit(solution)/shard_map/pallas_call | solution.py:448
  172.4 4.5 %all-to-all-done.4 = bf16[8,32,384]{2,1,0:T(8,128)(2,1)S(1)} async-done(((bf16[8,32,384]{2,1,0:T(8,128)(2,1)}), bf16[8,32,384]{2,1,0:T(8,128)(2,1)S(1)}, u32[]{:S(2)}, u32[]{:S(2)}) %all-to-all-start.4) | async-done | bytes 196640 | tf_op jit(solution)/shard_map/all_to_all | solution.py:497
  177.0 0.9 collective-permute-start.9
  177.8 2.4 %collective-permute-start.10 = (bf16[32,384]{1,0:T(8,128)(2,1)S(1)}, bf16[32,384]{1,0:T(8,128)(2,1)S(1)}, u32[]{:S(2)}, u32[]{:S(2)}) collective-permute-start(bf16[32,384]{1,0:T(8,128)(2,1)S(1)} %reduce_sum.12), channel_id=1, source_target_pairs={{0,16},{8,24},{16,0},{24,8},{32,48},{40,56},{48,32},{56,40},{64,80... | collective-permute-start | bytes 73736 | tf_op jit(solution)/shard_map/ppermute | solution.py:503
  180.3 0.1 collective-permute-start.11
  180.4 0.6 collective-permute-done.9
  180.9 1.1 collective-permute-done.10
  182.0 0.9 collective-permute-done.11
  183.0 5.7 %collective-permute-start.12 = (bf16[128,384]{1,0:T(8,128)(2,1)S(1)}, bf16[128,384]{1,0:T(8,128)(2,1)S(1)}, u32[]{:S(2)}, u32[]{:S(2)}) collective-permute-start(bf16[128,384]{1,0:T(8,128)(2,1)S(1)} %bitcast.56), channel_id=1, source_target_pairs={{0,1},{1,0},{2,3},{3,2},{4,5},{5,4},{6,7},{7,6},{8,9},{9,8},{10,11... | collective-permute-start | bytes 294920 | tf_op jit(solution)/shard_map/ppermute | solution.py:506
  188.6 0.9 collective-permute-done.12.other
  189.6 0.8 shard_map.156
  (29 shorter events, 0.2 us)
Async XLA Ops:
  7.8 54.3 %copy-start.2 = (f32[128]{0:T(128)S(1)}, f32[128]{0:T(128)}, u32[]{:S(2)}) copy-start(f32[128]{0:T(128)} %param.16) | copy-start | bytes 1540
  7.8 54.3 %copy-start.3 = (f32[128]{0:T(128)S(1)}, f32[128]{0:T(128)}, u32[]{:S(2)}) copy-start(f32[128]{0:T(128)} %param.15) | copy-start | bytes 1540
  7.8 54.3 %copy-start.4 = (f32[18,72,128]{2,1,0:T(8,128)S(1)}, f32[18,72,128]{2,1,0:T(8,128)}, u32[]{:S(2)}) copy-start(f32[18,72,128]{2,1,0:T(8,128)} %param.12) | copy-start | bytes 1990660
  7.8 54.3 %copy-start.5 = (f32[18,72,128]{2,1,0:T(8,128)S(1)}, f32[18,72,128]{2,1,0:T(8,128)}, u32[]{:S(2)}) copy-start(f32[18,72,128]{2,1,0:T(8,128)} %param.13) | copy-start | bytes 1990660
  7.8 54.3 %copy-start.6 = (f32[128,640]{1,0:T(8,128)S(1)}, f32[128,640]{1,0:T(8,128)}, u32[]{:S(2)}) copy-start(f32[128,640]{1,0:T(8,128)} %weight.7) | copy-start | bytes 983044
  7.8 54.3 %copy-start.7 = (f32[128,128]{1,0:T(8,128)S(1)}, f32[128,128]{1,0:T(8,128)}, u32[]{:S(2)}) copy-start(f32[128,128]{1,0:T(8,128)} %out_weight.3) | copy-start | bytes 196612
  7.8 54.3 %copy-start.8 = (f32[640]{0:T(1024)S(1)}, f32[640]{0:T(1024)}, u32[]{:S(2)}) copy-start(f32[640]{0:T(1024)} %param.18) | copy-start | bytes 7684
  7.8 54.3 %copy-start.9 = (f32[128]{0:T(128)S(1)}, f32[128]{0:T(128)}, u32[]{:S(2)}) copy-start(f32[128]{0:T(128)} %param.19) | copy-start | bytes 1540
  7.9 54.3 %copy-start.12 = (f32[1,1536]{1,0:T(1,128)S(1)}, f32[1,1536]{1,0:T(1,128)}, u32[]{:S(2)}) copy-start(f32[1,1536]{1,0:T(1,128)} %get-tuple-element.23.mask) | copy-start | bytes 18436
  50.4 1.8 collective-permute-start
  52.2 1.3 copy-start
  56.9 23.8 %all-to-all-start.1 = ((bf16[256,2,384]{2,1,0:T(2,128)(2,1)}), bf16[256,2,384]{2,1,0:T(2,128)(2,1)S(1)}, u32[]{:S(2)}, u32[]{:S(2)}) async-start(bf16[256,2,384]{2,1,0:T(2,128)(2,1)} %reshape.75), calls=%async_computation.1 | async-start | bytes 786432 | tf_op jit(solution)/shard_map/all_to_all | solution.py:511
  67.8 38.5 %copy-start.1 = (bf16[576,1024]{1,0:T(8,128)(2,1)S(1)}, bf16[576,1024]{1,0:T(8,128)(2,1)}, u32[]{:S(2)}) copy-start(bf16[576,1024]{1,0:T(8,128)(2,1)} %constant.97.clone.spread) | copy-start | bytes 3538948
  109.4 2.5 %collective-permute-start.1 = (bf16[256,768]{1,0:T(8,128)(2,1)S(1)}, bf16[256,768]{1,0:T(8,128)(2,1)S(1)}, u32[]{:S(2)}, u32[]{:S(2)}) collective-permute-start(bf16[256,768]{1,0:T(8,128)(2,1)S(1)} %get-tuple-element.29), channel_id=1, source_target_pairs={{0,1},{1,0},{2,3},{3,2},{4,5},{5,4},{6,7},{7,6},{8,9},{9,8},{10,11... | collective-permute-start | bytes 1179656 | tf_op jit(solution)/shard_map/ppermute | solution.py:587
  109.6 11.1 %copy-start.10 = (f32[128]{0:T(128)S(1)}, f32[128]{0:T(128)}, u32[]{:S(2)}) copy-start(f32[128]{0:T(128)} %param.20) | copy-start | bytes 1540
  109.6 11.1 %copy-start.11 = (f32[128]{0:T(128)S(1)}, f32[128]{0:T(128)}, u32[]{:S(2)}) copy-start(f32[128]{0:T(128)} %param.22) | copy-start | bytes 1540
  113.8 33.1 %all-to-all-start.3 = ((bf16[256,2,768]{2,1,0:T(2,128)(2,1)}), bf16[256,2,768]{2,1,0:T(2,128)(2,1)}, u32[]{:S(2)}, u32[]{:S(2)}) async-start(bf16[256,2,768]{2,1,0:T(2,128)(2,1)} %copy.18), calls=%async_computation.3 | async-start | bytes 1572864 | tf_op jit(solution)/shard_map/all_to_all | solution.py:511
  151.8 1.5 collective-permute-start.2
  153.4 5.1 %collective-permute-start.3 = (f32[32,384]{1,0:T(8,128)S(1)}, f32[32,384]{1,0:T(8,128)S(1)}, u32[]{:S(2)}, u32[]{:S(2)}) collective-permute-start(f32[32,384]{1,0:T(8,128)S(1)} %get-tuple-element.40), channel_id=1, source_target_pairs={{0,8},{8,16},{16,24},{24,0},{32,40},{40,48},{48,56},{56,32},{64,72... | collective-permute-start | bytes 147464 | tf_op jit(solution)/shard_map/ppermute | solution.py:492
  153.5 5.0 %collective-permute-start.4 = (f32[32,384]{1,0:T(8,128)S(1)}, f32[32,384]{1,0:T(8,128)S(1)}, u32[]{:S(2)}, u32[]{:S(2)}) collective-permute-start(f32[32,384]{1,0:T(8,128)S(1)} %get-tuple-element.39), channel_id=1, source_target_pairs={{0,16},{8,24},{16,0},{24,8},{32,48},{40,56},{48,32},{56,40},{64,80... | collective-permute-start | bytes 147464 | tf_op jit(solution)/shard_map/ppermute | solution.py:492
  154.6 4.6 %collective-permute-start.5 = (f32[32,384]{1,0:T(8,128)S(1)}, f32[32,384]{1,0:T(8,128)S(1)}, u32[]{:S(2)}, u32[]{:S(2)}) collective-permute-start(f32[32,384]{1,0:T(8,128)S(1)} %get-tuple-element.38), channel_id=1, source_target_pairs={{0,24},{8,0},{16,8},{24,16},{32,56},{40,32},{48,40},{56,48},{64,88... | collective-permute-start | bytes 147464 | tf_op jit(solution)/shard_map/ppermute | solution.py:492
  159.2 4.6 %collective-permute-start.6 = (f32[32,384]{1,0:T(8,128)S(1)}, f32[32,384]{1,0:T(8,128)S(1)}, u32[]{:S(2)}, u32[]{:S(2)}) collective-permute-start(f32[32,384]{1,0:T(8,128)S(1)} %fusion.1), channel_id=1, source_target_pairs={{0,128},{8,136},{16,144},{24,152},{32,160},{40,168},{48,176},{56,1... | collective-permute-start | bytes 147464 | tf_op jit(solution)/shard_map/ppermute | solution.py:477
  159.7 4.6 %collective-permute-start.7 = (f32[32,384]{1,0:T(8,128)S(1)}, f32[32,384]{1,0:T(8,128)S(1)}, u32[]{:S(2)}, u32[]{:S(2)}) collective-permute-start(f32[32,384]{1,0:T(8,128)S(1)} %fusion.1), channel_id=1, source_target_pairs={{0,64},{8,72},{16,80},{24,88},{32,96},{40,104},{48,112},{56,120},{... | collective-permute-start | bytes 147464 | tf_op jit(solution)/shard_map/ppermute | solution.py:477
  160.7 3.6 %collective-permute-start.8 = (f32[32,384]{1,0:T(8,128)S(1)}, f32[32,384]{1,0:T(8,128)S(1)}, u32[]{:S(2)}, u32[]{:S(2)}) collective-permute-start(f32[32,384]{1,0:T(8,128)S(1)} %fusion.1), channel_id=1, source_target_pairs={{0,192},{8,200},{16,208},{24,216},{32,224},{40,232},{48,240},{56,2... | collective-permute-start | bytes 147464 | tf_op jit(solution)/shard_map/ppermute | solution.py:477
  165.0 12.0 %all-to-all-start.4 = ((bf16[8,32,384]{2,1,0:T(8,128)(2,1)}), bf16[8,32,384]{2,1,0:T(8,128)(2,1)S(1)}, u32[]{:S(2)}, u32[]{:S(2)}) async-start(bf16[8,32,384]{2,1,0:T(8,128)(2,1)} %broadcast_in_dim.22), calls=%async_computation.4 | async-start | bytes 393216 | tf_op jit(solution)/shard_map/all_to_all | solution.py:497
  177.0 4.0 %collective-permute-start.9 = (bf16[32,384]{1,0:T(8,128)(2,1)S(1)}, bf16[32,384]{1,0:T(8,128)(2,1)S(1)}, u32[]{:S(2)}, u32[]{:S(2)}) collective-permute-start(bf16[32,384]{1,0:T(8,128)(2,1)S(1)} %reduce_sum.12), channel_id=1, source_target_pairs={{0,8},{8,16},{16,24},{24,0},{32,40},{40,48},{48,56},{56,32},{64,72... | collective-permute-start | bytes 73736 | tf_op jit(solution)/shard_map/ppermute | solution.py:503
  177.8 4.2 %collective-permute-start.10 = (bf16[32,384]{1,0:T(8,128)(2,1)S(1)}, bf16[32,384]{1,0:T(8,128)(2,1)S(1)}, u32[]{:S(2)}, u32[]{:S(2)}) collective-permute-start(bf16[32,384]{1,0:T(8,128)(2,1)S(1)} %reduce_sum.12), channel_id=1, source_target_pairs={{0,16},{8,24},{16,0},{24,8},{32,48},{40,56},{48,32},{56,40},{64,80... | collective-permute-start | bytes 73736 | tf_op jit(solution)/shard_map/ppermute | solution.py:503
  180.3 2.7 %collective-permute-start.11 = (bf16[32,384]{1,0:T(8,128)(2,1)S(1)}, bf16[32,384]{1,0:T(8,128)(2,1)S(1)}, u32[]{:S(2)}, u32[]{:S(2)}) collective-permute-start(bf16[32,384]{1,0:T(8,128)(2,1)S(1)} %reduce_sum.12), channel_id=1, source_target_pairs={{0,24},{8,0},{16,8},{24,16},{32,56},{40,32},{48,40},{56,48},{64,88... | collective-permute-start | bytes 73736 | tf_op jit(solution)/shard_map/ppermute | solution.py:503
  183.0 6.6 %collective-permute-start.12 = (bf16[128,384]{1,0:T(8,128)(2,1)S(1)}, bf16[128,384]{1,0:T(8,128)(2,1)S(1)}, u32[]{:S(2)}, u32[]{:S(2)}) collective-permute-start(bf16[128,384]{1,0:T(8,128)(2,1)S(1)} %bitcast.56), channel_id=1, source_target_pairs={{0,1},{1,0},{2,3},{3,2},{4,5},{5,4},{6,7},{7,6},{8,9},{9,8},{10,11... | collective-permute-start | bytes 294920 | tf_op jit(solution)/shard_map/ppermute | solution.py:506
